TPU v7x, 32 devices: a whole 2x2x4 slice. The times are simulated.
32 devices in a mesh: dp: 8 (over z, y), tm: 4 (over x, core).
Axes of the slice: x: 2, y: 2, z: 4, core: 2. Of those that a mesh axis runs over, the one named last changes fastest.
Arguments:
- frames: bfloat16 [8, 1024, 1536], P('dp', 'tm'), may hold values from -6 to 6
- lengths: int32 [8], P('dp'), may hold values from 256 to 1024
- ln_gain: float32 [1536], replicated, may hold values from 0.1 to 1.9
- w_query: bfloat16 [1536, 768], P('dp'), may hold values from -0.15625 to 0.15625
- w_key: bfloat16 [1536, 768], P('dp'), may hold values from -0.15625 to 0.15625
- w_value: bfloat16 [1536, 768], P('dp'), may hold values from -0.15625 to 0.15625
- w_output: bfloat16 [768, 1536], P('dp'), may hold values from -0.21875 to 0.21875
- w_position: bfloat16 [1536, 768], P(None, 'tm'), may hold values from -0.15625 to 0.15625
- bias_content: float32 [8, 96], replicated, may hold values from -60 to 60, as said below
- bias_position: float32 [8, 96], replicated, may hold values from -3 to 3
Outputs:
- attended: bfloat16 [8, 1024, 1536], P('dp', 'tm')
Inputs may be any that keep to these rules, and one draw needn't show every extreme that they name: `lengths`: number of valid frames of each utterance; later frames are padding. `bias_content`: content biases; in some draws they reach magnitudes near 60.
All inputs are finite; a program needn't handle non-finite values.
Results may differ from a plain program's by a relative error of at most 0.012.
The roundings to bfloat16 on the way count: a program that leaves them out, or rounds other values in their place, can miss the bound.
Values may be sent and summed in bfloat16 or wider, within the bound.
No kernel may reach another device: no remote copies, remote signals or barrier semaphores. Data moves between devices by JAX's collectives and lax.ppermute only.
A program may use at most 64 MiB of HBM per device.

v0:
```python
import math

import jax
import jax.numpy as jnp
from jax import lax
from jax.sharding import PartitionSpec as P

epsilon = 1e-05
masked_score = -1e30


def padded(block, sides, width):
    for axis, dim in sides:
        count = lax.axis_size(axis)
        forward = [(i, i + 1) for i in range(count - 1)]
        backward = [(target, source) for source, target in forward]
        low = lax.ppermute(
            lax.slice_in_dim(block, block.shape[dim] - width, None, axis=dim), axis, forward
        )
        high = lax.ppermute(lax.slice_in_dim(block, 0, width, axis=dim), axis, backward)
        block = jnp.concatenate([low, block, high], axis=dim)
    return block


def layer_norm(frame_rows, ln_gain):
    widened = frame_rows.astype(jnp.float32)
    row_mean = jnp.mean(widened, axis=-1, keepdims=True)
    centered = widened - row_mean
    row_var = jnp.mean(centered * centered, axis=-1, keepdims=True)
    return (centered * lax.rsqrt(row_var + epsilon) * ln_gain).astype(jnp.bfloat16)


def sinusoid(row_count, model_width):
    offsets = jnp.arange(row_count, dtype=jnp.float32) - (row_count // 2 - 1)
    half_width = model_width // 2
    frequency = jnp.exp(
        jnp.arange(half_width, dtype=jnp.float32) * (-2.0 * math.log(10000.0) / model_width)
    )
    angles = offsets[:, None] * frequency[None, :]
    return jnp.concatenate([jnp.sin(angles), jnp.cos(angles)], axis=1).astype(jnp.bfloat16)


def rel_shift(position_full):
    block_len = position_full.shape[0]
    span_len = position_full.shape[1]
    skewed = position_full.reshape(-1)[: block_len * (span_len - 1)].reshape(
        block_len, span_len - 1
    )
    return skewed[:, block_len - 1 : 4 * block_len - 1]


def attend(
    query_proj, key_rows, value_rows, rel_heads, bias_content, bias_position, valid_len, first_pos
):
    block_len = query_proj.shape[0]
    head_count, head_size = bias_content.shape
    query_pos = first_pos + jnp.arange(block_len, dtype=jnp.int32)
    key_pos = first_pos - block_len + jnp.arange(3 * block_len, dtype=jnp.int32)
    key_valid = (key_pos >= 0) & (key_pos < valid_len)
    query_valid = (query_pos < valid_len).astype(jnp.float32)
    split_query = query_proj.reshape(block_len, head_count, head_size).astype(jnp.float32)
    with_content = (split_query + bias_content[None]).astype(jnp.bfloat16).transpose(1, 0, 2)
    with_position = (split_query + bias_position[None]).astype(jnp.bfloat16).transpose(1, 0, 2)
    key_heads = key_rows.reshape(3 * block_len, head_count, head_size).transpose(1, 0, 2)
    value_heads = value_rows.reshape(3 * block_len, head_count, head_size).transpose(1, 0, 2)
    scale = 1.0 / math.sqrt(head_size)

    def one_head(operands):
        content_query, position_query, key_head, value_head, rel_head = operands
        content = jnp.dot(content_query, key_head.T, preferred_element_type=jnp.float32)
        shifted = rel_shift(jnp.dot(position_query, rel_head.T, preferred_element_type=jnp.float32))
        scores = jnp.where(key_valid[None, :], (content + shifted) * scale, masked_score)
        row_max = jnp.max(scores, axis=1, keepdims=True)
        raised = jnp.exp(scores - row_max)
        totals = jnp.sum(raised, axis=1, keepdims=True)
        weights = (raised / totals).astype(jnp.bfloat16)
        return jnp.dot(weights, value_head, preferred_element_type=jnp.float32)

    context = lax.map(one_head, (with_content, with_position, key_heads, value_heads, rel_heads))
    context = context.transpose(1, 0, 2) * query_valid[:, None, None]
    return context.astype(jnp.bfloat16).reshape(block_len, head_count * head_size)


def column_cut(weight_shard, tm_index, tm_count):
    slice_width = weight_shard.shape[1] // tm_count
    return lax.dynamic_slice_in_dim(weight_shard, tm_index * slice_width, slice_width, 1)


def body(
    frames,
    lengths,
    ln_gain,
    w_query,
    w_key,
    w_value,
    w_output,
    w_position,
    bias_content,
    bias_position,
):
    frame_rows = frames[0]
    valid_len = lengths[0]
    block_len = frame_rows.shape[0]
    model_width = frame_rows.shape[1]
    head_count, head_size = bias_content.shape
    tm_index = lax.axis_index("tm")
    first_pos = tm_index * block_len
    normed = layer_norm(frame_rows, ln_gain)
    rel_share = jnp.dot(
        sinusoid(4 * block_len, model_width), w_position, preferred_element_type=jnp.float32
    ).astype(jnp.bfloat16)
    relative = lax.all_gather(rel_share, "tm", axis=1, tiled=True)
    rel_heads = relative.reshape(4 * block_len, head_count, head_size).transpose(1, 0, 2)
    tm_count = lax.axis_size("tm")
    slice_query, slice_key, slice_value, slice_output = (
        lax.all_gather(column_cut(w_query, tm_index, tm_count), "dp", axis=0, tiled=True),
        lax.all_gather(column_cut(w_key, tm_index, tm_count), "dp", axis=0, tiled=True),
        lax.all_gather(column_cut(w_value, tm_index, tm_count), "dp", axis=0, tiled=True),
        lax.all_gather(column_cut(w_output, tm_index, tm_count), "dp", axis=0, tiled=True),
    )
    full_query, full_key, full_value, full_output = (
        lax.all_gather(slice_query, "tm", axis=1, tiled=True),
        lax.all_gather(slice_key, "tm", axis=1, tiled=True),
        lax.all_gather(slice_value, "tm", axis=1, tiled=True),
        lax.all_gather(slice_output, "tm", axis=1, tiled=True),
    )
    query_sum = jnp.dot(normed, full_query, preferred_element_type=jnp.float32)
    key_sum = jnp.dot(normed, full_key, preferred_element_type=jnp.float32)
    value_sum = jnp.dot(normed, full_value, preferred_element_type=jnp.float32)
    query_proj = query_sum.astype(jnp.bfloat16)
    key_proj = key_sum.astype(jnp.bfloat16)
    value_proj = value_sum.astype(jnp.bfloat16)
    stacked = jnp.stack((key_proj, value_proj))
    widened = padded(stacked, (("tm", 1),), block_len)
    key_rows = widened[0]
    value_rows = widened[1]
    context = attend(
        query_proj,
        key_rows,
        value_rows,
        rel_heads,
        bias_content,
        bias_position,
        valid_len,
        first_pos,
    )
    mixed_out = jnp.dot(context, full_output, preferred_element_type=jnp.float32)
    attended = (frame_rows.astype(jnp.float32) + mixed_out).astype(jnp.bfloat16)
    return attended[None]


def solution(mesh):
    placed = (
        P("dp", "tm", None),
        P("dp"),
        P(),
        P("dp", None),
        P("dp", None),
        P("dp", None),
        P("dp", None),
        P(None, "tm"),
        P(),
        P(),
    )
    return jax.shard_map(
        body, mesh=mesh, in_specs=placed, out_specs=P("dp", "tm", None), check_vma=False
    )
```

profile of v0, /device:TPU:0, one launch (start us, length us, event | category | flops | bytes accessed | tf_op | source)
XLA Modules:
  0.0 255.4 jit_solution(5457594881442320766)
XLA Ops:
  7.6 33.8 %all_gather.29 = bf16[1536,192]{1,0:T(8,128)(2,1)S(1)} all-gather(bf16[192,192]{1,0:T(8,128)(2,1)S(1)} %constant_dynamic-slice_fusion.1), channel_id=1, replica_groups=mesh['dp'=8,'tm'=4] {'dp'}, dimensions={0}, use_global_device_ids=true | all-gather | bytes 663552 | tf_op jit(solution)/shard_map/all_gather | solution.py:117
  43.6 32.0 %all_gather.31 = bf16[1536,192]{1,0:T(8,128)(2,1)S(1)} all-gather(bf16[192,192]{1,0:T(8,128)(2,1)S(1)} %constant_dynamic-slice_fusion), channel_id=1, replica_groups=mesh['dp'=8,'tm'=4] {'dp'}, dimensions={0}, use_global_device_ids=true | all-gather | bytes 663552 | tf_op jit(solution)/shard_map/all_gather | solution.py:118
  76.8 11.8 %fusion.24 = (bf16[1024,768]{1,0:T(8,128)(2,1)S(1)}, bf16[1024,768]{1,0:T(8,128)(2,1)S(1)}) fusion(f32[768]{0:T(1024)S(1)} %multiply_exponential_fusion, f32[1024]{0:T(1024)S(1)} %iota_add_fusion.1), kind=kLoop, calls=%fused_computation.31 | loop fusion | flops 2359296 | bytes 3152896 | tf_op jit(solution)/shard_map/convert.1
  88.6 1.9 fusion.38
  91.7 32.1 %all_gather.27 = bf16[1536,192]{1,0:T(8,128)(2,1)S(1)} all-gather(bf16[192,192]{1,0:T(8,128)(2,1)S(1)} %constant_dynamic-slice_fusion.2), channel_id=1, replica_groups=mesh['dp'=8,'tm'=4] {'dp'}, dimensions={0}, use_global_device_ids=true | all-gather | bytes 663552 | tf_op jit(solution)/shard_map/all_gather | solution.py:116
  126.4 2.5 fusion.42
  128.9 2.5 fusion.43
  132.4 2.2 collective-permute-start
  135.9 33.5 %all_gather.34 = bf16[768,384]{1,0:T(8,128)(2,1)} all-gather(bf16[96,384]{1,0:T(8,128)(2,1)S(1)} %constant_dynamic-slice_fusion.3), channel_id=1, replica_groups=mesh['dp'=8,'tm'=4] {'dp'}, dimensions={0}, use_global_device_ids=true | all-gather | bytes 663552 | tf_op jit(solution)/shard_map/all_gather | solution.py:119
  170.1 3.7 %copy.40 = bf16[1024,8,96]{2,0,1:T(8,128)(2,1)} copy(bf16[1024,8,96]{0,2,1:T(8,128)(2,1)} %bitcast.101) | data formatting | bytes 3145728 | tf_op jit(solution)/shard_map/reshape | solution.py:113
  173.9 3.4 %fusion.41 = f32[256,768]{1,0:T(8,128)} fusion(bf16[1536,768]{0,1:T(8,128)(2,1)} %all-gather.6.cloned.1.call-done, bf16[1,256,1536]{2,1,0:T(8,128)(2,1)S(1)} %copy-done.1, f32[1536]{0:T(1024)S(1)} %copy-done.6, f32[256]{0:T(256)S(1)} %add_rsqrt_fusion, f32[256]{0:T(256)S(1)} %broadcast_multiply_fusion), kind=kOutput, calls=%fused_computation.53 | convolution fusion | flops 606339072 | bytes 3940352 | tf_op jit(solution)/shard_map/dot_general | solution.py:127
  179.8 1.7 pad_maximum_fusion
  182.7 2.4 copy.41
  185.0 1.4 copy.39
  186.5 57.9 %while.11 = (s32[]{:T(128)}, f32[8,256,96]{1,2,0:T(8,128)}, bf16[8,256,96]{1,2,0:T(8,128)(2,1)}, bf16[8,768,96]{1,2,0:T(8,128)(2,1)}, bf16[8,256,96]{1,2,0:T(8,1...) while((s32[]{:T(128)}, f32[8,256,96]{1,2,0:T(8,128)}, ...), condition=%wide.region_5.6_spmd.clone, body=%wide.region_2.5_spmd.clone.sunk | while | flops 127601152 | bytes 12295845 | solution.py:79
  191.7 2.0 fusion.71
  199.0 2.0 fusion.71
  206.2 2.0 fusion.71
  213.4 2.0 fusion.71
  220.6 2.0 fusion.71
  227.9 2.0 fusion.71
  235.1 2.0 fusion.71
  242.3 2.0 fusion.71
  245.6 3.3 %fusion.31 = bf16[1,256,1536]{2,1,0:T(8,128)(2,1)} fusion(bf16[256,768]{0,1:T(8,128)(2,1)S(1)} %bitcast.102, bf16[768,1536]{1,0:T(8,128)(2,1)} %all-gather.14.cloned.1.call-done, bf16[1,256,1536]{2,1,0:T(8,128)(2,1)S(1)} %copy-done.1), kind=kOutput, calls=%fused_computation.39 | convolution fusion | flops 605159424 | bytes 4325376 | tf_op jit(solution)/shard_map/dot_general | solution.py:147
  (128 shorter events, 56.7 us)
Async XLA Ops:
  6.5 82.1 %copy-start = (bf16[1536,192]{0,1:T(8,128)(2,1)S(1)}, bf16[1536,192]{0,1:T(8,128)(2,1)}, u32[]{:S(2)}) copy-start(bf16[1536,192]{0,1:T(8,128)(2,1)} %param.19) | copy-start | bytes 1769476
  6.5 119.9 %all-gather.8.cloned.1.call-start = ((), (), s32[]{:S(2)}) async-start(), calls=%async_computation.1 | async-start | bytes 2949120 | tf_op jit(solution)/shard_map/all_gather | solution.py:123
  42.5 86.5 %all-gather.10.cloned.1.call-start = ((), (), s32[]{:S(2)}) async-start(), calls=%async_computation.2 | async-start | bytes 2949120 | tf_op jit(solution)/shard_map/all_gather | solution.py:124
  76.7 93.5 %all-gather.12.cloned.1.call-start = ((), (), s32[]{:S(2)}) async-start(), calls=%async_computation.3 | async-start | bytes 1966080 | tf_op jit(solution)/shard_map/all_gather | solution.py:112
  90.5 35.3 %copy-start.1 = (bf16[1,256,1536]{2,1,0:T(8,128)(2,1)S(1)}, bf16[1,256,1536]{2,1,0:T(8,128)(2,1)}, u32[]{:S(2)}) copy-start(bf16[1,256,1536]{2,1,0:T(8,128)(2,1)} %param.12) | copy-start | bytes 2359300
  90.6 83.3 %all-gather.6.cloned.1.call-start = ((), (), s32[]{:S(2)}) async-start(), calls=%async_computation | async-start | bytes 2949120 | tf_op jit(solution)/shard_map/all_gather | solution.py:122
  123.7 2.7 %copy-start.6 = (f32[1536]{0:T(1024)S(1)}, f32[1536]{0:T(1024)}, u32[]{:S(2)}) copy-start(f32[1536]{0:T(1024)} %param.14) | copy-start | bytes 18436
  124.9 120.7 %all-gather.14.cloned.1.call-start = ((), (), s32[]{:S(2)}) async-start(), calls=%async_computation.4 | async-start | bytes 2949120 | tf_op jit(solution)/shard_map/all_gather | solution.py:125
  132.4 47.4 %collective-permute-start = (bf16[2,256,768]{2,1,0:T(8,128)(2,1)}, bf16[2,256,768]{2,1,0:T(8,128)(2,1)}, u32[]{:S(2)}, u32[]{:S(2)}) collective-permute-start(bf16[2,256,768]{2,1,0:T(8,128)(2,1)} %pad_maximum_fusion.1), channel_id=1, source_target_pairs={{0,1},{1,2},{2,3},{4,5},{5,6},{6,7},{8,9},{9,10},{10,11},{12,13},{... | collective-permute-start | bytes 2359304 | tf_op jit(solution)/shard_map/ppermute | solution.py:17
  134.6 45.2 %collective-permute-start.1 = (bf16[2,256,768]{2,1,0:T(8,128)(2,1)}, bf16[2,256,768]{2,1,0:T(8,128)(2,1)}, u32[]{:S(2)}, u32[]{:S(2)}) collective-permute-start(bf16[2,256,768]{2,1,0:T(8,128)(2,1)} %pad_maximum_fusion.1), channel_id=1, source_target_pairs={{1,0},{2,1},{3,2},{5,4},{6,5},{7,6},{9,8},{10,9},{11,10},{13,12},{... | collective-permute-start | bytes 2359304 | tf_op jit(solution)/shard_map/ppermute | solution.py:20
  177.3 1.4 copy-start.4
  177.3 1.4 copy-start.5
  191.7 2.0 copy-start.3
  193.7 0.8 copy-start.2
  198.9 2.0 copy-start.3
  201.0 0.8 copy-start.2
  206.2 2.0 copy-start.3
  213.4 2.0 copy-start.3
  215.4 0.8 copy-start.2
  220.6 2.0 copy-start.3
  227.9 2.0 copy-start.3
  235.1 2.0 copy-start.3
  237.1 0.8 copy-start.2
  242.3 2.0 copy-start.3
  (4 other events, 3.2 us)
Sparse Core Ops, SparseCore 0:
  42.6 25.0 all-gather.7
  76.8 25.1 all-gather.9
  103.5 19.6 all-gather.11
  125.0 28.7 all-gather.5
  169.6 27.2 all-gather.13
where the time goes:
time: 257 us; the launch traced here: 255 us
  blocking collectives  131 us (51%)
  matrix products  50.9 us (20%)
  local copies, waits for them, and re-layouts  30.4 us (12%)
  other arithmetic  24.7 us (10%)
  between operations  14 us (5%)
  starting transfers between devices  3.64 us (1%)
    all_gather x1, blocking collectives, body(): lax.all_gather(column_cut(w_key, tm_index, tm_count), 'dp', axis=0, tiled...  33.8 us
    all_gather x1, blocking collectives, body(): lax.all_gather(column_cut(w_output, tm_index, tm_count), 'dp', axis=0, ti...  33.5 us
    all_gather x1, blocking collectives, body(): lax.all_gather(column_cut(w_query, tm_index, tm_count), 'dp', axis=0, til...  32.1 us
    all_gather x1, blocking collectives, body(): lax.all_gather(column_cut(w_value, tm_index, tm_count), 'dp', axis=0, til...  32 us
    dot_general x8, matrix products, one_head(): return jnp.dot(weights, value_head, preferred_element_type=jnp.float32)  16.1 us
    another operation x1, other arithmetic  11.8 us
    dot_general x8, matrix products, one_head(): jnp.dot(content_query, key_head.T, preferred_element_type=jnp.float32)  10.9 us
    dot_general x8, matrix products, one_head(): jnp.dot(position_query, rel_head.T, preferred_element_type=jnp.float32)  10.2 us
  transfers between devices with their start and end apart: 7, of which 0 were waited for; matrix products, arithmetic and copies ran while one was open for 37% of the time, Pallas kernels for 0%

commit v1 on v0

--- a/solution.py
+++ b/solution.py
@@ -1,8 +1,11 @@
+import functools
 import math
 
 import jax
 import jax.numpy as jnp
 from jax import lax
+from jax.experimental import pallas as pl
+from jax.experimental.pallas import tpu as pltpu
 from jax.sharding import PartitionSpec as P
 
 epsilon = 1e-05
@@ -86,7 +89,7 @@
     return lax.dynamic_slice_in_dim(weight_shard, tm_index * slice_width, slice_width, 1)
 
 
-def body(
+def body_blocks(
     frames,
     lengths,
     ln_gain,
@@ -149,6 +152,242 @@
     return attended[None]
 
 
+lanes = 128
+whole = pl.BlockSpec(memory_space=pltpu.VMEM)
+scalars = pl.BlockSpec(memory_space=pltpu.SMEM)
+
+
+def call(kernel, out_shape, args, scratch=(), flops=0, data=0):
+    return pl.pallas_call(
+        kernel,
+        out_shape=out_shape,
+        in_specs=[scalars] + [whole] * (len(args) - 1),
+        out_specs=jax.tree.map(lambda _: whole, out_shape),
+        scratch_shapes=list(scratch),
+        cost_estimate=pl.CostEstimate(flops=flops, bytes_accessed=data, transcendentals=0),
+        compiler_params=pltpu.CompilerParams(vmem_limit_bytes=48 * 1024 * 1024),
+    )(*args)
+
+
+def swap(block, axis, distance):
+    count = lax.axis_size(axis)
+    return lax.ppermute(block, axis, [(i, i ^ distance) for i in range(count)])
+
+
+def gather_pieces(block, axis):
+    count = lax.axis_size(axis)
+    pieces = {0: block}
+    for far in range(2, count, 2):
+        pieces[far] = swap(block, axis, far)
+    for far in range(0, count, 2):
+        pieces[far ^ 1] = swap(pieces[far], axis, 1)
+    return [pieces[k] for k in range(count)]
+
+
+def cut_kernel(tm_count, info, query_ref, key_ref, value_ref, out_ref, cut_ref, half_ref):
+    width = query_ref.shape[1] // tm_count
+    half_width = half_ref.shape[1]
+    for index in range(tm_count):
+
+        @pl.when(info[0] == index)
+        def _():
+            for part, ref in enumerate((query_ref, key_ref, value_ref)):
+                cut_ref[:, part * width : (part + 1) * width] = ref[
+                    :, index * width : (index + 1) * width
+                ]
+            side = (index % 2) * half_width
+            half_ref[...] = out_ref[:, side : side + half_width]
+
+
+def norm_kernel(info, frame_ref, gain_ref, normed_ref):
+    normed_ref[...] = layer_norm(frame_ref[...], gain_ref[...])
+
+
+def stack_kernel(count, info, *refs):
+    out_ref = refs[count]
+    rows = refs[0].shape[0]
+    for k in range(count):
+        start = pl.multiple_of((info[1] ^ k) * rows, 16)
+        out_ref[pl.ds(start, rows), :] = refs[k][...]
+
+
+def heads_kernel(tm_count, dp_count, head_size, info, *refs):
+    normed_refs, refs = refs[:tm_count], refs[tm_count:]
+    cut_refs, refs = refs[:dp_count], refs[dp_count:]
+    rel_ref, content_ref, position_ref = refs[:3]
+    context_refs = refs[3 : 3 + tm_count]
+    weight, relative, biases, query, key, value = refs[3 + tm_count :]
+    block_len = normed_refs[0].shape[0]
+    rows, cut_width = cut_refs[0].shape
+    width = cut_width // 3
+    head_count = width // head_size
+    wide = query.shape[1]
+    tm_index, dp_index, valid_len = info[0], info[1], info[2]
+
+    weight[...] = jnp.zeros_like(weight)
+    relative[...] = jnp.zeros_like(relative)
+    biases[...] = jnp.zeros_like(biases)
+    for h in range(head_count):
+        spot = slice(h * lanes, h * lanes + head_size)
+        relative[:, spot] = rel_ref[:, h * head_size : (h + 1) * head_size]
+        row = pl.ds(tm_index * head_count + h, 1)
+        biases[0:1, spot] = content_ref[row, :]
+        biases[1:2, spot] = position_ref[row, :]
+    for k in range(dp_count):
+        start = pl.multiple_of((dp_index ^ k) * rows, 16)
+        for part in range(3):
+            for h in range(head_count):
+                source = part * width + h * head_size
+                target = part * wide + h * lanes
+                weight[pl.ds(start, rows), target : target + head_size] = cut_refs[k][
+                    :, source : source + head_size
+                ]
+
+    for k in range(tm_count):
+        start = pl.multiple_of((tm_index ^ k) * block_len, block_len)
+        for part, ref in enumerate((query, key, value)):
+            ref[pl.ds(start, block_len), :] = jnp.dot(
+                normed_refs[k][...],
+                weight[:, part * wide : (part + 1) * wide],
+                preferred_element_type=jnp.float32,
+            ).astype(jnp.bfloat16)
+
+    scale = 1.0 / math.sqrt(head_size)
+    across = (((1,), (1,)), ((), ()))
+    for block in range(tm_count):
+        low, high = max(block - 1, 0), min(block + 1, tm_count - 1)
+        span = (high - low + 1) * block_len
+        first = (low - block + 1) * block_len
+        heads = []
+        for h in range(head_count):
+            lane = slice(h * lanes, (h + 1) * lanes)
+            widened = query[block * block_len : (block + 1) * block_len, lane].astype(jnp.float32)
+            with_content = (widened + biases[0:1, lane]).astype(jnp.bfloat16)
+            with_position = (widened + biases[1:2, lane]).astype(jnp.bfloat16)
+            keys = slice(low * block_len, (high + 1) * block_len)
+            content = lax.dot_general(
+                with_content, key[keys, lane], across, preferred_element_type=jnp.float32
+            )
+            position = lax.dot_general(
+                with_position,
+                relative[first : first + span + block_len, lane],
+                across,
+                preferred_element_type=jnp.float32,
+            )
+            shifted = pltpu.roll(position, span + 1, 1, stride=1, stride_axis=0)[:, :span]
+            key_pos = low * block_len + lax.broadcasted_iota(jnp.int32, (1, span), 1)
+            scores = jnp.where(key_pos < valid_len, (content + shifted) * scale, masked_score)
+            raised = jnp.exp(scores - jnp.max(scores, axis=1, keepdims=True))
+            totals = jnp.sum(raised, axis=1, keepdims=True)
+            weights = (raised * (1.0 / totals)).astype(jnp.bfloat16)
+            context = jnp.dot(weights, value[keys, lane], preferred_element_type=jnp.float32)
+            query_pos = block * block_len + lax.broadcasted_iota(jnp.int32, (block_len, 1), 0)
+            context = jnp.where(query_pos < valid_len, context, 0.0)
+            heads.append(context[:, :head_size].astype(jnp.bfloat16))
+        for k in range(tm_count):
+
+            @pl.when((tm_index ^ k) == block)
+            def _():
+                for h in range(head_count):
+                    context_refs[k][:, h * head_size : (h + 1) * head_size] = heads[h]
+
+
+def out_kernel(tm_count, info, *refs):
+    context_refs, (own_ref, other_ref, frame_ref, out_ref) = refs[:tm_count], refs[tm_count:]
+    width = context_refs[0].shape[1]
+    half_width = own_ref.shape[1]
+    for side, ref in enumerate((own_ref, other_ref)):
+        lane = pl.ds(pl.multiple_of((lax.rem(info[0], 2) ^ side) * half_width, lanes), half_width)
+        total = frame_ref[:, lane].astype(jnp.float32)
+        mixed = jnp.zeros_like(total)
+        for k in range(tm_count):
+            start = pl.multiple_of((info[0] ^ k) * width, 16)
+            mixed += jnp.dot(
+                context_refs[k][...], ref[pl.ds(start, width), :], preferred_element_type=jnp.float32
+            )
+        out_ref[:, lane] = (total + mixed).astype(jnp.bfloat16)
+
+
+def body_heads(
+    frames,
+    lengths,
+    ln_gain,
+    w_query,
+    w_key,
+    w_value,
+    w_output,
+    w_position,
+    bias_content,
+    bias_position,
+):
+    half = jnp.bfloat16
+    frame_rows = frames[0]
+    block_len, model_width = frame_rows.shape
+    head_size = bias_content.shape[1]
+    inner_width = w_query.shape[1]
+    tm_count, dp_count = lax.axis_size("tm"), lax.axis_size("dp")
+    tm_index, dp_index = lax.axis_index("tm"), lax.axis_index("dp")
+    info = jnp.stack((tm_index, dp_index, lengths[0])).astype(jnp.int32)
+    width = inner_width // tm_count
+    wide = width // head_size * lanes
+
+    cut, half_output = call(
+        functools.partial(cut_kernel, tm_count),
+        (
+            jax.ShapeDtypeStruct((w_query.shape[0], 3 * width), half),
+            jax.ShapeDtypeStruct((w_output.shape[0], model_width // 2), half),
+        ),
+        (info, w_query, w_key, w_value, w_output),
+    )
+    normed = call(
+        norm_kernel,
+        jax.ShapeDtypeStruct((block_len, model_width), half),
+        (info, frame_rows, ln_gain[None]),
+    )
+    cuts = gather_pieces(cut, "dp")
+    normed_all = gather_pieces(normed, "tm")
+    relative = jnp.dot(
+        sinusoid(4 * block_len, model_width), w_position, preferred_element_type=jnp.float32
+    ).astype(half)
+    output_pieces = gather_pieces(half_output, "dp")
+    total_len = tm_count * block_len
+    contexts = call(
+        functools.partial(heads_kernel, tm_count, dp_count, head_size),
+        [jax.ShapeDtypeStruct((block_len, width), half)] * tm_count,
+        (info, *normed_all, *cuts, relative, bias_content, bias_position),
+        [
+            pltpu.VMEM((model_width, 3 * wide), half),
+            pltpu.VMEM((4 * block_len, wide), half),
+            pltpu.VMEM((8, wide), jnp.float32),
+            pltpu.VMEM((total_len, wide), half),
+            pltpu.VMEM((total_len, wide), half),
+            pltpu.VMEM((total_len, wide), half),
+        ],
+    )
+    own_output = call(
+        functools.partial(stack_kernel, dp_count),
+        jax.ShapeDtypeStruct((inner_width, model_width // 2), half),
+        (info, *output_pieces),
+    )
+    other_output = swap(own_output, "tm", 1)
+    mine = [contexts[0]] + [swap(contexts[k], "tm", k) for k in range(1, tm_count)]
+    attended = call(
+        functools.partial(out_kernel, tm_count),
+        jax.ShapeDtypeStruct((block_len, model_width), half),
+        (info, *mine, own_output, other_output, frame_rows),
+    )
+    return attended[None]
+
+
+def body(*args):
+    tm_count, dp_count = lax.axis_size("tm"), lax.axis_size("dp")
+    head_count, head_size = args[-1].shape
+    powers = all(n > 1 and n & (n - 1) == 0 for n in (tm_count, dp_count))
+    if powers and head_count % tm_count == 0 and head_size <= lanes:
+        return body_heads(*args)
+    return body_blocks(*args)
+
+
 def solution(mesh):
     placed = (
         P("dp", "tm", None),

time: 257 us -> 108 us (0.42)
  the two profiles are of different devices: /device:TPU:0 before, /device:TPU:9 now
where the time goes in v1:
time: 108 us
  waiting for transfers between devices  45.4 us (42%)
  starting transfers between devices  22.3 us (21%)
  Pallas kernels  18.2 us (17%)
  other arithmetic  11.9 us (11%)
  local copies, waits for them, and re-layouts  7.3 us (7%)
  matrix products  1.92 us (2%)
    ppermute x21, waiting for transfers between devices, swap(): return lax.ppermute(block, axis, [(i, i ^ distance) for i in range(count)])  45.4 us
    ppermute x21, starting transfers between devices, swap(): return lax.ppermute(block, axis, [(i, i ^ distance) for i in range(count)])  22.3 us
    pallas_call x5, Pallas kernels, call(): pl.pallas_call(kernel, out_shape=out_shape, in_specs=[scalars] + [whole]...  18.2 us
    another operation x1, other arithmetic  11.8 us
    unnamed x30, local copies, waits for them, and re-layouts  5.4 us
  transfers between devices with their start and end apart: 21, of which 11 were waited for; matrix products, arithmetic and copies ran while one was open for 14% of the time, Pallas kernels for 13%

profile of v1, /device:TPU:9, one launch (start us, length us, event | category | flops | bytes accessed | tf_op | source)
XLA Modules:
  0.0 107.9 jit_solution(12587346581319388470)
XLA Ops:
  3.7 1.3 %collective-permute-start.1 = (bf16[256,1536]{1,0:T(8,128)(2,1)S(1)}, bf16[256,1536]{1,0:T(8,128)(2,1)}, u32[]{:S(2)}, u32[]{:S(2)}) collective-permute-start(bf16[256,1536]{1,0:T(8,128)(2,1)S(1)} %shard_map.100.refs_0_), channel_id=1, source_target_pairs={{0,2},{1,3},{2,0},{3,1},{4,6},{5,7},{6,4},{7,5},{8,10},{9,11},{10,... | collective-permute-start | bytes 2359304 | tf_op jit(solution)/shard_map/ppermute | solution.py:174
  5.9 2.3 %collective-permute-start.16 = (bf16[96,768]{1,0:T(8,128)(2,1)S(1)}, bf16[96,768]{1,0:T(8,128)(2,1)S(1)}, u32[]{:S(2)}, u32[]{:S(2)}) collective-permute-start(bf16[96,768]{1,0:T(8,128)(2,1)S(1)} %get-tuple-element.16.refs_0_), channel_id=1, source_target_pairs={{0,16},{4,20},{8,24},{12,28},{16,0},{20,4},{24,8},{28,12},{1,17},{... | collective-permute-start | bytes 442376 | tf_op jit(solution)/shard_map/ppermute | solution.py:174
  8.4 1.2 %collective-permute-start.13 = (bf16[96,768]{1,0:T(8,128)(2,1)S(1)}, bf16[96,768]{1,0:T(8,128)(2,1)S(1)}, u32[]{:S(2)}, u32[]{:S(2)}) collective-permute-start(bf16[96,768]{1,0:T(8,128)(2,1)S(1)} %get-tuple-element.16.refs_0_), channel_id=1, source_target_pairs={{0,4},{4,0},{8,12},{12,8},{16,20},{20,16},{24,28},{28,24},{1,5},{5... | collective-permute-start | bytes 442376 | tf_op jit(solution)/shard_map/ppermute | solution.py:174
  11.5 2.8 %collective-permute-done.16.refs_4_ = bf16[96,768]{1,0:T(8,128)(2,1)S(1)} collective-permute-done((bf16[96,768]{1,0:T(8,128)(2,1)S(1)}, bf16[96,768]{1,0:T(8,128)(2,1)S(1)}, u32[]{:S(2)}, u32[]{:S(2)}) %collective-permute-start.16) | collective-permute-done | bytes 147488 | tf_op jit(solution)/shard_map/ppermute | solution.py:174
  14.3 1.2 %collective-permute-start.17 = (bf16[96,768]{1,0:T(8,128)(2,1)S(1)}, bf16[96,768]{1,0:T(8,128)(2,1)S(1)}, u32[]{:S(2)}, u32[]{:S(2)}) collective-permute-start(bf16[96,768]{1,0:T(8,128)(2,1)S(1)} %collective-permute-done.16.refs_4_), channel_id=1, source_target_pairs={{0,4},{4,0},{8,12},{12,8},{16,20},{20,16},{24,28},{28,24},{1,5},{5... | collective-permute-start | bytes 442376 | tf_op jit(solution)/shard_map/ppermute | solution.py:174
  15.6 5.2 %collective-permute-done.18.refs_6_ = bf16[96,768]{1,0:T(8,128)(2,1)S(1)} collective-permute-done((bf16[96,768]{1,0:T(8,128)(2,1)S(1)}, bf16[96,768]{1,0:T(8,128)(2,1)S(1)}, u32[]{:S(2)}, u32[]{:S(2)}) %collective-permute-start.18) | collective-permute-done | bytes 147488 | tf_op jit(solution)/shard_map/ppermute | solution.py:174
  20.8 1.2 %collective-permute-start.19 = (bf16[96,768]{1,0:T(8,128)(2,1)S(1)}, bf16[96,768]{1,0:T(8,128)(2,1)S(1)}, u32[]{:S(2)}, u32[]{:S(2)}) collective-permute-start(bf16[96,768]{1,0:T(8,128)(2,1)S(1)} %collective-permute-done.18.refs_6_), channel_id=1, source_target_pairs={{0,4},{4,0},{8,12},{12,8},{16,20},{20,16},{24,28},{28,24},{1,5},{5... | collective-permute-start | bytes 442376 | tf_op jit(solution)/shard_map/ppermute | solution.py:174
  22.1 4.6 %collective-permute-done.19.refs_7_ = bf16[96,768]{1,0:T(8,128)(2,1)S(1)} collective-permute-done((bf16[96,768]{1,0:T(8,128)(2,1)S(1)}, bf16[96,768]{1,0:T(8,128)(2,1)S(1)}, u32[]{:S(2)}, u32[]{:S(2)}) %collective-permute-start.19) | collective-permute-done | bytes 147488 | tf_op jit(solution)/shard_map/ppermute | solution.py:174
  27.3 1.7 %collective-permute-start.20 = (bf16[768,768]{1,0:T(8,128)(2,1)S(1)}, bf16[768,768]{1,0:T(8,128)(2,1)}, u32[]{:S(2)}, u32[]{:S(2)}) collective-permute-start(bf16[768,768]{1,0:T(8,128)(2,1)S(1)} %shard_map.103.refs_4_), channel_id=1, source_target_pairs={{0,1},{1,0},{2,3},{3,2},{4,5},{5,4},{6,7},{7,6},{8,9},{9,8},{10,11... | collective-permute-start | bytes 3538952 | tf_op jit(solution)/shard_map/ppermute | solution.py:174
  29.8 1.3 %collective-permute-start.6 = (bf16[192,576]{1,0:T(8,128)(2,1)S(1)}, bf16[192,576]{1,0:T(8,128)(2,1)}, u32[]{:S(2)}, u32[]{:S(2)}) collective-permute-start(bf16[192,576]{1,0:T(8,128)(2,1)S(1)} %get-tuple-element.11.refs_4_), channel_id=1, source_target_pairs={{0,16},{4,20},{8,24},{12,28},{16,0},{20,4},{24,8},{28,12},{1,17},{... | collective-permute-start | bytes 663560 | tf_op jit(solution)/shard_map/ppermute | solution.py:174
  31.7 8.0 %collective-permute-done.4.refs_6_ = bf16[192,576]{1,0:T(8,128)(2,1)S(1)} collective-permute-done((bf16[192,576]{1,0:T(8,128)(2,1)S(1)}, bf16[192,576]{1,0:T(8,128)(2,1)S(1)}, u32[]{:S(2)}, u32[]{:S(2)}) %collective-permute-start.4) | collective-permute-done | bytes 221216 | tf_op jit(solution)/shard_map/ppermute | solution.py:174
  40.6 1.9 %collective-permute-done.6.refs_8_ = bf16[192,576]{1,0:T(8,128)(2,1)} collective-permute-done((bf16[192,576]{1,0:T(8,128)(2,1)S(1)}, bf16[192,576]{1,0:T(8,128)(2,1)}, u32[]{:S(2)}, u32[]{:S(2)}) %collective-permute-start.6) | collective-permute-done | bytes 221216 | tf_op jit(solution)/shard_map/ppermute | solution.py:174
  42.5 1.2 %collective-permute-start.3 = (bf16[192,576]{1,0:T(8,128)(2,1)S(1)}, bf16[192,576]{1,0:T(8,128)(2,1)S(1)}, u32[]{:S(2)}, u32[]{:S(2)}) collective-permute-start(bf16[192,576]{1,0:T(8,128)(2,1)S(1)} %get-tuple-element.11.refs_4_), channel_id=1, source_target_pairs={{0,4},{4,0},{8,12},{12,8},{16,20},{20,16},{24,28},{28,24},{1,5},{5... | collective-permute-start | bytes 663560 | tf_op jit(solution)/shard_map/ppermute | solution.py:174
  43.8 9.6 %collective-permute-done.8.refs_10_ = bf16[192,576]{1,0:T(8,128)(2,1)} collective-permute-done((bf16[192,576]{1,0:T(8,128)(2,1)S(1)}, bf16[192,576]{1,0:T(8,128)(2,1)}, u32[]{:S(2)}, u32[]{:S(2)}) %collective-permute-start.8) | collective-permute-done | bytes 221216 | tf_op jit(solution)/shard_map/ppermute | solution.py:174
  54.6 11.8 %fusion = (bf16[1024,768]{1,0:T(8,128)(2,1)S(1)}, bf16[1024,768]{1,0:T(8,128)(2,1)S(1)}) fusion(f32[768]{0:T(1024)S(1)} %multiply_exponential_fusion, f32[1024]{0:T(1024)S(1)} %iota_add_fusion), kind=kLoop, calls=%fused_computation.2 | loop fusion | flops 2359296 | bytes 3152896 | tf_op jit(solution)/shard_map/convert
  68.1 1.2 %collective-permute-start.9 = (bf16[192,576]{1,0:T(8,128)(2,1)}, bf16[192,576]{1,0:T(8,128)(2,1)}, u32[]{:S(2)}, u32[]{:S(2)}) collective-permute-start(bf16[192,576]{1,0:T(8,128)(2,1)} %collective-permute-done.8.refs_10_), channel_id=1, source_target_pairs={{0,4},{4,0},{8,12},{12,8},{16,20},{20,16},{24,28},{28,24},{1,5},{5... | collective-permute-start | bytes 663560 | tf_op jit(solution)/shard_map/ppermute | solution.py:174
  69.3 1.9 %fusion.6 = bf16[1024,192]{0,1:T(8,128)(2,1)} fusion(bf16[1536,192]{0,1:T(8,128)(2,1)S(1)} %copy-done, bf16[1024,768]{1,0:T(8,128)(2,1)S(1)} %get-tuple-element.18, bf16[1024,768]{1,0:T(8,128)(2,1)S(1)} %get-tuple-element.17), kind=kOutput, calls=%fused_computation.8 | convolution fusion | flops 610467840 | bytes 4128768 | tf_op jit(solution)/shard_map/dot_general | solution.py:349
  73.5 5.3 %collective-permute-done.9.refs_11_ = bf16[192,576]{1,0:T(8,128)(2,1)} collective-permute-done((bf16[192,576]{1,0:T(8,128)(2,1)}, bf16[192,576]{1,0:T(8,128)(2,1)}, u32[]{:S(2)}, u32[]{:S(2)}) %collective-permute-start.9) | collective-permute-done | bytes 221216 | tf_op jit(solution)/shard_map/ppermute | solution.py:174
  81.6 12.6 %shard_map.102 = (bf16[256,192]{1,0:T(8,128)(2,1)S(1)}, bf16[256,192]{1,0:T(8,128)(2,1)S(1)}, bf16[256,192]{1,0:T(8,128)(2,1)S(1)}, bf16[256,192]{1,0:T(8,128)(2,1)S(1)}) custom-call(s32[3]{0:T(128)S(1)} %pad_add_fusion.info, bf16[256,1536]{1,0:T(8,128)(2,1)S(1)} %shard_map.100.refs_0_, bf16[256,1536]{1,0:T(8,128)(2,1)} %collective-permute-done.refs_1_, ...), custom_call_target="tpu_custom_call" | custom-call | tf_op jit(solution)/shard_map/pallas_call | solution.py:161
  94.2 2.4 %collective-permute-start.10 = (bf16[256,192]{1,0:T(8,128)(2,1)S(1)}, bf16[256,192]{1,0:T(8,128)(2,1)S(1)}, u32[]{:S(2)}, u32[]{:S(2)}) collective-permute-start(bf16[256,192]{1,0:T(8,128)(2,1)S(1)} %get-tuple-element.13), channel_id=1, source_target_pairs={{0,1},{1,0},{2,3},{3,2},{4,5},{5,4},{6,7},{7,6},{8,9},{9,8},{10,11... | collective-permute-start | bytes 294920 | tf_op jit(solution)/shard_map/ppermute | solution.py:174
  97.0 1.4 %collective-permute-start.12 = (bf16[256,192]{1,0:T(8,128)(2,1)S(1)}, bf16[256,192]{1,0:T(8,128)(2,1)S(1)}, u32[]{:S(2)}, u32[]{:S(2)}) collective-permute-start(bf16[256,192]{1,0:T(8,128)(2,1)S(1)} %get-tuple-element.15), channel_id=1, source_target_pairs={{0,3},{1,2},{2,1},{3,0},{4,7},{5,6},{6,5},{7,4},{8,11},{9,10},{10,... | collective-permute-start | bytes 294920 | tf_op jit(solution)/shard_map/ppermute | solution.py:174
  98.4 3.4 %collective-permute-done.11.refs_2_ = bf16[256,192]{1,0:T(8,128)(2,1)S(1)} collective-permute-done((bf16[256,192]{1,0:T(8,128)(2,1)S(1)}, bf16[256,192]{1,0:T(8,128)(2,1)S(1)}, u32[]{:S(2)}, u32[]{:S(2)}) %collective-permute-start.11) | collective-permute-done | bytes 98336 | tf_op jit(solution)/shard_map/ppermute | solution.py:174
  101.7 3.0 %collective-permute-done.12.refs_3_ = bf16[256,192]{1,0:T(8,128)(2,1)S(1)} collective-permute-done((bf16[256,192]{1,0:T(8,128)(2,1)S(1)}, bf16[256,192]{1,0:T(8,128)(2,1)S(1)}, u32[]{:S(2)}, u32[]{:S(2)}) %collective-permute-start.12) | collective-permute-done | bytes 98336 | tf_op jit(solution)/shard_map/ppermute | solution.py:174
  104.7 3.2 %shard_map.104 = bf16[256,1536]{1,0:T(8,128)(2,1)} custom-call(s32[3]{0:T(128)S(1)} %pad_add_fusion.info, bf16[256,192]{1,0:T(8,128)(2,1)S(1)} %get-tuple-element.12.refs_0_, bf16[256,192]{1,0:T(8,128)(2,1)S(1)} %collective-permute-done.10.refs_1_, bf16[256,192]{1,0:T(8,128)(2,1)S(1)} %collective-permute-done.11.refs_2_, ...), custom_call_target="tpu_custom_call" | custom-call | tf_op jit(solution)/shard_map/pallas_call | solution.py:161
  (60 shorter events, 17.1 us)
Async XLA Ops:
  0.0 69.3 %copy-start = (bf16[1536,192]{0,1:T(8,128)(2,1)S(1)}, bf16[1536,192]{0,1:T(8,128)(2,1)}, u32[]{:S(2)}) copy-start(bf16[1536,192]{0,1:T(8,128)(2,1)} %param.17) | copy-start | bytes 1769476
  3.7 36.8 %collective-permute-start.1 = (bf16[256,1536]{1,0:T(8,128)(2,1)S(1)}, bf16[256,1536]{1,0:T(8,128)(2,1)}, u32[]{:S(2)}, u32[]{:S(2)}) collective-permute-start(bf16[256,1536]{1,0:T(8,128)(2,1)S(1)} %shard_map.100.refs_0_), channel_id=1, source_target_pairs={{0,2},{1,3},{2,0},{3,1},{4,6},{5,7},{6,4},{7,5},{8,10},{9,11},{10,... | collective-permute-start | bytes 2359304 | tf_op jit(solution)/shard_map/ppermute | solution.py:174
  5.7 4.6 %collective-permute-start.14 = (bf16[96,768]{1,0:T(8,128)(2,1)S(1)}, bf16[96,768]{1,0:T(8,128)(2,1)S(1)}, u32[]{:S(2)}, u32[]{:S(2)}) collective-permute-start(bf16[96,768]{1,0:T(8,128)(2,1)S(1)} %get-tuple-element.16.refs_0_), channel_id=1, source_target_pairs={{0,8},{4,12},{8,0},{12,4},{16,24},{20,28},{24,16},{28,20},{1,9},{5... | collective-permute-start | bytes 442376 | tf_op jit(solution)/shard_map/ppermute | solution.py:174
  5.9 8.4 %collective-permute-start.16 = (bf16[96,768]{1,0:T(8,128)(2,1)S(1)}, bf16[96,768]{1,0:T(8,128)(2,1)S(1)}, u32[]{:S(2)}, u32[]{:S(2)}) collective-permute-start(bf16[96,768]{1,0:T(8,128)(2,1)S(1)} %get-tuple-element.16.refs_0_), channel_id=1, source_target_pairs={{0,16},{4,20},{8,24},{12,28},{16,0},{20,4},{24,8},{28,12},{1,17},{... | collective-permute-start | bytes 442376 | tf_op jit(solution)/shard_map/ppermute | solution.py:174
  8.2 12.6 %collective-permute-start.18 = (bf16[96,768]{1,0:T(8,128)(2,1)S(1)}, bf16[96,768]{1,0:T(8,128)(2,1)S(1)}, u32[]{:S(2)}, u32[]{:S(2)}) collective-permute-start(bf16[96,768]{1,0:T(8,128)(2,1)S(1)} %get-tuple-element.16.refs_0_), channel_id=1, source_target_pairs={{0,24},{4,28},{8,16},{12,20},{16,8},{20,12},{24,0},{28,4},{1,25},{... | collective-permute-start | bytes 442376 | tf_op jit(solution)/shard_map/ppermute | solution.py:174
  8.4 13.6 %collective-permute-start.13 = (bf16[96,768]{1,0:T(8,128)(2,1)S(1)}, bf16[96,768]{1,0:T(8,128)(2,1)S(1)}, u32[]{:S(2)}, u32[]{:S(2)}) collective-permute-start(bf16[96,768]{1,0:T(8,128)(2,1)S(1)} %get-tuple-element.16.refs_0_), channel_id=1, source_target_pairs={{0,4},{4,0},{8,12},{12,8},{16,20},{20,16},{24,28},{28,24},{1,5},{5... | collective-permute-start | bytes 442376 | tf_op jit(solution)/shard_map/ppermute | solution.py:174
  10.3 11.8 %collective-permute-start.15 = (bf16[96,768]{1,0:T(8,128)(2,1)S(1)}, bf16[96,768]{1,0:T(8,128)(2,1)S(1)}, u32[]{:S(2)}, u32[]{:S(2)}) collective-permute-start(bf16[96,768]{1,0:T(8,128)(2,1)S(1)} %collective-permute-done.14.refs_2_), channel_id=1, source_target_pairs={{0,4},{4,0},{8,12},{12,8},{16,20},{20,16},{24,28},{28,24},{1,5},{5... | collective-permute-start | bytes 442376 | tf_op jit(solution)/shard_map/ppermute | solution.py:174
  14.3 7.7 %collective-permute-start.17 = (bf16[96,768]{1,0:T(8,128)(2,1)S(1)}, bf16[96,768]{1,0:T(8,128)(2,1)S(1)}, u32[]{:S(2)}, u32[]{:S(2)}) collective-permute-start(bf16[96,768]{1,0:T(8,128)(2,1)S(1)} %collective-permute-done.16.refs_4_), channel_id=1, source_target_pairs={{0,4},{4,0},{8,12},{12,8},{16,20},{20,16},{24,28},{28,24},{1,5},{5... | collective-permute-start | bytes 442376 | tf_op jit(solution)/shard_map/ppermute | solution.py:174
  20.8 5.9 %collective-permute-start.19 = (bf16[96,768]{1,0:T(8,128)(2,1)S(1)}, bf16[96,768]{1,0:T(8,128)(2,1)S(1)}, u32[]{:S(2)}, u32[]{:S(2)}) collective-permute-start(bf16[96,768]{1,0:T(8,128)(2,1)S(1)} %collective-permute-done.18.refs_6_), channel_id=1, source_target_pairs={{0,4},{4,0},{8,12},{12,8},{16,20},{20,16},{24,28},{28,24},{1,5},{5... | collective-permute-start | bytes 442376 | tf_op jit(solution)/shard_map/ppermute | solution.py:174
  27.3 71.1 %collective-permute-start.20 = (bf16[768,768]{1,0:T(8,128)(2,1)S(1)}, bf16[768,768]{1,0:T(8,128)(2,1)}, u32[]{:S(2)}, u32[]{:S(2)}) collective-permute-start(bf16[768,768]{1,0:T(8,128)(2,1)S(1)} %shard_map.103.refs_4_), channel_id=1, source_target_pairs={{0,1},{1,0},{2,3},{3,2},{4,5},{5,4},{6,7},{7,6},{8,9},{9,8},{10,11... | collective-permute-start | bytes 3538952 | tf_op jit(solution)/shard_map/ppermute | solution.py:174
  29.0 10.7 %collective-permute-start.4 = (bf16[192,576]{1,0:T(8,128)(2,1)S(1)}, bf16[192,576]{1,0:T(8,128)(2,1)S(1)}, u32[]{:S(2)}, u32[]{:S(2)}) collective-permute-start(bf16[192,576]{1,0:T(8,128)(2,1)S(1)} %get-tuple-element.11.refs_4_), channel_id=1, source_target_pairs={{0,8},{4,12},{8,0},{12,4},{16,24},{20,28},{24,16},{28,20},{1,9},{5... | collective-permute-start | bytes 663560 | tf_op jit(solution)/shard_map/ppermute | solution.py:174
  29.8 12.8 %collective-permute-start.6 = (bf16[192,576]{1,0:T(8,128)(2,1)S(1)}, bf16[192,576]{1,0:T(8,128)(2,1)}, u32[]{:S(2)}, u32[]{:S(2)}) collective-permute-start(bf16[192,576]{1,0:T(8,128)(2,1)S(1)} %get-tuple-element.11.refs_4_), channel_id=1, source_target_pairs={{0,16},{4,20},{8,24},{12,28},{16,0},{20,4},{24,8},{28,12},{1,17},{... | collective-permute-start | bytes 663560 | tf_op jit(solution)/shard_map/ppermute | solution.py:174
  31.1 22.3 %collective-permute-start.8 = (bf16[192,576]{1,0:T(8,128)(2,1)S(1)}, bf16[192,576]{1,0:T(8,128)(2,1)}, u32[]{:S(2)}, u32[]{:S(2)}) collective-permute-start(bf16[192,576]{1,0:T(8,128)(2,1)S(1)} %get-tuple-element.11.refs_4_), channel_id=1, source_target_pairs={{0,24},{4,28},{8,16},{12,20},{16,8},{20,12},{24,0},{28,4},{1,25},{... | collective-permute-start | bytes 663560 | tf_op jit(solution)/shard_map/ppermute | solution.py:174
  39.7 26.7 %copy-start.7 = (bf16[192,576]{1,0:T(8,128)(2,1)}, bf16[192,576]{1,0:T(8,128)(2,1)S(1)}, u32[]{:S(2)}) copy-start(bf16[192,576]{1,0:T(8,128)(2,1)S(1)} %collective-permute-done.4.refs_6_) | copy-start | bytes 663556
  39.7 39.1 %collective-permute-start = (bf16[256,1536]{1,0:T(8,128)(2,1)S(1)}, bf16[256,1536]{1,0:T(8,128)(2,1)}, u32[]{:S(2)}, u32[]{:S(2)}) collective-permute-start(bf16[256,1536]{1,0:T(8,128)(2,1)S(1)} %shard_map.100.refs_0_), channel_id=1, source_target_pairs={{0,1},{1,0},{2,3},{3,2},{4,5},{5,4},{6,7},{7,6},{8,9},{9,8},{10,11... | collective-permute-start | bytes 2359304 | tf_op jit(solution)/shard_map/ppermute | solution.py:174
  40.5 38.2 %collective-permute-start.2 = (bf16[256,1536]{1,0:T(8,128)(2,1)}, bf16[256,1536]{1,0:T(8,128)(2,1)}, u32[]{:S(2)}, u32[]{:S(2)}) collective-permute-start(bf16[256,1536]{1,0:T(8,128)(2,1)} %collective-permute-done.1.refs_2_), channel_id=1, source_target_pairs={{0,1},{1,0},{2,3},{3,2},{4,5},{5,4},{6,7},{7,6},{8,9},{9,8},{10,11... | collective-permute-start | bytes 2359304 | tf_op jit(solution)/shard_map/ppermute | solution.py:174
  42.5 23.9 %collective-permute-start.3 = (bf16[192,576]{1,0:T(8,128)(2,1)S(1)}, bf16[192,576]{1,0:T(8,128)(2,1)S(1)}, u32[]{:S(2)}, u32[]{:S(2)}) collective-permute-start(bf16[192,576]{1,0:T(8,128)(2,1)S(1)} %get-tuple-element.11.refs_4_), channel_id=1, source_target_pairs={{0,4},{4,0},{8,12},{12,8},{16,20},{20,16},{24,28},{28,24},{1,5},{5... | collective-permute-start | bytes 663560 | tf_op jit(solution)/shard_map/ppermute | solution.py:174
  53.4 14.0 %collective-permute-start.5 = (bf16[192,576]{1,0:T(8,128)(2,1)S(1)}, bf16[192,576]{1,0:T(8,128)(2,1)S(1)}, u32[]{:S(2)}, u32[]{:S(2)}) collective-permute-start(bf16[192,576]{1,0:T(8,128)(2,1)S(1)} %collective-permute-done.4.refs_6_), channel_id=1, source_target_pairs={{0,4},{4,0},{8,12},{12,8},{16,20},{20,16},{24,28},{28,24},{1,5},{5... | collective-permute-start | bytes 663560 | tf_op jit(solution)/shard_map/ppermute | solution.py:174
  67.2 6.3 %collective-permute-start.7 = (bf16[192,576]{1,0:T(8,128)(2,1)}, bf16[192,576]{1,0:T(8,128)(2,1)}, u32[]{:S(2)}, u32[]{:S(2)}) collective-permute-start(bf16[192,576]{1,0:T(8,128)(2,1)} %collective-permute-done.6.refs_8_), channel_id=1, source_target_pairs={{0,4},{4,0},{8,12},{12,8},{16,20},{20,16},{24,28},{28,24},{1,5},{5... | collective-permute-start | bytes 663560 | tf_op jit(solution)/shard_map/ppermute | solution.py:174
  68.1 10.7 %collective-permute-start.9 = (bf16[192,576]{1,0:T(8,128)(2,1)}, bf16[192,576]{1,0:T(8,128)(2,1)}, u32[]{:S(2)}, u32[]{:S(2)}) collective-permute-start(bf16[192,576]{1,0:T(8,128)(2,1)} %collective-permute-done.8.refs_10_), channel_id=1, source_target_pairs={{0,4},{4,0},{8,12},{12,8},{16,20},{20,16},{24,28},{28,24},{1,5},{5... | collective-permute-start | bytes 663560 | tf_op jit(solution)/shard_map/ppermute | solution.py:174
  72.4 32.3 %copy-start.2 = (bf16[1,256,1536]{2,1,0:T(8,128)(2,1)S(1)}, bf16[1,256,1536]{2,1,0:T(8,128)(2,1)}, u32[]{:S(2)}) copy-start(bf16[1,256,1536]{2,1,0:T(8,128)(2,1)} %param.10) | copy-start | bytes 2359300
  94.2 4.2 %collective-permute-start.10 = (bf16[256,192]{1,0:T(8,128)(2,1)S(1)}, bf16[256,192]{1,0:T(8,128)(2,1)S(1)}, u32[]{:S(2)}, u32[]{:S(2)}) collective-permute-start(bf16[256,192]{1,0:T(8,128)(2,1)S(1)} %get-tuple-element.13), channel_id=1, source_target_pairs={{0,1},{1,0},{2,3},{3,2},{4,5},{5,4},{6,7},{7,6},{8,9},{9,8},{10,11... | collective-permute-start | bytes 294920 | tf_op jit(solution)/shard_map/ppermute | solution.py:174
  96.7 5.1 %collective-permute-start.11 = (bf16[256,192]{1,0:T(8,128)(2,1)S(1)}, bf16[256,192]{1,0:T(8,128)(2,1)S(1)}, u32[]{:S(2)}, u32[]{:S(2)}) collective-permute-start(bf16[256,192]{1,0:T(8,128)(2,1)S(1)} %get-tuple-element.14), channel_id=1, source_target_pairs={{0,2},{1,3},{2,0},{3,1},{4,6},{5,7},{6,4},{7,5},{8,10},{9,11},{10,... | collective-permute-start | bytes 294920 | tf_op jit(solution)/shard_map/ppermute | solution.py:174
  97.0 7.8 %collective-permute-start.12 = (bf16[256,192]{1,0:T(8,128)(2,1)S(1)}, bf16[256,192]{1,0:T(8,128)(2,1)S(1)}, u32[]{:S(2)}, u32[]{:S(2)}) collective-permute-start(bf16[256,192]{1,0:T(8,128)(2,1)S(1)} %get-tuple-element.15), channel_id=1, source_target_pairs={{0,3},{1,2},{2,1},{3,0},{4,7},{5,6},{6,5},{7,4},{8,11},{9,10},{10,... | collective-permute-start | bytes 294920 | tf_op jit(solution)/shard_map/ppermute | solution.py:174
  (12 other events, 33.6 us)

commit v2 on v0

--- a/solution.py
+++ b/solution.py
@@ -1,8 +1,11 @@
+import functools
 import math
 
 import jax
 import jax.numpy as jnp
 from jax import lax
+from jax.experimental import pallas as pl
+from jax.experimental.pallas import tpu as pltpu
 from jax.sharding import PartitionSpec as P
 
 epsilon = 1e-05
@@ -86,7 +89,7 @@
     return lax.dynamic_slice_in_dim(weight_shard, tm_index * slice_width, slice_width, 1)
 
 
-def body(
+def body_blocks(
     frames,
     lengths,
     ln_gain,
@@ -149,6 +152,429 @@
     return attended[None]
 
 
+lanes = 128
+half = jnp.bfloat16
+across = (((1,), (1,)), ((), ()))
+near = pl.BlockSpec(memory_space=pltpu.VMEM)
+far = pl.BlockSpec(memory_space=pl.ANY)
+scalars = pl.BlockSpec(memory_space=pltpu.SMEM)
+
+
+def call(kernel, out_shape, operands, scratch=(), micros=1.0, room=24):
+    arrays, specs = zip(*operands)
+    return pl.pallas_call(
+        kernel,
+        out_shape=out_shape,
+        in_specs=list(specs),
+        out_specs=jax.tree.map(lambda _: near, out_shape),
+        scratch_shapes=list(scratch),
+        cost_estimate=pl.CostEstimate(
+            flops=int(micros * 1.1e9), bytes_accessed=4096, transcendentals=0
+        ),
+        compiler_params=pltpu.CompilerParams(vmem_limit_bytes=room * 1024 * 1024),
+    )(*arrays)
+
+
+def shaped(*shape):
+    return jax.ShapeDtypeStruct(shape, half)
+
+
+def swap(block, axis, distance):
+    count = lax.axis_size(axis)
+    return lax.ppermute(block, axis, [(i, i ^ distance) for i in range(count)])
+
+
+def send_far(block, axis):
+    return {0: block} | {k: swap(block, axis, k) for k in range(2, lax.axis_size(axis), 2)}
+
+
+def send_beside(pieces, axis):
+    everything = pieces | {k ^ 1: swap(pieces[k], axis, 1) for k in pieces}
+    return [everything[k] for k in sorted(everything)]
+
+
+def later(value, *others):
+    return lax.optimization_barrier((value, *others))[0]
+
+
+def cut_first_kernel(tm_count, info, query_ref, key_ref, cut_ref):
+    width = query_ref.shape[1] // tm_count
+    for index in range(tm_count):
+
+        @pl.when(info[0] == index)
+        def _():
+            columns = slice(index * width, (index + 1) * width)
+            cut_ref[:, :width] = query_ref[:, columns]
+            cut_ref[:, width:] = key_ref[:, columns]
+
+
+def cut_second_kernel(tm_count, info, *refs):
+    value_ref, cut_ref = refs[0], refs[-1]
+    rows = value_ref.shape[0]
+    width = value_ref.shape[1] // tm_count
+    for index in range(tm_count):
+
+        @pl.when(info[0] == index)
+        def _():
+            columns = slice(index * width, (index + 1) * width)
+            cut_ref[:, :width] = value_ref[: rows // 2, columns]
+            cut_ref[:, width:] = value_ref[rows // 2 :, columns]
+
+
+def cut_output_kernel(info, *refs):
+    output_ref, half_ref = refs[0], refs[-1]
+    width = half_ref.shape[1]
+    start = pl.multiple_of(lax.rem(info[0], 2) * width, lanes)
+    half_ref[...] = output_ref[:, pl.ds(start, width)]
+
+
+def norm_kernel(info, frame_ref, gain_ref, normed_ref):
+    normed_ref[...] = layer_norm(frame_ref[...], gain_ref[...])
+
+
+def angle_tables(row_count, model_width, step):
+    half_width = model_width // 2
+    frequency = jnp.exp(
+        jnp.arange(half_width, dtype=jnp.float32) * (-2.0 * math.log(10000.0) / model_width)
+    )
+    coarse = jnp.arange(row_count // step, dtype=jnp.float32) * step - (row_count // 2 - 1)
+    fine = jnp.arange(step, dtype=jnp.float32)
+    angles = jnp.concatenate([coarse, fine])[:, None] * frequency[None, :]
+    return jnp.sin(angles), jnp.cos(angles)
+
+
+def relative_kernel(head_size, step, info, sin_ref, cos_ref, position_ref, rel_ref, encoding):
+    row_count, model_width = encoding.shape
+    half_width = model_width // 2
+    coarse_count = row_count // step
+    fine_sin, fine_cos = sin_ref[coarse_count:, :], cos_ref[coarse_count:, :]
+    for index in range(coarse_count):
+        coarse_sin, coarse_cos = sin_ref[index : index + 1, :], cos_ref[index : index + 1, :]
+        rows = slice(index * step, (index + 1) * step)
+        encoding[rows, :half_width] = (coarse_sin * fine_cos + coarse_cos * fine_sin).astype(half)
+        encoding[rows, half_width:] = (coarse_cos * fine_cos - coarse_sin * fine_sin).astype(half)
+    projected = lax.dot_general(
+        encoding[...], position_ref[...], across, preferred_element_type=jnp.float32
+    ).astype(half)
+    rel_ref[...] = jnp.zeros_like(rel_ref)
+    for h in range(rel_ref.shape[1] // lanes):
+        rel_ref[:, h * lanes : h * lanes + head_size] = projected[
+            :, h * head_size : (h + 1) * head_size
+        ]
+
+
+def load(sources, targets, sems):
+    copies = [
+        pltpu.make_async_copy(source, target, sems.at[i])
+        for i, (source, target) in enumerate(zip(sources, targets))
+    ]
+    for copy in copies:
+        copy.start()
+    return copies
+
+
+def query_key_kernel(tm_count, dp_count, head_size, info, *refs):
+    normed_refs, refs = refs[:tm_count], refs[tm_count:]
+    cut_refs, refs = refs[:dp_count], refs[dp_count:]
+    query_ref, key_ref, normed, cuts, weight, cut_sems, normed_sems = refs[1:]
+    block_len = normed.shape[0] // tm_count
+    rows, cut_width = cuts.shape[1:]
+    wide = query_ref.shape[1]
+    width = cut_width // 2
+    spots = [pl.multiple_of((info[0] ^ k) * block_len, block_len) for k in range(tm_count)]
+    cut_copies = load(cut_refs, [cuts.at[k] for k in range(dp_count)], cut_sems)
+    normed_copies = load(
+        normed_refs, [normed.at[pl.ds(spot, block_len), :] for spot in spots], normed_sems
+    )
+    weight[...] = jnp.zeros_like(weight)
+    for k in range(dp_count):
+        cut_copies[k].wait()
+        start = pl.multiple_of((info[1] ^ k) * rows, 16)
+        for part in range(2):
+            for h in range(width // head_size):
+                source = part * width + h * head_size
+                target = part * wide + h * lanes
+                weight[pl.ds(start, rows), target : target + head_size] = cuts[
+                    k, :, source : source + head_size
+                ]
+    for copy in normed_copies:
+        copy.wait()
+    for part, ref in enumerate((query_ref, key_ref)):
+        ref[...] = jnp.dot(
+            normed[...],
+            weight[:, part * wide : (part + 1) * wide],
+            preferred_element_type=jnp.float32,
+        ).astype(half)
+
+
+def softmax_kernel(
+    tm_count, info, query, key, relative, content_ref, position_ref, weights_ref, biases
+):
+    head_count, head_size = weights_ref.shape[1], content_ref.shape[1]
+    block_len = weights_ref.shape[2]
+    tm_index, valid_len = info[0], info[2]
+    biases[...] = jnp.zeros_like(biases)
+    for h in range(head_count):
+        row = pl.ds(tm_index * head_count + h, 1)
+        biases[0:1, h * lanes : h * lanes + head_size] = content_ref[row, :]
+        biases[1:2, h * lanes : h * lanes + head_size] = position_ref[row, :]
+    scale = 1.0 / math.sqrt(head_size)
+    for block in range(tm_count):
+        low, high = max(block - 1, 0), min(block + 1, tm_count - 1)
+        span = (high - low + 1) * block_len
+        first = (low - block + 1) * block_len
+        keys = slice(low * block_len, (high + 1) * block_len)
+        for h in range(head_count):
+            lane = slice(h * lanes, (h + 1) * lanes)
+            widened = query[block * block_len : (block + 1) * block_len, lane].astype(jnp.float32)
+            with_content = (widened + biases[0:1, lane]).astype(half)
+            with_position = (widened + biases[1:2, lane]).astype(half)
+            content = lax.dot_general(
+                with_content, key[keys, lane], across, preferred_element_type=jnp.float32
+            )
+            position = lax.dot_general(
+                with_position,
+                relative[first : first + span + block_len, lane],
+                across,
+                preferred_element_type=jnp.float32,
+            )
+            shifted = pltpu.roll(position, span + 1, 1, stride=1, stride_axis=0)[:, :span]
+            key_pos = low * block_len + lax.broadcasted_iota(jnp.int32, (1, span), 1)
+            scores = jnp.where(key_pos < valid_len, (content + shifted) * scale, masked_score)
+            raised = jnp.exp(scores - jnp.max(scores, axis=1, keepdims=True))
+            totals = jnp.sum(raised, axis=1, keepdims=True)
+            if first > 0:
+                weights_ref[block, h, :, :first] = jnp.zeros((block_len, first), half)
+            weights_ref[block, h, :, first : first + span] = (raised * (1.0 / totals)).astype(half)
+            if first + span < 3 * block_len:
+                weights_ref[block, h, :, first + span :] = jnp.zeros(
+                    (block_len, 3 * block_len - first - span), half
+                )
+
+
+def mix_values(info, distances, weights_ref, value, context_refs, head_size):
+    block_len = weights_ref.shape[2]
+    for k, context_ref in zip(distances, context_refs):
+        block = info[0] ^ k
+        query_pos = block * block_len + lax.broadcasted_iota(jnp.int32, (block_len, 1), 0)
+        window = pl.ds(pl.multiple_of(block * block_len, block_len), 3 * block_len)
+        width = context_ref.shape[1] // 2
+        for h in range(weights_ref.shape[1]):
+            context = jnp.dot(
+                weights_ref[block, h],
+                value[window, h * lanes : (h + 1) * lanes],
+                preferred_element_type=jnp.float32,
+            )
+            context = jnp.where(query_pos < info[2], context, 0.0)[:, :head_size].astype(half)
+            for part in range(2):
+                lane = part * width + h * head_size
+                context_ref[:, lane : lane + head_size] = context[
+                    part * (block_len // 2) : (part + 1) * (block_len // 2), :
+                ]
+
+
+def value_kernel(tm_count, dp_count, head_size, distances, info, *refs):
+    normed, cut_refs, refs = refs[0], refs[1 : 1 + dp_count], refs[1 + dp_count :]
+    weights_ref, value, refs = refs[0], refs[1], refs[2:]
+    context_refs, (cuts, weight, cut_sems) = refs[: len(distances)], refs[len(distances) :]
+    block_len = normed.shape[0] // tm_count
+    rows = cuts.shape[1]
+    width = cuts.shape[2] // 2
+    cut_copies = load(cut_refs, [cuts.at[k] for k in range(dp_count)], cut_sems)
+    weight[...] = jnp.zeros_like(weight)
+    value[:block_len, :] = jnp.zeros_like(value[:block_len, :])
+    value[(tm_count + 1) * block_len :, :] = jnp.zeros_like(value[:block_len, :])
+    for k in range(dp_count):
+        cut_copies[k].wait()
+        start = pl.multiple_of((info[1] ^ k) * rows * 2, 16)
+        for part in range(2):
+            for h in range(width // head_size):
+                source = part * width + h * head_size
+                weight[
+                    pl.ds(start + part * rows, rows), h * lanes : h * lanes + head_size
+                ] = cuts[k, :, source : source + head_size]
+    value[block_len : (tm_count + 1) * block_len, :] = jnp.dot(
+        normed[...], weight[...], preferred_element_type=jnp.float32
+    ).astype(half)
+    mix_values(info, distances, weights_ref, value, context_refs, head_size)
+
+
+def mix_kernel(head_size, distances, info, weights_ref, value, *context_refs):
+    mix_values(info, distances, weights_ref, value, context_refs, head_size)
+
+
+def stack_kernel(count, info, *refs):
+    stacked = refs[count]
+    sems = refs[count + 1]
+    rows = refs[0].shape[0]
+    spots = [pl.multiple_of((info[1] ^ k) * rows, 16) for k in range(count)]
+    for copy in load(refs[:count], [stacked.at[pl.ds(spot, rows), :] for spot in spots], sems):
+        copy.wait()
+
+
+def out_kernel(tm_count, info, *refs):
+    context_refs, (own_ref, other_ref, frame_ref, out_ref) = refs[:tm_count], refs[tm_count:]
+    width = context_refs[0].shape[1] // 2
+    half_width = own_ref.shape[1]
+    contexts = [
+        jnp.concatenate([ref[:, :width], ref[:, width:]], axis=0) for ref in context_refs
+    ]
+    for side, ref in enumerate((own_ref, other_ref)):
+        lane = pl.ds(pl.multiple_of((lax.rem(info[0], 2) ^ side) * half_width, lanes), half_width)
+        mixed = jnp.zeros((contexts[0].shape[0], half_width), jnp.float32)
+        for k in range(tm_count):
+            start = pl.multiple_of((info[0] ^ k) * width, 16)
+            mixed += jnp.dot(
+                contexts[k], ref[pl.ds(start, width), :], preferred_element_type=jnp.float32
+            )
+        out_ref[:, lane] = (frame_ref[:, lane].astype(jnp.float32) + mixed).astype(half)
+
+
+def body_heads(
+    frames,
+    lengths,
+    ln_gain,
+    w_query,
+    w_key,
+    w_value,
+    w_output,
+    w_position,
+    bias_content,
+    bias_position,
+):
+    frame_rows = frames[0]
+    block_len, model_width = frame_rows.shape
+    head_size = bias_content.shape[1]
+    in_rows, inner_width = w_query.shape
+    out_rows = w_output.shape[0]
+    tm_count, dp_count = lax.axis_size("tm"), lax.axis_size("dp")
+    info = jnp.stack((lax.axis_index("tm"), lax.axis_index("dp"), lengths[0])).astype(jnp.int32)
+    scalar = (info, scalars)
+    width = inner_width // tm_count
+    heads = width // head_size
+    wide = heads * lanes
+    total_len = tm_count * block_len
+    row_count = 4 * block_len
+
+    cut_first = call(
+        functools.partial(cut_first_kernel, tm_count),
+        shaped(in_rows, 2 * width),
+        (scalar, (w_query, near), (w_key, near)),
+    )
+    normed_own = call(
+        norm_kernel,
+        shaped(block_len, model_width),
+        (scalar, (frame_rows, near), (ln_gain[None], near)),
+    )
+    first_far = send_far(cut_first, "dp")
+    normed_far = send_far(normed_own, "tm")
+    cut_second = call(
+        functools.partial(cut_second_kernel, tm_count),
+        shaped(in_rows // 2, 2 * width),
+        (scalar, (w_value, near)),
+    )
+    half_output = call(
+        cut_output_kernel, shaped(out_rows, model_width // 2), (scalar, (w_output, near))
+    )
+    arrived = [first_far[k] for k in range(2, dp_count, 2)]
+    second_far = send_far(later(cut_second, *arrived), "dp")
+    first_pieces = send_beside(first_far, "dp")
+    normed_pieces = send_beside({k: later(x, *arrived) for k, x in normed_far.items()}, "tm")
+    second_pieces = send_beside(second_far, "dp")
+    output_far = send_far(later(half_output, *first_pieces[1:]), "dp")
+    step = 32
+    sines, cosines = angle_tables(row_count, model_width, step)
+    relative = call(
+        functools.partial(relative_kernel, head_size, step),
+        shaped(row_count, wide),
+        (scalar, (sines, near), (cosines, near), (w_position.T, near)),
+        [pltpu.VMEM((row_count, model_width), half)],
+        micros=3.0,
+    )
+    query, key, normed = call(
+        functools.partial(query_key_kernel, tm_count, dp_count, head_size),
+        (shaped(total_len, wide), shaped(total_len, wide), shaped(total_len, model_width)),
+        (
+            scalar,
+            *((x, far) for x in normed_pieces),
+            *((x, far) for x in first_pieces),
+            (relative, far),
+        ),
+        [
+            pltpu.VMEM((dp_count, in_rows, 2 * width), half),
+            pltpu.VMEM((model_width, 2 * wide), half),
+            pltpu.SemaphoreType.DMA((dp_count,)),
+            pltpu.SemaphoreType.DMA((tm_count,)),
+        ],
+        micros=3.0,
+    )
+    weights = call(
+        functools.partial(softmax_kernel, tm_count),
+        shaped(tm_count, heads, block_len, 3 * block_len),
+        (
+            scalar,
+            (query, near),
+            (key, near),
+            (relative, near),
+            (bias_content, near),
+            (bias_position, near),
+        ),
+        [pltpu.VMEM((8, wide), jnp.float32)],
+        micros=6.0,
+    )
+    away = range(2, tm_count)
+    value, *contexts = call(
+        functools.partial(value_kernel, tm_count, dp_count, head_size, away),
+        [shaped(total_len + 2 * block_len, wide)]
+        + [shaped(block_len // 2, 2 * width)] * len(away),
+        (scalar, (normed, near), *((x, far) for x in second_pieces), (weights, near)),
+        [
+            pltpu.VMEM((dp_count, in_rows // 2, 2 * width), half),
+            pltpu.VMEM((model_width, wide), half),
+            pltpu.SemaphoreType.DMA((dp_count,)),
+        ],
+        micros=2.5,
+    )
+    mine = {k: swap(context, "tm", k) for k, context in zip(away, contexts)}
+    own, beside = call(
+        functools.partial(mix_kernel, head_size, range(2)),
+        [shaped(block_len // 2, 2 * width)] * 2,
+        (scalar, (weights, near), (value, near)),
+    )
+    output_pieces = send_beside({k: later(x, value) for k, x in output_far.items()}, "dp")
+    mine[0], mine[1] = own, swap(beside, "tm", 1)
+    own_output = call(
+        functools.partial(stack_kernel, dp_count),
+        shaped(inner_width, model_width // 2),
+        (scalar, *((x, far) for x in output_pieces)),
+        [pltpu.SemaphoreType.DMA((dp_count,))],
+    )
+    other_output = swap(own_output, "tm", 1)
+    attended = call(
+        functools.partial(out_kernel, tm_count),
+        shaped(block_len, model_width),
+        (
+            scalar,
+            *((mine[k], near) for k in range(tm_count)),
+            (own_output, near),
+            (other_output, near),
+            (frame_rows, near),
+        ),
+        micros=2.0,
+    )
+    return attended[None]
+
+
+def body(*args):
+    tm_count, dp_count = lax.axis_size("tm"), lax.axis_size("dp")
+    head_count, head_size = args[-1].shape
+    powers = all(n > 1 and n & (n - 1) == 0 for n in (tm_count, dp_count))
+    fits = head_size <= lanes and args[3].shape[0] % 32 == 0 and args[6].shape[0] % 16 == 0
+    if powers and fits and head_count % tm_count == 0:
+        return body_heads(*args)
+    return body_blocks(*args)
+
+
 def solution(mesh):
     placed = (
         P("dp", "tm", None),

time: 257 us -> 91.9 us (0.36)
  blocking collectives: 131 us -> 0 us
  matrix products: 50.9 us -> 0 us
  starting transfers between devices: 3.64 us -> 37.1 us
  local copies, waits for them, and re-layouts: 30.4 us -> 1.89 us
  Pallas kernels: 0 us -> 25.7 us
  waiting for transfers between devices: 0.17 us -> 25.2 us
  other arithmetic: 24.7 us -> 0.93 us
  between operations: 14 us -> 0.87 us
    all_gather x4 -> x0, blocking collectives: 131 us -> none  [the longest x1 33.8 us: body(): lax.all_gather(column_cut(w_key, tm_index, tm_count), 'dp', axis=0, tiled...]
    dot_general x29 -> x0, matrix products: 50.9 us -> none  [the longest x8 16.1 us: one_head(): return jnp.dot(weights, value_head, preferred_element_type=jnp.float32)]
    ppermute x2 -> x28, starting transfers between devices: 3.47 us -> 37.1 us  [swap(): return lax.ppermute(block, axis, [(i, i ^ distance) for i in range(count)])]
    pallas_call x0 -> x11, Pallas kernels: none -> 25.7 us  [call(): pl.pallas_call(kernel, out_shape=out_shape, in_specs=list(specs), out_spe...]
    ppermute x2 -> x28, waiting for transfers between devices: 0.01 us -> 25.2 us  [swap(): return lax.ppermute(block, axis, [(i, i ^ distance) for i in range(count)])]
    another operation x2 -> x1, other arithmetic: 12.8 us -> 0.08 us  [body_heads(): jnp.stack((lax.axis_index('tm'), lax.axis_index('dp'), lengths[0]))]
    reshape x9 -> x0, local copies, waits for them, and re-layouts: 8.74 us -> none  [the longest x8 5.02 us: rel_shift(): position_full.reshape(-1)[:block_len * (span_len - 1)]]
    while x40 -> x0, local copies, waits for them, and re-layouts: 7.93 us -> none
  transfers between devices with their start and end apart: 7 -> 28, of which waited for: 0 -> 11; matrix products, arithmetic and copies ran while one was open for 37% -> 1% of each run, Pallas kernels for 0% -> 22%
where the time goes in v2:
time: 91.9 us; the launch traced here: 91.7 us
  starting transfers between devices  37.1 us (40%)
  Pallas kernels  25.7 us (28%)
  waiting for transfers between devices  25.2 us (27%)
  local copies, waits for them, and re-layouts  1.89 us (2%)
  other arithmetic  0.93 us (1%)
    ppermute x28, starting transfers between devices, swap(): return lax.ppermute(block, axis, [(i, i ^ distance) for i in range(count)])  37.1 us
    pallas_call x11, Pallas kernels, call(): pl.pallas_call(kernel, out_shape=out_shape, in_specs=list(specs), out_spe...  25.7 us
    ppermute x28, waiting for transfers between devices, swap(): return lax.ppermute(block, axis, [(i, i ^ distance) for i in range(count)])  25.2 us
  transfers between devices with their start and end apart: 28, of which 11 were waited for; matrix products, arithmetic and copies ran while one was open for 1% of the time, Pallas kernels for 22%

profile of v2, /device:TPU:0, one launch (start us, length us, event | category | flops | bytes accessed | tf_op | source)
XLA Modules:
  0.0 91.7 jit_solution(11295719722538425030)
XLA Ops:
  3.6 3.0 %collective-permute-start.4 = (bf16[256,1536]{1,0:T(8,128)(2,1)S(1)}, bf16[256,1536]{1,0:T(8,128)(2,1)S(1)}, u32[]{:S(2)}, u32[]{:S(2)}) collective-permute-start(bf16[256,1536]{1,0:T(8,128)(2,1)S(1)} %shard_map.100.refs_0_), channel_id=1, source_target_pairs={{0,2},{1,3},{2,0},{3,1},{4,6},{5,7},{6,4},{7,5},{8,10},{9,11},{10,... | collective-permute-start | bytes 2359304 | tf_op jit(solution)/shard_map/ppermute | solution.py:184
  7.3 1.6 %collective-permute-start = (bf16[192,384]{1,0:T(8,128)(2,1)S(1)}, bf16[192,384]{1,0:T(8,128)(2,1)S(1)}, u32[]{:S(2)}, u32[]{:S(2)}) collective-permute-start(bf16[192,384]{1,0:T(8,128)(2,1)S(1)} %shard_map.101.refs_4_), channel_id=1, source_target_pairs={{0,8},{4,12},{8,0},{12,4},{16,24},{20,28},{24,16},{28,20},{1,9},{5... | collective-permute-start | bytes 442376 | tf_op jit(solution)/shard_map/ppermute | solution.py:184
  9.0 2.6 %collective-permute-start.1 = (bf16[192,384]{1,0:T(8,128)(2,1)S(1)}, bf16[192,384]{1,0:T(8,128)(2,1)S(1)}, u32[]{:S(2)}, u32[]{:S(2)}) collective-permute-start(bf16[192,384]{1,0:T(8,128)(2,1)S(1)} %shard_map.101.refs_4_), channel_id=1, source_target_pairs={{0,16},{4,20},{8,24},{12,28},{16,0},{20,4},{24,8},{28,12},{1,17},{... | collective-permute-start | bytes 442376 | tf_op jit(solution)/shard_map/ppermute | solution.py:184
  14.5 8.3 %collective-permute-done.1.refs_8_ = bf16[192,384]{1,0:T(8,128)(2,1)S(1)} collective-permute-done((bf16[192,384]{1,0:T(8,128)(2,1)S(1)}, bf16[192,384]{1,0:T(8,128)(2,1)S(1)}, u32[]{:S(2)}, u32[]{:S(2)}) %collective-permute-start.1) | collective-permute-done | bytes 147488 | tf_op jit(solution)/shard_map/ppermute | solution.py:184
  25.0 1.8 %collective-permute-start.7 = (bf16[192,384]{1,0:T(8,128)(2,1)S(1)}, bf16[192,384]{1,0:T(8,128)(2,1)S(1)}, u32[]{:S(2)}, u32[]{:S(2)}) collective-permute-start(bf16[192,384]{1,0:T(8,128)(2,1)S(1)} %collective-permute-done.refs_6_), channel_id=1, source_target_pairs={{0,4},{4,0},{8,12},{12,8},{16,20},{20,16},{24,28},{28,24},{1,5},{5... | collective-permute-start | bytes 442376 | tf_op jit(solution)/shard_map/ppermute | solution.py:184
  27.1 1.8 %collective-permute-start.9 = (bf16[192,384]{1,0:T(8,128)(2,1)S(1)}, bf16[192,384]{1,0:T(8,128)(2,1)S(1)}, u32[]{:S(2)}, u32[]{:S(2)}) collective-permute-start(bf16[192,384]{1,0:T(8,128)(2,1)S(1)} %collective-permute-done.2.refs_10_), channel_id=1, source_target_pairs={{0,4},{4,0},{8,12},{12,8},{16,20},{20,16},{24,28},{28,24},{1,5},{5... | collective-permute-start | bytes 442376 | tf_op jit(solution)/shard_map/ppermute | solution.py:184
  28.9 1.7 %shard_map.102.refs_12_.relative = bf16[1024,256]{1,0:T(8,128)(2,1)S(1)} custom-call(s32[3]{0:T(128)S(1)} %pad_add_fusion.info, f32[64,768]{1,0:T(8,128)S(1)} %get-tuple-element.38.sin_ref, f32[64,768]{1,0:T(8,128)S(1)} %get-tuple-element.37.cos_ref, bf16[192,1536]{1,0:T(8,128)(2,1)S(1)} %bitcast.7), custom_call_target="tpu_custom_call" | custom-call | flops 3300000000 | bytes 4096 | tf_op jit(solution)/shard_map/pallas_call | solution.py:165
  31.7 1.8 %collective-permute-start.11 = (bf16[96,384]{1,0:T(8,128)(2,1)S(1)}, bf16[96,384]{1,0:T(8,128)(2,1)S(1)}, u32[]{:S(2)}, u32[]{:S(2)}) collective-permute-start(bf16[96,384]{1,0:T(8,128)(2,1)S(1)} %shard_map.105.refs_1_), channel_id=1, source_target_pairs={{0,8},{4,12},{8,0},{12,4},{16,24},{20,28},{24,16},{28,20},{1,9},{5... | collective-permute-start | bytes 221192 | tf_op jit(solution)/shard_map/ppermute | solution.py:184
  34.9 2.8 %collective-permute-start.13 = (bf16[96,384]{1,0:T(8,128)(2,1)S(1)}, bf16[96,384]{1,0:T(8,128)(2,1)S(1)}, u32[]{:S(2)}, u32[]{:S(2)}) collective-permute-start(bf16[96,384]{1,0:T(8,128)(2,1)S(1)} %shard_map.105.refs_1_), channel_id=1, source_target_pairs={{0,16},{4,20},{8,24},{12,28},{16,0},{20,4},{24,8},{28,12},{1,17},{... | collective-permute-start | bytes 221192 | tf_op jit(solution)/shard_map/ppermute | solution.py:184
  37.7 3.8 %collective-permute-start.15 = (bf16[96,384]{1,0:T(8,128)(2,1)S(1)}, bf16[96,384]{1,0:T(8,128)(2,1)S(1)}, u32[]{:S(2)}, u32[]{:S(2)}) collective-permute-start(bf16[96,384]{1,0:T(8,128)(2,1)S(1)} %shard_map.105.refs_1_), channel_id=1, source_target_pairs={{0,24},{4,28},{8,16},{12,20},{16,8},{20,12},{24,0},{28,4},{1,25},{... | collective-permute-start | bytes 221192 | tf_op jit(solution)/shard_map/ppermute | solution.py:184
  42.1 1.6 %collective-permute-start.10 = (bf16[96,384]{1,0:T(8,128)(2,1)S(1)}, bf16[96,384]{1,0:T(8,128)(2,1)S(1)}, u32[]{:S(2)}, u32[]{:S(2)}) collective-permute-start(bf16[96,384]{1,0:T(8,128)(2,1)S(1)} %shard_map.105.refs_1_), channel_id=1, source_target_pairs={{0,4},{4,0},{8,12},{12,8},{16,20},{20,16},{24,28},{28,24},{1,5},{5... | collective-permute-start | bytes 221192 | tf_op jit(solution)/shard_map/ppermute | solution.py:184
  44.2 1.5 %collective-permute-start.14 = (bf16[96,384]{1,0:T(8,128)(2,1)S(1)}, bf16[96,384]{1,0:T(8,128)(2,1)S(1)}, u32[]{:S(2)}, u32[]{:S(2)}) collective-permute-start(bf16[96,384]{1,0:T(8,128)(2,1)S(1)} %collective-permute-done.13.refs_5_), channel_id=1, source_target_pairs={{0,4},{4,0},{8,12},{12,8},{16,20},{20,16},{24,28},{28,24},{1,5},{5... | collective-permute-start | bytes 221192 | tf_op jit(solution)/shard_map/ppermute | solution.py:184
  46.3 3.5 %collective-permute-start.25 = (bf16[96,768]{1,0:T(8,128)(2,1)S(1)}, bf16[96,768]{1,0:T(8,128)(2,1)S(1)}, u32[]{:S(2)}, u32[]{:S(2)}) collective-permute-start(bf16[96,768]{1,0:T(8,128)(2,1)S(1)} %shard_map.108.refs_0_), channel_id=1, source_target_pairs={{0,24},{4,28},{8,16},{12,20},{16,8},{20,12},{24,0},{28,4},{1,25},{... | collective-permute-start | bytes 442376 | tf_op jit(solution)/shard_map/ppermute | solution.py:184
  49.8 5.4 %shard_map.103 = (bf16[1024,256]{1,0:T(8,128)(2,1)S(1)}, bf16[1024,256]{1,0:T(8,128)(2,1)S(1)}, bf16[1024,1536]{1,0:T(8,128)(2,1)S(1)}) custom-call(s32[3]{0:T(128)S(1)} %pad_add_fusion.info, bf16[256,1536]{1,0:T(8,128)(2,1)S(1)} %shard_map.100.refs_0_, bf16[256,1536]{1,0:T(8,128)(2,1)S(1)} %collective-permute-done.3.refs_1_, ...), custom_call_target="tpu_custom_call" | custom-call | flops 3300000000 | bytes 4096 | tf_op jit(solution)/shard_map/pallas_call | solution.py:165
  55.2 5.0 %shard_map.104.refs_9_.weights_ref = bf16[4,2,256,768]{3,2,1,0:T(8,128)(2,1)S(1)} custom-call(s32[3]{0:T(128)S(1)} %pad_add_fusion.info, bf16[1024,256]{1,0:T(8,128)(2,1)S(1)} %get-tuple-element.23.query, bf16[1024,256]{1,0:T(8,128)(2,1)S(1)} %get-tuple-element.24.key, bf16[1024,256]{1,0:T(8,128)(2,1)S(1)} %shard_map.102.refs_12_.relative, ...), custom_call_target="tpu_custom_call" | custom-call | flops 6600000000 | bytes 4096 | tf_op jit(solution)/shard_map/pallas_call | solution.py:165
  61.2 4.7 %shard_map.106 = (bf16[1536,256]{1,0:T(8,128)(2,1)S(1)}, bf16[128,384]{1,0:T(8,128)(2,1)S(1)}, bf16[128,384]{1,0:T(8,128)(2,1)S(1)}) custom-call(s32[3]{0:T(128)S(1)} %pad_add_fusion.info, bf16[1024,1536]{1,0:T(8,128)(2,1)S(1)} %get-tuple-element.25.refs_0_, bf16[96,384]{1,0:T(8,128)(2,1)S(1)} %shard_map.105.refs_1_, ...), custom_call_target="tpu_custom_call" | custom-call | flops 2750000128 | bytes 4096 | tf_op jit(solution)/shard_map/pallas_call | solution.py:165
  65.9 1.6 %collective-permute-start.26 = (bf16[96,768]{1,0:T(8,128)(2,1)S(1)}, bf16[96,768]{1,0:T(8,128)(2,1)S(1)}, u32[]{:S(2)}, u32[]{:S(2)}) collective-permute-start(bf16[96,768]{1,0:T(8,128)(2,1)S(1)} %collective-permute-done.25.refs_6_), channel_id=1, source_target_pairs={{0,4},{4,0},{8,12},{12,8},{16,20},{20,16},{24,28},{28,24},{1,5},{5... | collective-permute-start | bytes 442376 | tf_op jit(solution)/shard_map/ppermute | solution.py:184
  71.1 1.7 %collective-permute-done.26.refs_7_ = bf16[96,768]{1,0:T(8,128)(2,1)S(1)} collective-permute-done((bf16[96,768]{1,0:T(8,128)(2,1)S(1)}, bf16[96,768]{1,0:T(8,128)(2,1)S(1)}, u32[]{:S(2)}, u32[]{:S(2)}) %collective-permute-start.26) | collective-permute-done | bytes 147488 | tf_op jit(solution)/shard_map/ppermute | solution.py:184
  72.8 2.8 %collective-permute-done.24.refs_5_ = bf16[96,768]{1,0:T(8,128)(2,1)S(1)} collective-permute-done((bf16[96,768]{1,0:T(8,128)(2,1)S(1)}, bf16[96,768]{1,0:T(8,128)(2,1)S(1)}, u32[]{:S(2)}, u32[]{:S(2)}) %collective-permute-start.24) | collective-permute-done | bytes 147488 | tf_op jit(solution)/shard_map/ppermute | solution.py:184
  75.5 1.6 %collective-permute-done.22.refs_3_ = bf16[96,768]{1,0:T(8,128)(2,1)S(1)} collective-permute-done((bf16[96,768]{1,0:T(8,128)(2,1)S(1)}, bf16[96,768]{1,0:T(8,128)(2,1)S(1)}, u32[]{:S(2)}, u32[]{:S(2)}) %collective-permute-start.22) | collective-permute-done | bytes 147488 | tf_op jit(solution)/shard_map/ppermute | solution.py:184
  77.1 1.6 %collective-permute-done.20.refs_1_ = bf16[96,768]{1,0:T(8,128)(2,1)S(1)} collective-permute-done((bf16[96,768]{1,0:T(8,128)(2,1)S(1)}, bf16[96,768]{1,0:T(8,128)(2,1)S(1)}, u32[]{:S(2)}, u32[]{:S(2)}) %collective-permute-start.20) | collective-permute-done | bytes 147488 | tf_op jit(solution)/shard_map/ppermute | solution.py:184
  78.7 2.2 %shard_map.109.refs_4_ = bf16[768,768]{1,0:T(8,128)(2,1)S(1)} custom-call(s32[3]{0:T(128)S(1)} %pad_add_fusion.info, bf16[96,768]{1,0:T(8,128)(2,1)S(1)} %shard_map.108.refs_0_, bf16[96,768]{1,0:T(8,128)(2,1)S(1)} %collective-permute-done.20.refs_1_, bf16[96,768]{1,0:T(8,128)(2,1)S(1)} %collective-permute-done.21.refs_2_, ...), custom_call_target="tpu_custom_call" | custom-call | flops 1100000000 | bytes 4096 | tf_op jit(solution)/shard_map/pallas_call | solution.py:165
  84.2 3.6 %collective-permute-done.18.refs_2_ = bf16[128,384]{1,0:T(8,128)(2,1)S(1)} collective-permute-done((bf16[128,384]{1,0:T(8,128)(2,1)S(1)}, bf16[128,384]{1,0:T(8,128)(2,1)S(1)}, u32[]{:S(2)}, u32[]{:S(2)}) %collective-permute-start.18) | collective-permute-done | bytes 98336 | tf_op jit(solution)/shard_map/ppermute | solution.py:184
  89.3 2.4 %shard_map.110 = bf16[256,1536]{1,0:T(8,128)(2,1)} custom-call(s32[3]{0:T(128)S(1)} %pad_add_fusion.info, bf16[128,384]{1,0:T(8,128)(2,1)S(1)} %get-tuple-element.28.refs_0_, bf16[128,384]{1,0:T(8,128)(2,1)S(1)} %collective-permute-done.17.refs_1_, bf16[128,384]{1,0:T(8,128)(2,1)S(1)} %collective-permute-done.18.refs_2_, ...), custom_call_target="tpu_custom_call" | custom-call | flops 2200000000 | bytes 4096 | tf_op jit(solution)/shard_map/pallas_call | solution.py:165
  (68 shorter events, 22.4 us)
Async XLA Ops:
  3.6 20.5 %collective-permute-start.4 = (bf16[256,1536]{1,0:T(8,128)(2,1)S(1)}, bf16[256,1536]{1,0:T(8,128)(2,1)S(1)}, u32[]{:S(2)}, u32[]{:S(2)}) collective-permute-start(bf16[256,1536]{1,0:T(8,128)(2,1)S(1)} %shard_map.100.refs_0_), channel_id=1, source_target_pairs={{0,2},{1,3},{2,0},{3,1},{4,6},{5,7},{6,4},{7,5},{8,10},{9,11},{10,... | collective-permute-start | bytes 2359304 | tf_op jit(solution)/shard_map/ppermute | solution.py:184
  7.3 7.2 %collective-permute-start = (bf16[192,384]{1,0:T(8,128)(2,1)S(1)}, bf16[192,384]{1,0:T(8,128)(2,1)S(1)}, u32[]{:S(2)}, u32[]{:S(2)}) collective-permute-start(bf16[192,384]{1,0:T(8,128)(2,1)S(1)} %shard_map.101.refs_4_), channel_id=1, source_target_pairs={{0,8},{4,12},{8,0},{12,4},{16,24},{20,28},{24,16},{28,20},{1,9},{5... | collective-permute-start | bytes 442376 | tf_op jit(solution)/shard_map/ppermute | solution.py:184
  9.0 13.9 %collective-permute-start.1 = (bf16[192,384]{1,0:T(8,128)(2,1)S(1)}, bf16[192,384]{1,0:T(8,128)(2,1)S(1)}, u32[]{:S(2)}, u32[]{:S(2)}) collective-permute-start(bf16[192,384]{1,0:T(8,128)(2,1)S(1)} %shard_map.101.refs_4_), channel_id=1, source_target_pairs={{0,16},{4,20},{8,24},{12,28},{16,0},{20,4},{24,8},{28,12},{1,17},{... | collective-permute-start | bytes 442376 | tf_op jit(solution)/shard_map/ppermute | solution.py:184
  11.5 11.3 %collective-permute-start.2 = (bf16[192,384]{1,0:T(8,128)(2,1)S(1)}, bf16[192,384]{1,0:T(8,128)(2,1)S(1)}, u32[]{:S(2)}, u32[]{:S(2)}) collective-permute-start(bf16[192,384]{1,0:T(8,128)(2,1)S(1)} %shard_map.101.refs_4_), channel_id=1, source_target_pairs={{0,24},{4,28},{8,16},{12,20},{16,8},{20,12},{24,0},{28,4},{1,25},{... | collective-permute-start | bytes 442376 | tf_op jit(solution)/shard_map/ppermute | solution.py:184
  11.8 15.4 %collective-permute-start.6 = (bf16[192,384]{1,0:T(8,128)(2,1)S(1)}, bf16[192,384]{1,0:T(8,128)(2,1)S(1)}, u32[]{:S(2)}, u32[]{:S(2)}) collective-permute-start(bf16[192,384]{1,0:T(8,128)(2,1)S(1)} %shard_map.101.refs_4_), channel_id=1, source_target_pairs={{0,4},{4,0},{8,12},{12,8},{16,20},{20,16},{24,28},{28,24},{1,5},{5... | collective-permute-start | bytes 442376 | tf_op jit(solution)/shard_map/ppermute | solution.py:184
  22.8 22.9 %collective-permute-start.3 = (bf16[256,1536]{1,0:T(8,128)(2,1)S(1)}, bf16[256,1536]{1,0:T(8,128)(2,1)S(1)}, u32[]{:S(2)}, u32[]{:S(2)}) collective-permute-start(bf16[256,1536]{1,0:T(8,128)(2,1)S(1)} %shard_map.100.refs_0_), channel_id=1, source_target_pairs={{0,1},{1,0},{2,3},{3,2},{4,5},{5,4},{6,7},{7,6},{8,9},{9,8},{10,11... | collective-permute-start | bytes 2359304 | tf_op jit(solution)/shard_map/ppermute | solution.py:184
  24.2 22.1 %collective-permute-start.5 = (bf16[256,1536]{1,0:T(8,128)(2,1)S(1)}, bf16[256,1536]{1,0:T(8,128)(2,1)S(1)}, u32[]{:S(2)}, u32[]{:S(2)}) collective-permute-start(bf16[256,1536]{1,0:T(8,128)(2,1)S(1)} %collective-permute-done.4.refs_2_), channel_id=1, source_target_pairs={{0,1},{1,0},{2,3},{3,2},{4,5},{5,4},{6,7},{7,6},{8,9},{9,8},{10,11... | collective-permute-start | bytes 2359304 | tf_op jit(solution)/shard_map/ppermute | solution.py:184
  25.0 6.7 %collective-permute-start.7 = (bf16[192,384]{1,0:T(8,128)(2,1)S(1)}, bf16[192,384]{1,0:T(8,128)(2,1)S(1)}, u32[]{:S(2)}, u32[]{:S(2)}) collective-permute-start(bf16[192,384]{1,0:T(8,128)(2,1)S(1)} %collective-permute-done.refs_6_), channel_id=1, source_target_pairs={{0,4},{4,0},{8,12},{12,8},{16,20},{20,16},{24,28},{28,24},{1,5},{5... | collective-permute-start | bytes 442376 | tf_op jit(solution)/shard_map/ppermute | solution.py:184
  26.9 8.0 %collective-permute-start.8 = (bf16[192,384]{1,0:T(8,128)(2,1)S(1)}, bf16[192,384]{1,0:T(8,128)(2,1)S(1)}, u32[]{:S(2)}, u32[]{:S(2)}) collective-permute-start(bf16[192,384]{1,0:T(8,128)(2,1)S(1)} %collective-permute-done.1.refs_8_), channel_id=1, source_target_pairs={{0,4},{4,0},{8,12},{12,8},{16,20},{20,16},{24,28},{28,24},{1,5},{5... | collective-permute-start | bytes 442376 | tf_op jit(solution)/shard_map/ppermute | solution.py:184
  27.1 10.6 %collective-permute-start.9 = (bf16[192,384]{1,0:T(8,128)(2,1)S(1)}, bf16[192,384]{1,0:T(8,128)(2,1)S(1)}, u32[]{:S(2)}, u32[]{:S(2)}) collective-permute-start(bf16[192,384]{1,0:T(8,128)(2,1)S(1)} %collective-permute-done.2.refs_10_), channel_id=1, source_target_pairs={{0,4},{4,0},{8,12},{12,8},{16,20},{20,16},{24,28},{28,24},{1,5},{5... | collective-permute-start | bytes 442376 | tf_op jit(solution)/shard_map/ppermute | solution.py:184
  31.7 10.4 %collective-permute-start.11 = (bf16[96,384]{1,0:T(8,128)(2,1)S(1)}, bf16[96,384]{1,0:T(8,128)(2,1)S(1)}, u32[]{:S(2)}, u32[]{:S(2)}) collective-permute-start(bf16[96,384]{1,0:T(8,128)(2,1)S(1)} %shard_map.105.refs_1_), channel_id=1, source_target_pairs={{0,8},{4,12},{8,0},{12,4},{16,24},{20,28},{24,16},{28,20},{1,9},{5... | collective-permute-start | bytes 221192 | tf_op jit(solution)/shard_map/ppermute | solution.py:184
  34.9 8.8 %collective-permute-start.13 = (bf16[96,384]{1,0:T(8,128)(2,1)S(1)}, bf16[96,384]{1,0:T(8,128)(2,1)S(1)}, u32[]{:S(2)}, u32[]{:S(2)}) collective-permute-start(bf16[96,384]{1,0:T(8,128)(2,1)S(1)} %shard_map.105.refs_1_), channel_id=1, source_target_pairs={{0,16},{4,20},{8,24},{12,28},{16,0},{20,4},{24,8},{28,12},{1,17},{... | collective-permute-start | bytes 221192 | tf_op jit(solution)/shard_map/ppermute | solution.py:184
  42.1 18.1 %collective-permute-start.10 = (bf16[96,384]{1,0:T(8,128)(2,1)S(1)}, bf16[96,384]{1,0:T(8,128)(2,1)S(1)}, u32[]{:S(2)}, u32[]{:S(2)}) collective-permute-start(bf16[96,384]{1,0:T(8,128)(2,1)S(1)} %shard_map.105.refs_1_), channel_id=1, source_target_pairs={{0,4},{4,0},{8,12},{12,8},{16,20},{20,16},{24,28},{28,24},{1,5},{5... | collective-permute-start | bytes 221192 | tf_op jit(solution)/shard_map/ppermute | solution.py:184
  43.7 16.6 %collective-permute-start.12 = (bf16[96,384]{1,0:T(8,128)(2,1)S(1)}, bf16[96,384]{1,0:T(8,128)(2,1)S(1)}, u32[]{:S(2)}, u32[]{:S(2)}) collective-permute-start(bf16[96,384]{1,0:T(8,128)(2,1)S(1)} %collective-permute-done.11.refs_3_), channel_id=1, source_target_pairs={{0,4},{4,0},{8,12},{12,8},{16,20},{20,16},{24,28},{28,24},{1,5},{5... | collective-permute-start | bytes 221192 | tf_op jit(solution)/shard_map/ppermute | solution.py:184
  44.2 17.0 %collective-permute-start.14 = (bf16[96,384]{1,0:T(8,128)(2,1)S(1)}, bf16[96,384]{1,0:T(8,128)(2,1)S(1)}, u32[]{:S(2)}, u32[]{:S(2)}) collective-permute-start(bf16[96,384]{1,0:T(8,128)(2,1)S(1)} %collective-permute-done.13.refs_5_), channel_id=1, source_target_pairs={{0,4},{4,0},{8,12},{12,8},{16,20},{20,16},{24,28},{28,24},{1,5},{5... | collective-permute-start | bytes 221192 | tf_op jit(solution)/shard_map/ppermute | solution.py:184
  45.8 15.5 %collective-permute-start.16 = (bf16[96,384]{1,0:T(8,128)(2,1)S(1)}, bf16[96,384]{1,0:T(8,128)(2,1)S(1)}, u32[]{:S(2)}, u32[]{:S(2)}) collective-permute-start(bf16[96,384]{1,0:T(8,128)(2,1)S(1)} %collective-permute-done.15.refs_7_), channel_id=1, source_target_pairs={{0,4},{4,0},{8,12},{12,8},{16,20},{20,16},{24,28},{28,24},{1,5},{5... | collective-permute-start | bytes 221192 | tf_op jit(solution)/shard_map/ppermute | solution.py:184
  46.3 19.6 %collective-permute-start.25 = (bf16[96,768]{1,0:T(8,128)(2,1)S(1)}, bf16[96,768]{1,0:T(8,128)(2,1)S(1)}, u32[]{:S(2)}, u32[]{:S(2)}) collective-permute-start(bf16[96,768]{1,0:T(8,128)(2,1)S(1)} %shard_map.108.refs_0_), channel_id=1, source_target_pairs={{0,24},{4,28},{8,16},{12,20},{16,8},{20,12},{24,0},{28,4},{1,25},{... | collective-permute-start | bytes 442376 | tf_op jit(solution)/shard_map/ppermute | solution.py:184
  60.3 7.3 %collective-permute-start.23 = (bf16[96,768]{1,0:T(8,128)(2,1)S(1)}, bf16[96,768]{1,0:T(8,128)(2,1)S(1)}, u32[]{:S(2)}, u32[]{:S(2)}) collective-permute-start(bf16[96,768]{1,0:T(8,128)(2,1)S(1)} %shard_map.108.refs_0_), channel_id=1, source_target_pairs={{0,16},{4,20},{8,24},{12,28},{16,0},{20,4},{24,8},{28,12},{1,17},{... | collective-permute-start | bytes 442376 | tf_op jit(solution)/shard_map/ppermute | solution.py:184
  60.3 8.7 %collective-permute-start.21 = (bf16[96,768]{1,0:T(8,128)(2,1)S(1)}, bf16[96,768]{1,0:T(8,128)(2,1)S(1)}, u32[]{:S(2)}, u32[]{:S(2)}) collective-permute-start(bf16[96,768]{1,0:T(8,128)(2,1)S(1)} %shard_map.108.refs_0_), channel_id=1, source_target_pairs={{0,8},{4,12},{8,0},{12,4},{16,24},{20,28},{24,16},{28,20},{1,9},{5... | collective-permute-start | bytes 442376 | tf_op jit(solution)/shard_map/ppermute | solution.py:184
  65.9 6.8 %collective-permute-start.26 = (bf16[96,768]{1,0:T(8,128)(2,1)S(1)}, bf16[96,768]{1,0:T(8,128)(2,1)S(1)}, u32[]{:S(2)}, u32[]{:S(2)}) collective-permute-start(bf16[96,768]{1,0:T(8,128)(2,1)S(1)} %collective-permute-done.25.refs_6_), channel_id=1, source_target_pairs={{0,4},{4,0},{8,12},{12,8},{16,20},{20,16},{24,28},{28,24},{1,5},{5... | collective-permute-start | bytes 442376 | tf_op jit(solution)/shard_map/ppermute | solution.py:184
  67.5 8.0 %collective-permute-start.24 = (bf16[96,768]{1,0:T(8,128)(2,1)S(1)}, bf16[96,768]{1,0:T(8,128)(2,1)S(1)}, u32[]{:S(2)}, u32[]{:S(2)}) collective-permute-start(bf16[96,768]{1,0:T(8,128)(2,1)S(1)} %collective-permute-done.23.refs_4_), channel_id=1, source_target_pairs={{0,4},{4,0},{8,12},{12,8},{16,20},{20,16},{24,28},{28,24},{1,5},{5... | collective-permute-start | bytes 442376 | tf_op jit(solution)/shard_map/ppermute | solution.py:184
  69.0 8.1 %collective-permute-start.22 = (bf16[96,768]{1,0:T(8,128)(2,1)S(1)}, bf16[96,768]{1,0:T(8,128)(2,1)S(1)}, u32[]{:S(2)}, u32[]{:S(2)}) collective-permute-start(bf16[96,768]{1,0:T(8,128)(2,1)S(1)} %collective-permute-done.21.refs_2_), channel_id=1, source_target_pairs={{0,4},{4,0},{8,12},{12,8},{16,20},{20,16},{24,28},{28,24},{1,5},{5... | collective-permute-start | bytes 442376 | tf_op jit(solution)/shard_map/ppermute | solution.py:184
  69.6 9.1 %collective-permute-start.20 = (bf16[96,768]{1,0:T(8,128)(2,1)S(1)}, bf16[96,768]{1,0:T(8,128)(2,1)S(1)}, u32[]{:S(2)}, u32[]{:S(2)}) collective-permute-start(bf16[96,768]{1,0:T(8,128)(2,1)S(1)} %shard_map.108.refs_0_), channel_id=1, source_target_pairs={{0,4},{4,0},{8,12},{12,8},{16,20},{20,16},{24,28},{28,24},{1,5},{5... | collective-permute-start | bytes 442376 | tf_op jit(solution)/shard_map/ppermute | solution.py:184
  80.9 8.4 %collective-permute-start.27 = (bf16[768,768]{1,0:T(8,128)(2,1)S(1)}, bf16[768,768]{1,0:T(8,128)(2,1)S(1)}, u32[]{:S(2)}, u32[]{:S(2)}) collective-permute-start(bf16[768,768]{1,0:T(8,128)(2,1)S(1)} %shard_map.109.refs_4_), channel_id=1, source_target_pairs={{0,1},{1,0},{2,3},{3,2},{4,5},{5,4},{6,7},{7,6},{8,9},{9,8},{10,11... | collective-permute-start | bytes 3538952 | tf_op jit(solution)/shard_map/ppermute | solution.py:184
  (13 other events, 115.5 us)

commit v3 on v2

--- a/solution.py
+++ b/solution.py
@@ -156,7 +156,7 @@
 half = jnp.bfloat16
 across = (((1,), (1,)), ((), ()))
 near = pl.BlockSpec(memory_space=pltpu.VMEM)
-far = pl.BlockSpec(memory_space=pl.ANY)
+far = pl.BlockSpec(memory_space=pltpu.HBM)
 scalars = pl.BlockSpec(memory_space=pltpu.SMEM)
 
 
@@ -189,7 +189,9 @@
 
 
 def send_beside(pieces, axis):
-    everything = pieces | {k ^ 1: swap(pieces[k], axis, 1) for k in pieces}
+    everything = dict(pieces)
+    for k, piece in pieces.items():
+        everything[k ^ 1] = swap(piece, axis, 1)
     return [everything[k] for k in sorted(everything)]
 
 
@@ -197,39 +199,27 @@
     return lax.optimization_barrier((value, *others))[0]
 
 
-def cut_first_kernel(tm_count, info, query_ref, key_ref, cut_ref):
-    width = query_ref.shape[1] // tm_count
+def prepare_kernel(tm_count, info, *refs):
+    gain_ref, cut_ref, half_ref, normed_ref, stage, frame, sems = refs[5:]
+    rows, width = stage.shape[1], stage.shape[2] // tm_count
+    query_ref, key_ref, value_ref = (stage.at[i] for i in range(3))
+    half_width = half_ref.shape[1]
+    side = pl.ds(pl.multiple_of(lax.rem(info[0], 2) * half_width, lanes), half_width)
+    sources = (refs[4], *refs[:3], refs[3].at[:, side])
+    copies = load(sources, (frame, query_ref, key_ref, value_ref, half_ref), sems)
+    copies[0].wait()
+    normed_ref[...] = layer_norm(frame[...], gain_ref[...])
+    for copy in copies[1:]:
+        copy.wait()
     for index in range(tm_count):
 
         @pl.when(info[0] == index)
         def _():
             columns = slice(index * width, (index + 1) * width)
-            cut_ref[:, :width] = query_ref[:, columns]
-            cut_ref[:, width:] = key_ref[:, columns]
-
-
-def cut_second_kernel(tm_count, info, *refs):
-    value_ref, cut_ref = refs[0], refs[-1]
-    rows = value_ref.shape[0]
-    width = value_ref.shape[1] // tm_count
-    for index in range(tm_count):
-
-        @pl.when(info[0] == index)
-        def _():
-            columns = slice(index * width, (index + 1) * width)
-            cut_ref[:, :width] = value_ref[: rows // 2, columns]
-            cut_ref[:, width:] = value_ref[rows // 2 :, columns]
-
-
-def cut_output_kernel(info, *refs):
-    output_ref, half_ref = refs[0], refs[-1]
-    width = half_ref.shape[1]
-    start = pl.multiple_of(lax.rem(info[0], 2) * width, lanes)
-    half_ref[...] = output_ref[:, pl.ds(start, width)]
-
-
-def norm_kernel(info, frame_ref, gain_ref, normed_ref):
-    normed_ref[...] = layer_norm(frame_ref[...], gain_ref[...])
+            cut_ref[:rows, :width] = query_ref[:, columns]
+            cut_ref[:rows, width:] = key_ref[:, columns]
+            cut_ref[rows:, :width] = value_ref[: rows // 2, columns]
+            cut_ref[rows:, width:] = value_ref[rows // 2 :, columns]
 
 
 def angle_tables(row_count, model_width, step):
@@ -273,33 +263,39 @@
     return copies
 
 
-def query_key_kernel(tm_count, dp_count, head_size, info, *refs):
+def project_kernel(tm_count, dp_count, head_size, info, *refs):
     normed_refs, refs = refs[:tm_count], refs[tm_count:]
     cut_refs, refs = refs[:dp_count], refs[dp_count:]
-    query_ref, key_ref, normed, cuts, weight, cut_sems, normed_sems = refs[1:]
+    query_ref, key_ref, value_ref, normed, cuts, weight, cut_sems, normed_sems = refs
     block_len = normed.shape[0] // tm_count
-    rows, cut_width = cuts.shape[1:]
+    rows, width = cuts.shape[1] * 2 // 3, cuts.shape[2] // 2
     wide = query_ref.shape[1]
-    width = cut_width // 2
     spots = [pl.multiple_of((info[0] ^ k) * block_len, block_len) for k in range(tm_count)]
     cut_copies = load(cut_refs, [cuts.at[k] for k in range(dp_count)], cut_sems)
     normed_copies = load(
         normed_refs, [normed.at[pl.ds(spot, block_len), :] for spot in spots], normed_sems
     )
     weight[...] = jnp.zeros_like(weight)
+    value_ref[:block_len, :] = jnp.zeros_like(value_ref[:block_len, :])
+    value_ref[(tm_count + 1) * block_len :, :] = jnp.zeros_like(value_ref[:block_len, :])
     for k in range(dp_count):
         cut_copies[k].wait()
         start = pl.multiple_of((info[1] ^ k) * rows, 16)
-        for part in range(2):
-            for h in range(width // head_size):
+        for h in range(width // head_size):
+            for part in range(2):
                 source = part * width + h * head_size
                 target = part * wide + h * lanes
                 weight[pl.ds(start, rows), target : target + head_size] = cuts[
-                    k, :, source : source + head_size
+                    k, :rows, source : source + head_size
                 ]
+                target = 2 * wide + h * lanes
+                weight[
+                    pl.ds(start + part * (rows // 2), rows // 2), target : target + head_size
+                ] = cuts[k, rows:, source : source + head_size]
     for copy in normed_copies:
         copy.wait()
-    for part, ref in enumerate((query_ref, key_ref)):
+    shift = slice(block_len, (tm_count + 1) * block_len)
+    for part, ref in enumerate((query_ref, key_ref, value_ref.at[shift, :])):
         ref[...] = jnp.dot(
             normed[...],
             weight[:, part * wide : (part + 1) * wide],
@@ -373,60 +369,53 @@
                 ]
 
 
-def value_kernel(tm_count, dp_count, head_size, distances, info, *refs):
-    normed, cut_refs, refs = refs[0], refs[1 : 1 + dp_count], refs[1 + dp_count :]
-    weights_ref, value, refs = refs[0], refs[1], refs[2:]
-    context_refs, (cuts, weight, cut_sems) = refs[: len(distances)], refs[len(distances) :]
-    block_len = normed.shape[0] // tm_count
-    rows = cuts.shape[1]
-    width = cuts.shape[2] // 2
-    cut_copies = load(cut_refs, [cuts.at[k] for k in range(dp_count)], cut_sems)
-    weight[...] = jnp.zeros_like(weight)
-    value[:block_len, :] = jnp.zeros_like(value[:block_len, :])
-    value[(tm_count + 1) * block_len :, :] = jnp.zeros_like(value[:block_len, :])
-    for k in range(dp_count):
-        cut_copies[k].wait()
-        start = pl.multiple_of((info[1] ^ k) * rows * 2, 16)
+def mix_kernel(head_size, distances, info, weights_ref, value, *context_refs):
+    rows = weights_ref.shape[2] // 2
+    if len(context_refs) == len(distances):
+        places = context_refs
+    else:
+        places = [
+            context_refs[i // 2].at[i % 2 * rows : (i % 2 + 1) * rows, :]
+            for i in range(len(distances))
+        ]
+    mix_values(info, distances, weights_ref, value, places, head_size)
+
+
+def pair_kernel(info, own_ref, beside_ref, pair_ref):
+    rows = own_ref.shape[0]
+    own = lax.rem(info[1], 2)
+    pair_ref[pl.ds(pl.multiple_of(own * rows, 16), rows), :] = own_ref[...]
+    pair_ref[pl.ds(pl.multiple_of((1 - own) * rows, 16), rows), :] = beside_ref[...]
+
+
+def out_kernel(tm_count, pair_count, info, *refs):
+    context_refs, refs = refs[:tm_count], refs[tm_count:]
+    pair_refs, refs = refs[: 2 * pair_count], refs[2 * pair_count :]
+    frame_ref, out_ref, weight, context, sems = refs
+    width = context_refs[0].shape[1] // 2
+    rows = pair_refs[0].shape[0]
+    half_width = weight.shape[2]
+    spots = []
+    for k in range(pair_count):
+        first = ((info[1] // 2) ^ k) * rows
+        source = first // width
+        spots.append(pl.multiple_of((source ^ info[0]) * width + first - source * width, 16))
+    copies = load(
+        pair_refs,
+        [weight.at[i // pair_count, pl.ds(spot, rows), :] for i, spot in enumerate(spots * 2)],
+        sems,
+    )
+    for k, ref in enumerate(context_refs):
         for part in range(2):
-            for h in range(width // head_size):
-                source = part * width + h * head_size
-                weight[
-                    pl.ds(start + part * rows, rows), h * lanes : h * lanes + head_size
-                ] = cuts[k, :, source : source + head_size]
-    value[block_len : (tm_count + 1) * block_len, :] = jnp.dot(
-        normed[...], weight[...], preferred_element_type=jnp.float32
-    ).astype(half)
-    mix_values(info, distances, weights_ref, value, context_refs, head_size)
-
-
-def mix_kernel(head_size, distances, info, weights_ref, value, *context_refs):
-    mix_values(info, distances, weights_ref, value, context_refs, head_size)
-
-
-def stack_kernel(count, info, *refs):
-    stacked = refs[count]
-    sems = refs[count + 1]
-    rows = refs[0].shape[0]
-    spots = [pl.multiple_of((info[1] ^ k) * rows, 16) for k in range(count)]
-    for copy in load(refs[:count], [stacked.at[pl.ds(spot, rows), :] for spot in spots], sems):
-        copy.wait()
-
-
-def out_kernel(tm_count, info, *refs):
-    context_refs, (own_ref, other_ref, frame_ref, out_ref) = refs[:tm_count], refs[tm_count:]
-    width = context_refs[0].shape[1] // 2
-    half_width = own_ref.shape[1]
-    contexts = [
-        jnp.concatenate([ref[:, :width], ref[:, width:]], axis=0) for ref in context_refs
-    ]
-    for side, ref in enumerate((own_ref, other_ref)):
+            context[
+                part * (context.shape[0] // 2) : (part + 1) * (context.shape[0] // 2),
+                k * width : (k + 1) * width,
+            ] = ref[:, part * width : (part + 1) * width]
+    for side in range(2):
+        for copy in copies[side * pair_count : (side + 1) * pair_count]:
+            copy.wait()
         lane = pl.ds(pl.multiple_of((lax.rem(info[0], 2) ^ side) * half_width, lanes), half_width)
-        mixed = jnp.zeros((contexts[0].shape[0], half_width), jnp.float32)
-        for k in range(tm_count):
-            start = pl.multiple_of((info[0] ^ k) * width, 16)
-            mixed += jnp.dot(
-                contexts[k], ref[pl.ds(start, width), :], preferred_element_type=jnp.float32
-            )
+        mixed = jnp.dot(context[...], weight[side], preferred_element_type=jnp.float32)
         out_ref[:, lane] = (frame_ref[:, lane].astype(jnp.float32) + mixed).astype(half)
 
 
@@ -456,32 +445,33 @@
     total_len = tm_count * block_len
     row_count = 4 * block_len
 
-    cut_first = call(
-        functools.partial(cut_first_kernel, tm_count),
-        shaped(in_rows, 2 * width),
-        (scalar, (w_query, near), (w_key, near)),
-    )
-    normed_own = call(
-        norm_kernel,
-        shaped(block_len, model_width),
-        (scalar, (frame_rows, near), (ln_gain[None], near)),
-    )
-    first_far = send_far(cut_first, "dp")
-    normed_far = send_far(normed_own, "tm")
-    cut_second = call(
-        functools.partial(cut_second_kernel, tm_count),
-        shaped(in_rows // 2, 2 * width),
-        (scalar, (w_value, near)),
-    )
-    half_output = call(
-        cut_output_kernel, shaped(out_rows, model_width // 2), (scalar, (w_output, near))
-    )
-    arrived = [first_far[k] for k in range(2, dp_count, 2)]
-    second_far = send_far(later(cut_second, *arrived), "dp")
-    first_pieces = send_beside(first_far, "dp")
-    normed_pieces = send_beside({k: later(x, *arrived) for k, x in normed_far.items()}, "tm")
-    second_pieces = send_beside(second_far, "dp")
-    output_far = send_far(later(half_output, *first_pieces[1:]), "dp")
+    cut, half_output, normed_own = call(
+        functools.partial(prepare_kernel, tm_count),
+        (
+            shaped(in_rows // 2 * 3, 2 * width),
+            shaped(out_rows, model_width // 2),
+            shaped(block_len, model_width),
+        ),
+        (
+            scalar,
+            *((x, far) for x in (w_query, w_key, w_value, w_output, frame_rows)),
+            (ln_gain, near),
+        ),
+        [
+            pltpu.VMEM((3, in_rows, inner_width), half),
+            pltpu.VMEM((block_len, model_width), half),
+            pltpu.SemaphoreType.DMA((5,)),
+        ],
+        room=56,
+    )
+    cut_far = send_far(cut, "dp")
+    pair = call(
+        pair_kernel,
+        shaped(2 * out_rows, model_width // 2),
+        (scalar, (half_output, near), (swap(half_output, "dp", 1), near)),
+        micros=0.5,
+    )
+    cut_pieces = send_beside(cut_far, "dp")
     step = 32
     sines, cosines = angle_tables(row_count, model_width, step)
     relative = call(
@@ -489,24 +479,26 @@
         shaped(row_count, wide),
         (scalar, (sines, near), (cosines, near), (w_position.T, near)),
         [pltpu.VMEM((row_count, model_width), half)],
-        micros=3.0,
-    )
-    query, key, normed = call(
-        functools.partial(query_key_kernel, tm_count, dp_count, head_size),
-        (shaped(total_len, wide), shaped(total_len, wide), shaped(total_len, model_width)),
+        micros=2.0,
+    )
+    normed_pieces = send_beside(send_far(normed_own, "tm"), "tm")
+    pairs = send_far(later(pair, *[cut_far[k] for k in range(2, dp_count, 2)]), "dp")
+    query, key, value = call(
+        functools.partial(project_kernel, tm_count, dp_count, head_size),
         (
-            scalar,
-            *((x, far) for x in normed_pieces),
-            *((x, far) for x in first_pieces),
-            (relative, far),
+            shaped(total_len, wide),
+            shaped(total_len, wide),
+            shaped(total_len + 2 * block_len, wide),
         ),
+        (scalar, *((x, far) for x in normed_pieces), *((x, far) for x in cut_pieces)),
         [
-            pltpu.VMEM((dp_count, in_rows, 2 * width), half),
-            pltpu.VMEM((model_width, 2 * wide), half),
+            pltpu.VMEM((total_len, model_width), half),
+            pltpu.VMEM((dp_count, in_rows // 2 * 3, 2 * width), half),
+            pltpu.VMEM((model_width, 3 * wide), half),
             pltpu.SemaphoreType.DMA((dp_count,)),
             pltpu.SemaphoreType.DMA((tm_count,)),
         ],
-        micros=3.0,
+        micros=6.0,
     )
     weights = call(
         functools.partial(softmax_kernel, tm_count),
@@ -520,47 +512,41 @@
             (bias_position, near),
         ),
         [pltpu.VMEM((8, wide), jnp.float32)],
-        micros=6.0,
+        micros=5.0,
     )
     away = range(2, tm_count)
-    value, *contexts = call(
-        functools.partial(value_kernel, tm_count, dp_count, head_size, away),
-        [shaped(total_len + 2 * block_len, wide)]
-        + [shaped(block_len // 2, 2 * width)] * len(away),
-        (scalar, (normed, near), *((x, far) for x in second_pieces), (weights, near)),
-        [
-            pltpu.VMEM((dp_count, in_rows // 2, 2 * width), half),
-            pltpu.VMEM((model_width, wide), half),
-            pltpu.SemaphoreType.DMA((dp_count,)),
-        ],
-        micros=2.5,
-    )
-    mine = {k: swap(context, "tm", k) for k, context in zip(away, contexts)}
+    doubles = call(
+        functools.partial(mix_kernel, head_size, away),
+        [shaped(block_len, 2 * width)] * (len(away) // 2),
+        (scalar, (weights, near), (value, near)),
+    )
+    received = {k: swap(double, "tm", k) for k, double in zip(away[::2], doubles)}
     own, beside = call(
         functools.partial(mix_kernel, head_size, range(2)),
         [shaped(block_len // 2, 2 * width)] * 2,
         (scalar, (weights, near), (value, near)),
     )
-    output_pieces = send_beside({k: later(x, value) for k, x in output_far.items()}, "dp")
-    mine[0], mine[1] = own, swap(beside, "tm", 1)
-    own_output = call(
-        functools.partial(stack_kernel, dp_count),
-        shaped(inner_width, model_width // 2),
-        (scalar, *((x, far) for x in output_pieces)),
-        [pltpu.SemaphoreType.DMA((dp_count,))],
-    )
-    other_output = swap(own_output, "tm", 1)
+    mine = {0: own, 1: swap(beside, "tm", 1)}
+    for k, double in received.items():
+        mine[k] = double[: block_len // 2]
+        mine[k + 1] = swap(double[block_len // 2 :], "tm", 1)
+    own_pairs = [pairs[k] for k in sorted(pairs)]
+    other_pairs = [swap(later(x, beside), "tm", 1) for x in own_pairs]
     attended = call(
-        functools.partial(out_kernel, tm_count),
+        functools.partial(out_kernel, tm_count, len(own_pairs)),
         shaped(block_len, model_width),
         (
             scalar,
             *((mine[k], near) for k in range(tm_count)),
-            (own_output, near),
-            (other_output, near),
+            *((x, far) for x in own_pairs + other_pairs),
             (frame_rows, near),
         ),
-        micros=2.0,
+        [
+            pltpu.VMEM((2, inner_width, model_width // 2), half),
+            pltpu.VMEM((block_len, inner_width), half),
+            pltpu.SemaphoreType.DMA((2 * len(own_pairs),)),
+        ],
+        micros=2.5,
     )
     return attended[None]
 
@@ -570,7 +556,8 @@
     head_count, head_size = args[-1].shape
     powers = all(n > 1 and n & (n - 1) == 0 for n in (tm_count, dp_count))
     fits = head_size <= lanes and args[3].shape[0] % 32 == 0 and args[6].shape[0] % 16 == 0
-    if powers and fits and head_count % tm_count == 0:
+    aligned = args[3].shape[1] // tm_count % (2 * args[6].shape[0]) == 0
+    if powers and fits and aligned and head_count % tm_count == 0:
         return body_heads(*args)
     return body_blocks(*args)
 

time: 91.9 us -> 77.5 us (0.84)
  starting transfers between devices: 37.1 us -> 24.9 us
  local copies, waits for them, and re-layouts: 1.89 us -> 0.06 us
  Pallas kernels: 25.7 us -> 24 us
    ppermute x28 -> x21, starting transfers between devices: 37.1 us -> 24.9 us  [swap(): return lax.ppermute(block, axis, [(i, i ^ distance) for i in range(count)])]
    pallas_call x11 -> x8, Pallas kernels: 25.7 us -> 24 us  [call(): pl.pallas_call(kernel, out_shape=out_shape, in_specs=list(specs), out_spe...]
    unnamed x18 -> x16, local copies, waits for them, and re-layouts: 1.18 us -> 0.04 us
    ppermute x28 -> x21, waiting for transfers between devices: 25.2 us -> 25.8 us  [swap(): return lax.ppermute(block, axis, [(i, i ^ distance) for i in range(count)])]
  transfers between devices with their start and end apart: 28 -> 21, of which waited for: 11 -> 11; matrix products, arithmetic and copies ran while one was open for 1% -> 1% of each run, Pallas kernels for 22% -> 22%
where the time goes in v3:
time: 77.5 us; the launch traced here: 77.3 us
  waiting for transfers between devices  25.8 us (33%)
  starting transfers between devices  24.9 us (32%)
  Pallas kernels  24 us (31%)
  other arithmetic  1.5 us (2%)
  between operations  1.06 us (1%)
    ppermute x21, waiting for transfers between devices, swap(): return lax.ppermute(block, axis, [(i, i ^ distance) for i in range(count)])  25.8 us
    ppermute x21, starting transfers between devices, swap(): return lax.ppermute(block, axis, [(i, i ^ distance) for i in range(count)])  24.9 us
    pallas_call x8, Pallas kernels, call(): pl.pallas_call(kernel, out_shape=out_shape, in_specs=list(specs), out_spe...  24 us
  transfers between devices with their start and end apart: 21, of which 11 were waited for; matrix products, arithmetic and copies ran while one was open for 1% of the time, Pallas kernels for 22%

profile of v3, /device:TPU:0, one launch (start us, length us, event | category | flops | bytes accessed | tf_op | source)
XLA Modules:
  0.0 77.3 jit_solution(4714807960023695735)
XLA Ops:
  1.4 3.5 %shard_map.100 = (bf16[288,384]{1,0:T(8,128)(2,1)}, bf16[96,768]{1,0:T(8,128)(2,1)}, bf16[256,1536]{1,0:T(8,128)(2,1)}) custom-call(s32[3]{0:T(128)} %pad_add_fusion.info, bf16[192,768]{1,0:T(8,128)(2,1)} %refs_0_.1, bf16[192,768]{1,0:T(8,128)(2,1)} %refs_1_.1, bf16[192,768]{1,0:T(8,128)(2,1)} %refs_2_.1, bf16[96,1536]{1,0:T(8,128)(2,1)} %refs_3_.1, ...), custom_call_target="tpu_custom_call" | custom-call | flops 1100000000 | bytes 4096 | tf_op jit(solution)/shard_map/pallas_call | solution.py:165
  4.9 3.0 %collective-permute-start.1 = (bf16[256,1536]{1,0:T(8,128)(2,1)}, bf16[256,1536]{1,0:T(8,128)(2,1)S(1)}, u32[]{:S(2)}, u32[]{:S(2)}) collective-permute-start(bf16[256,1536]{1,0:T(8,128)(2,1)} %get-tuple-element.18.refs_0_), channel_id=1, source_target_pairs={{0,2},{1,3},{2,0},{3,1},{4,6},{5,7},{6,4},{7,5},{8,10},{9,11},{10,... | collective-permute-start | bytes 2359304 | tf_op jit(solution)/shard_map/ppermute | solution.py:184
  7.9 1.6 %collective-permute-start.4 = (bf16[288,384]{1,0:T(8,128)(2,1)}, bf16[288,384]{1,0:T(8,128)(2,1)S(1)}, u32[]{:S(2)}, u32[]{:S(2)}) collective-permute-start(bf16[288,384]{1,0:T(8,128)(2,1)} %get-tuple-element.19.refs_4_), channel_id=1, source_target_pairs={{0,8},{4,12},{8,0},{12,4},{16,24},{20,28},{24,16},{28,20},{1,9},{5... | collective-permute-start | bytes 663560 | tf_op jit(solution)/shard_map/ppermute | solution.py:184
  9.5 2.6 %collective-permute-start.6 = (bf16[288,384]{1,0:T(8,128)(2,1)}, bf16[288,384]{1,0:T(8,128)(2,1)S(1)}, u32[]{:S(2)}, u32[]{:S(2)}) collective-permute-start(bf16[288,384]{1,0:T(8,128)(2,1)} %get-tuple-element.19.refs_4_), channel_id=1, source_target_pairs={{0,16},{4,20},{8,24},{12,28},{16,0},{20,4},{24,8},{28,12},{1,17},{... | collective-permute-start | bytes 663560 | tf_op jit(solution)/shard_map/ppermute | solution.py:184
  12.0 1.5 %collective-permute-start.13 = (bf16[96,768]{1,0:T(8,128)(2,1)}, bf16[96,768]{1,0:T(8,128)(2,1)S(1)}, u32[]{:S(2)}, u32[]{:S(2)}) collective-permute-start(bf16[96,768]{1,0:T(8,128)(2,1)} %get-tuple-element.25.own_ref), channel_id=1, source_target_pairs={{0,4},{4,0},{8,12},{12,8},{16,20},{20,16},{24,28},{28,24},{1,5},{5... | collective-permute-start | bytes 442376 | tf_op jit(solution)/shard_map/ppermute | solution.py:184
  13.6 12.1 %collective-permute-done.1.refs_2_ = bf16[256,1536]{1,0:T(8,128)(2,1)S(1)} collective-permute-done((bf16[256,1536]{1,0:T(8,128)(2,1)}, bf16[256,1536]{1,0:T(8,128)(2,1)S(1)}, u32[]{:S(2)}, u32[]{:S(2)}) %collective-permute-start.1) | collective-permute-done | bytes 786464 | tf_op jit(solution)/shard_map/ppermute | solution.py:184
  25.7 3.9 %collective-permute-start.8 = (bf16[288,384]{1,0:T(8,128)(2,1)}, bf16[288,384]{1,0:T(8,128)(2,1)S(1)}, u32[]{:S(2)}, u32[]{:S(2)}) collective-permute-start(bf16[288,384]{1,0:T(8,128)(2,1)} %get-tuple-element.19.refs_4_), channel_id=1, source_target_pairs={{0,24},{4,28},{8,16},{12,20},{16,8},{20,12},{24,0},{28,4},{1,25},{... | collective-permute-start | bytes 663560 | tf_op jit(solution)/shard_map/ppermute | solution.py:184
  29.7 1.5 %collective-permute-start.3 = (bf16[288,384]{1,0:T(8,128)(2,1)}, bf16[288,384]{1,0:T(8,128)(2,1)S(1)}, u32[]{:S(2)}, u32[]{:S(2)}) collective-permute-start(bf16[288,384]{1,0:T(8,128)(2,1)} %get-tuple-element.19.refs_4_), channel_id=1, source_target_pairs={{0,4},{4,0},{8,12},{12,8},{16,20},{20,16},{24,28},{28,24},{1,5},{5... | collective-permute-start | bytes 663560 | tf_op jit(solution)/shard_map/ppermute | solution.py:184
  32.5 3.5 %collective-permute-done.8.refs_10_ = bf16[288,384]{1,0:T(8,128)(2,1)S(1)} collective-permute-done((bf16[288,384]{1,0:T(8,128)(2,1)}, bf16[288,384]{1,0:T(8,128)(2,1)S(1)}, u32[]{:S(2)}, u32[]{:S(2)}) %collective-permute-start.8) | collective-permute-done | bytes 221216 | tf_op jit(solution)/shard_map/ppermute | solution.py:184
  36.1 1.5 %collective-permute-start.7 = (bf16[288,384]{1,0:T(8,128)(2,1)S(1)}, bf16[288,384]{1,0:T(8,128)(2,1)S(1)}, u32[]{:S(2)}, u32[]{:S(2)}) collective-permute-start(bf16[288,384]{1,0:T(8,128)(2,1)S(1)} %collective-permute-done.6.refs_8_), channel_id=1, source_target_pairs={{0,4},{4,0},{8,12},{12,8},{16,20},{20,16},{24,28},{28,24},{1,5},{5... | collective-permute-start | bytes 663560 | tf_op jit(solution)/shard_map/ppermute | solution.py:184
  38.1 1.5 %collective-permute-start.9 = (bf16[288,384]{1,0:T(8,128)(2,1)S(1)}, bf16[288,384]{1,0:T(8,128)(2,1)S(1)}, u32[]{:S(2)}, u32[]{:S(2)}) collective-permute-start(bf16[288,384]{1,0:T(8,128)(2,1)S(1)} %collective-permute-done.8.refs_10_), channel_id=1, source_target_pairs={{0,4},{4,0},{8,12},{12,8},{16,20},{20,16},{24,28},{28,24},{1,5},{5... | collective-permute-start | bytes 663560 | tf_op jit(solution)/shard_map/ppermute | solution.py:184
  39.7 1.7 %shard_map.102.relative = bf16[1024,256]{1,0:T(8,128)(2,1)S(1)} custom-call(s32[3]{0:T(128)S(1)} %copy-done, f32[64,768]{1,0:T(8,128)S(1)} %get-tuple-element.34.sin_ref, f32[64,768]{1,0:T(8,128)S(1)} %get-tuple-element.33.cos_ref, bf16[192,1536]{1,0:T(8,128)(2,1)S(1)} %bitcast.7), custom_call_target="tpu_custom_call" | custom-call | flops 2200000000 | bytes 4096 | tf_op jit(solution)/shard_map/pallas_call | solution.py:165
  42.0 0.9 %collective-permute-done.5.refs_7_ = bf16[288,384]{1,0:T(8,128)(2,1)S(1)} collective-permute-done((bf16[288,384]{1,0:T(8,128)(2,1)S(1)}, bf16[288,384]{1,0:T(8,128)(2,1)S(1)}, u32[]{:S(2)}, u32[]{:S(2)}) %collective-permute-start.5) | collective-permute-done | bytes 221216 | tf_op jit(solution)/shard_map/ppermute | solution.py:184
  42.9 1.2 %collective-permute-start.16 = (bf16[192,768]{1,0:T(8,128)(2,1)S(1)}, bf16[192,768]{1,0:T(8,128)(2,1)S(1)}, u32[]{:S(2)}, u32[]{:S(2)}) collective-permute-start(bf16[192,768]{1,0:T(8,128)(2,1)S(1)} %shard_map.106.refs_4_), channel_id=1, source_target_pairs={{0,24},{4,28},{8,16},{12,20},{16,8},{20,12},{24,0},{28,4},{1,25},{... | collective-permute-start | bytes 884744 | tf_op jit(solution)/shard_map/ppermute | solution.py:184
  44.1 3.5 %collective-permute-done.7.refs_9_ = bf16[288,384]{1,0:T(8,128)(2,1)S(1)} collective-permute-done((bf16[288,384]{1,0:T(8,128)(2,1)S(1)}, bf16[288,384]{1,0:T(8,128)(2,1)S(1)}, u32[]{:S(2)}, u32[]{:S(2)}) %collective-permute-start.7) | collective-permute-done | bytes 221216 | tf_op jit(solution)/shard_map/ppermute | solution.py:184
  47.6 2.2 %collective-permute-start.15 = (bf16[192,768]{1,0:T(8,128)(2,1)S(1)}, bf16[192,768]{1,0:T(8,128)(2,1)S(1)}, u32[]{:S(2)}, u32[]{:S(2)}) collective-permute-start(bf16[192,768]{1,0:T(8,128)(2,1)S(1)} %shard_map.106.refs_4_), channel_id=1, source_target_pairs={{0,16},{4,20},{8,24},{12,28},{16,0},{20,4},{24,8},{28,12},{1,17},{... | collective-permute-start | bytes 884744 | tf_op jit(solution)/shard_map/ppermute | solution.py:184
  49.8 1.9 %collective-permute-done.9.refs_11_ = bf16[288,384]{1,0:T(8,128)(2,1)S(1)} collective-permute-done((bf16[288,384]{1,0:T(8,128)(2,1)S(1)}, bf16[288,384]{1,0:T(8,128)(2,1)S(1)}, u32[]{:S(2)}, u32[]{:S(2)}) %collective-permute-start.9) | collective-permute-done | bytes 221216 | tf_op jit(solution)/shard_map/ppermute | solution.py:184
  52.2 7.6 %shard_map.101 = (bf16[1024,256]{1,0:T(8,128)(2,1)S(1)}, bf16[1024,256]{1,0:T(8,128)(2,1)S(1)}, bf16[1536,256]{1,0:T(8,128)(2,1)S(1)}) custom-call(s32[3]{0:T(128)S(1)} %copy-done, bf16[256,1536]{1,0:T(8,128)(2,1)S(1)} %copy-done.2, bf16[256,1536]{1,0:T(8,128)(2,1)S(1)} %collective-permute-done.refs_1_, ...), custom_call_target="tpu_custom_call" | custom-call | flops 6600000000 | bytes 4096 | tf_op jit(solution)/shard_map/pallas_call | solution.py:165
  59.9 5.0 %shard_map.103.weights_ref = bf16[4,2,256,768]{3,2,1,0:T(8,128)(2,1)S(1)} custom-call(s32[3]{0:T(128)S(1)} %copy-done, bf16[1024,256]{1,0:T(8,128)(2,1)S(1)} %get-tuple-element.20.query, bf16[1024,256]{1,0:T(8,128)(2,1)S(1)} %get-tuple-element.21.key, bf16[1024,256]{1,0:T(8,128)(2,1)S(1)} %shard_map.102.relative, f32[8,96]{1,0:T(8,128)S(1)} %copy-done.6, ...), custom_call_target="tpu_custom_call" | custom-call | flops 5500000256 | bytes 4096 | tf_op jit(solution)/shard_map/pallas_call | solution.py:165
  64.9 1.2 %shard_map.105 = bf16[256,384]{1,0:T(8,128)(2,1)S(1)} custom-call(s32[3]{0:T(128)S(1)} %copy-done, bf16[4,2,256,768]{3,2,1,0:T(8,128)(2,1)S(1)} %shard_map.103.weights_ref, bf16[1536,256]{1,0:T(8,128)(2,1)S(1)} %get-tuple-element.22.value), custom_call_target="tpu_custom_call" | custom-call | flops 1100000000 | bytes 4096 | tf_op jit(solution)/shard_map/pallas_call | solution.py:165
  66.0 1.6 %collective-permute-start.11 = (bf16[256,384]{1,0:T(8,128)(2,1)S(1)}, bf16[256,384]{1,0:T(8,128)(2,1)S(1)}, u32[]{:S(2)}, u32[]{:S(2)}) collective-permute-start(bf16[256,384]{1,0:T(8,128)(2,1)S(1)} %shard_map.105), channel_id=1, source_target_pairs={{0,2},{1,3},{2,0},{3,1},{4,6},{5,7},{6,4},{7,5},{8,10},{9,11},{10,... | collective-permute-start | bytes 589832 | tf_op jit(solution)/shard_map/ppermute | solution.py:184
  67.6 1.2 %shard_map.104 = (bf16[128,384]{1,0:T(8,128)(2,1)S(1)}, bf16[128,384]{1,0:T(8,128)(2,1)S(1)}) custom-call(s32[3]{0:T(128)S(1)} %copy-done, bf16[4,2,256,768]{3,2,1,0:T(8,128)(2,1)S(1)} %shard_map.103.weights_ref, bf16[1536,256]{1,0:T(8,128)(2,1)S(1)} %get-tuple-element.22.value), custom_call_target="tpu_custom_call" | custom-call | flops 1100000000 | bytes 4096 | tf_op jit(solution)/shard_map/pallas_call | solution.py:165
  69.4 1.9 %collective-permute-done.15.refs_6_ = bf16[192,768]{1,0:T(8,128)(2,1)S(1)} collective-permute-done((bf16[192,768]{1,0:T(8,128)(2,1)S(1)}, bf16[192,768]{1,0:T(8,128)(2,1)S(1)}, u32[]{:S(2)}, u32[]{:S(2)}) %collective-permute-start.15) | collective-permute-done | bytes 294944 | tf_op jit(solution)/shard_map/ppermute | solution.py:184
  73.8 3.3 %shard_map.107 = bf16[256,1536]{1,0:T(8,128)(2,1)} custom-call(s32[3]{0:T(128)S(1)} %copy-done, bf16[128,384]{1,0:T(8,128)(2,1)S(1)} %get-tuple-element.23.refs_0_, bf16[128,384]{1,0:T(8,128)(2,1)S(1)} %collective-permute-done.10.refs_1_, bf16[128,384]{1,0:T(8,128)(2,1)S(1)} %get-tuple-element.32.refs_2_, ...), custom_call_target="tpu_custom_call" | custom-call | flops 2750000128 | bytes 4096 | tf_op jit(solution)/shard_map/pallas_call | solution.py:165
  (49 shorter events, 6.9 us)
Async XLA Ops:
  0.0 39.7 %copy-start.3 = (bf16[1536,192]{0,1:T(8,128)(2,1)S(1)}, bf16[1536,192]{0,1:T(8,128)(2,1)}, u32[]{:S(2)}) copy-start(bf16[1536,192]{0,1:T(8,128)(2,1)} %param.17) | copy-start | bytes 1769476
  1.4 38.3 %copy-start = (s32[3]{0:T(128)S(1)}, s32[3]{0:T(128)}, u32[]{:S(2)}) copy-start(s32[3]{0:T(128)} %pad_add_fusion.info) | copy-start | bytes 40
  4.9 20.8 %collective-permute-start.1 = (bf16[256,1536]{1,0:T(8,128)(2,1)}, bf16[256,1536]{1,0:T(8,128)(2,1)S(1)}, u32[]{:S(2)}, u32[]{:S(2)}) collective-permute-start(bf16[256,1536]{1,0:T(8,128)(2,1)} %get-tuple-element.18.refs_0_), channel_id=1, source_target_pairs={{0,2},{1,3},{2,0},{3,1},{4,6},{5,7},{6,4},{7,5},{8,10},{9,11},{10,... | collective-permute-start | bytes 2359304 | tf_op jit(solution)/shard_map/ppermute | solution.py:184
  7.9 21.8 %collective-permute-start.4 = (bf16[288,384]{1,0:T(8,128)(2,1)}, bf16[288,384]{1,0:T(8,128)(2,1)S(1)}, u32[]{:S(2)}, u32[]{:S(2)}) collective-permute-start(bf16[288,384]{1,0:T(8,128)(2,1)} %get-tuple-element.19.refs_4_), channel_id=1, source_target_pairs={{0,8},{4,12},{8,0},{12,4},{16,24},{20,28},{24,16},{28,20},{1,9},{5... | collective-permute-start | bytes 663560 | tf_op jit(solution)/shard_map/ppermute | solution.py:184
  9.5 22.5 %collective-permute-start.6 = (bf16[288,384]{1,0:T(8,128)(2,1)}, bf16[288,384]{1,0:T(8,128)(2,1)S(1)}, u32[]{:S(2)}, u32[]{:S(2)}) collective-permute-start(bf16[288,384]{1,0:T(8,128)(2,1)} %get-tuple-element.19.refs_4_), channel_id=1, source_target_pairs={{0,16},{4,20},{8,24},{12,28},{16,0},{20,4},{24,8},{28,12},{1,17},{... | collective-permute-start | bytes 663560 | tf_op jit(solution)/shard_map/ppermute | solution.py:184
  12.0 40.2 %collective-permute-start = (bf16[256,1536]{1,0:T(8,128)(2,1)}, bf16[256,1536]{1,0:T(8,128)(2,1)S(1)}, u32[]{:S(2)}, u32[]{:S(2)}) collective-permute-start(bf16[256,1536]{1,0:T(8,128)(2,1)} %get-tuple-element.18.refs_0_), channel_id=1, source_target_pairs={{0,1},{1,0},{2,3},{3,2},{4,5},{5,4},{6,7},{7,6},{8,9},{9,8},{10,11... | collective-permute-start | bytes 2359304 | tf_op jit(solution)/shard_map/ppermute | solution.py:184
  12.0 13.7 %collective-permute-start.13 = (bf16[96,768]{1,0:T(8,128)(2,1)}, bf16[96,768]{1,0:T(8,128)(2,1)S(1)}, u32[]{:S(2)}, u32[]{:S(2)}) collective-permute-start(bf16[96,768]{1,0:T(8,128)(2,1)} %get-tuple-element.25.own_ref), channel_id=1, source_target_pairs={{0,4},{4,0},{8,12},{12,8},{16,20},{20,16},{24,28},{28,24},{1,5},{5... | collective-permute-start | bytes 442376 | tf_op jit(solution)/shard_map/ppermute | solution.py:184
  25.6 26.6 %collective-permute-start.2 = (bf16[256,1536]{1,0:T(8,128)(2,1)S(1)}, bf16[256,1536]{1,0:T(8,128)(2,1)S(1)}, u32[]{:S(2)}, u32[]{:S(2)}) collective-permute-start(bf16[256,1536]{1,0:T(8,128)(2,1)S(1)} %collective-permute-done.1.refs_2_), channel_id=1, source_target_pairs={{0,1},{1,0},{2,3},{3,2},{4,5},{5,4},{6,7},{7,6},{8,9},{9,8},{10,11... | collective-permute-start | bytes 2359304 | tf_op jit(solution)/shard_map/ppermute | solution.py:184
  25.7 10.3 %collective-permute-start.8 = (bf16[288,384]{1,0:T(8,128)(2,1)}, bf16[288,384]{1,0:T(8,128)(2,1)S(1)}, u32[]{:S(2)}, u32[]{:S(2)}) collective-permute-start(bf16[288,384]{1,0:T(8,128)(2,1)} %get-tuple-element.19.refs_4_), channel_id=1, source_target_pairs={{0,24},{4,28},{8,16},{12,20},{16,8},{20,12},{24,0},{28,4},{1,25},{... | collective-permute-start | bytes 663560 | tf_op jit(solution)/shard_map/ppermute | solution.py:184
  29.7 8.5 %collective-permute-start.3 = (bf16[288,384]{1,0:T(8,128)(2,1)}, bf16[288,384]{1,0:T(8,128)(2,1)S(1)}, u32[]{:S(2)}, u32[]{:S(2)}) collective-permute-start(bf16[288,384]{1,0:T(8,128)(2,1)} %get-tuple-element.19.refs_4_), channel_id=1, source_target_pairs={{0,4},{4,0},{8,12},{12,8},{16,20},{20,16},{24,28},{28,24},{1,5},{5... | collective-permute-start | bytes 663560 | tf_op jit(solution)/shard_map/ppermute | solution.py:184
  32.0 10.9 %collective-permute-start.5 = (bf16[288,384]{1,0:T(8,128)(2,1)S(1)}, bf16[288,384]{1,0:T(8,128)(2,1)S(1)}, u32[]{:S(2)}, u32[]{:S(2)}) collective-permute-start(bf16[288,384]{1,0:T(8,128)(2,1)S(1)} %collective-permute-done.4.refs_6_), channel_id=1, source_target_pairs={{0,4},{4,0},{8,12},{12,8},{16,20},{20,16},{24,28},{28,24},{1,5},{5... | collective-permute-start | bytes 663560 | tf_op jit(solution)/shard_map/ppermute | solution.py:184
  36.1 11.5 %collective-permute-start.7 = (bf16[288,384]{1,0:T(8,128)(2,1)S(1)}, bf16[288,384]{1,0:T(8,128)(2,1)S(1)}, u32[]{:S(2)}, u32[]{:S(2)}) collective-permute-start(bf16[288,384]{1,0:T(8,128)(2,1)S(1)} %collective-permute-done.6.refs_8_), channel_id=1, source_target_pairs={{0,4},{4,0},{8,12},{12,8},{16,20},{20,16},{24,28},{28,24},{1,5},{5... | collective-permute-start | bytes 663560 | tf_op jit(solution)/shard_map/ppermute | solution.py:184
  38.1 13.5 %collective-permute-start.9 = (bf16[288,384]{1,0:T(8,128)(2,1)S(1)}, bf16[288,384]{1,0:T(8,128)(2,1)S(1)}, u32[]{:S(2)}, u32[]{:S(2)}) collective-permute-start(bf16[288,384]{1,0:T(8,128)(2,1)S(1)} %collective-permute-done.8.refs_10_), channel_id=1, source_target_pairs={{0,4},{4,0},{8,12},{12,8},{16,20},{20,16},{24,28},{28,24},{1,5},{5... | collective-permute-start | bytes 663560 | tf_op jit(solution)/shard_map/ppermute | solution.py:184
  42.0 17.8 %copy-start.6 = (f32[8,96]{1,0:T(8,128)S(1)}, f32[8,96]{1,0:T(8,128)}, u32[]{:S(2)}) copy-start(f32[8,96]{1,0:T(8,128)} %content_ref.1) | copy-start | bytes 9220
  42.9 26.0 %collective-permute-start.16 = (bf16[192,768]{1,0:T(8,128)(2,1)S(1)}, bf16[192,768]{1,0:T(8,128)(2,1)S(1)}, u32[]{:S(2)}, u32[]{:S(2)}) collective-permute-start(bf16[192,768]{1,0:T(8,128)(2,1)S(1)} %shard_map.106.refs_4_), channel_id=1, source_target_pairs={{0,24},{4,28},{8,16},{12,20},{16,8},{20,12},{24,0},{28,4},{1,25},{... | collective-permute-start | bytes 884744 | tf_op jit(solution)/shard_map/ppermute | solution.py:184
  47.6 23.6 %collective-permute-start.15 = (bf16[192,768]{1,0:T(8,128)(2,1)S(1)}, bf16[192,768]{1,0:T(8,128)(2,1)S(1)}, u32[]{:S(2)}, u32[]{:S(2)}) collective-permute-start(bf16[192,768]{1,0:T(8,128)(2,1)S(1)} %shard_map.106.refs_4_), channel_id=1, source_target_pairs={{0,16},{4,20},{8,24},{12,28},{16,0},{20,4},{24,8},{28,12},{1,17},{... | collective-permute-start | bytes 884744 | tf_op jit(solution)/shard_map/ppermute | solution.py:184
  51.6 19.6 %collective-permute-start.14 = (bf16[192,768]{1,0:T(8,128)(2,1)S(1)}, bf16[192,768]{1,0:T(8,128)(2,1)S(1)}, u32[]{:S(2)}, u32[]{:S(2)}) collective-permute-start(bf16[192,768]{1,0:T(8,128)(2,1)S(1)} %shard_map.106.refs_4_), channel_id=1, source_target_pairs={{0,8},{4,12},{8,0},{12,4},{16,24},{20,28},{24,16},{28,20},{1,9},{5... | collective-permute-start | bytes 884744 | tf_op jit(solution)/shard_map/ppermute | solution.py:184
  66.0 5.7 %collective-permute-start.11 = (bf16[256,384]{1,0:T(8,128)(2,1)S(1)}, bf16[256,384]{1,0:T(8,128)(2,1)S(1)}, u32[]{:S(2)}, u32[]{:S(2)}) collective-permute-start(bf16[256,384]{1,0:T(8,128)(2,1)S(1)} %shard_map.105), channel_id=1, source_target_pairs={{0,2},{1,3},{2,0},{3,1},{4,6},{5,7},{6,4},{7,5},{8,10},{9,11},{10,... | collective-permute-start | bytes 589832 | tf_op jit(solution)/shard_map/ppermute | solution.py:184
  68.8 3.1 %collective-permute-start.10 = (bf16[128,384]{1,0:T(8,128)(2,1)S(1)}, bf16[128,384]{1,0:T(8,128)(2,1)S(1)}, u32[]{:S(2)}, u32[]{:S(2)}) collective-permute-start(bf16[128,384]{1,0:T(8,128)(2,1)S(1)} %get-tuple-element.24), channel_id=1, source_target_pairs={{0,1},{1,0},{2,3},{3,2},{4,5},{5,4},{6,7},{7,6},{8,9},{9,8},{10,11... | collective-permute-start | bytes 294920 | tf_op jit(solution)/shard_map/ppermute | solution.py:184
  68.9 3.5 %collective-permute-start.20 = (bf16[192,768]{1,0:T(8,128)(2,1)S(1)}, bf16[192,768]{1,0:T(8,128)(2,1)S(1)}, u32[]{:S(2)}, u32[]{:S(2)}) collective-permute-start(bf16[192,768]{1,0:T(8,128)(2,1)S(1)} %collective-permute-done.16.refs_7_), channel_id=1, source_target_pairs={{0,1},{1,0},{2,3},{3,2},{4,5},{5,4},{6,7},{7,6},{8,9},{9,8},{10,11... | collective-permute-start | bytes 884744 | tf_op jit(solution)/shard_map/ppermute | solution.py:184
  71.2 1.6 %collective-permute-start.19 = (bf16[192,768]{1,0:T(8,128)(2,1)S(1)}, bf16[192,768]{1,0:T(8,128)(2,1)S(1)}, u32[]{:S(2)}, u32[]{:S(2)}) collective-permute-start(bf16[192,768]{1,0:T(8,128)(2,1)S(1)} %collective-permute-done.15.refs_6_), channel_id=1, source_target_pairs={{0,1},{1,0},{2,3},{3,2},{4,5},{5,4},{6,7},{7,6},{8,9},{9,8},{10,11... | collective-permute-start | bytes 884744 | tf_op jit(solution)/shard_map/ppermute | solution.py:184
  71.3 2.0 %collective-permute-start.18 = (bf16[192,768]{1,0:T(8,128)(2,1)S(1)}, bf16[192,768]{1,0:T(8,128)(2,1)S(1)}, u32[]{:S(2)}, u32[]{:S(2)}) collective-permute-start(bf16[192,768]{1,0:T(8,128)(2,1)S(1)} %collective-permute-done.14.refs_5_), channel_id=1, source_target_pairs={{0,1},{1,0},{2,3},{3,2},{4,5},{5,4},{6,7},{7,6},{8,9},{9,8},{10,11... | collective-permute-start | bytes 884744 | tf_op jit(solution)/shard_map/ppermute | solution.py:184
  71.8 1.9 %collective-permute-start.17 = (bf16[192,768]{1,0:T(8,128)(2,1)S(1)}, bf16[192,768]{1,0:T(8,128)(2,1)S(1)}, u32[]{:S(2)}, u32[]{:S(2)}) collective-permute-start(bf16[192,768]{1,0:T(8,128)(2,1)S(1)} %shard_map.106.refs_4_), channel_id=1, source_target_pairs={{0,1},{1,0},{2,3},{3,2},{4,5},{5,4},{6,7},{7,6},{8,9},{9,8},{10,11... | collective-permute-start | bytes 884744 | tf_op jit(solution)/shard_map/ppermute | solution.py:184
  71.9 1.9 %collective-permute-start.12 = (bf16[128,384]{1,0:T(8,128)(2,1)S(1)}, bf16[128,384]{1,0:T(8,128)(2,1)S(1)}, u32[]{:S(2)}, u32[]{:S(2)}) collective-permute-start(bf16[128,384]{1,0:T(8,128)(2,1)S(1)} %get-tuple-element.31), channel_id=1, source_target_pairs={{0,1},{1,0},{2,3},{3,2},{4,5},{5,4},{6,7},{7,6},{8,9},{9,8},{10,11... | collective-permute-start | bytes 294920 | tf_op jit(solution)/shard_map/ppermute | solution.py:184
  (5 other events, 52.5 us)

commit v4 on v3

--- a/solution.py
+++ b/solution.py
@@ -200,7 +200,7 @@
 
 
 def prepare_kernel(tm_count, info, *refs):
-    gain_ref, cut_ref, half_ref, normed_ref, stage, frame, sems = refs[5:]
+    gain_ref, cut_ref, both_ref, half_ref, normed_ref, stage, frame, sems = refs[5:]
     rows, width = stage.shape[1], stage.shape[2] // tm_count
     query_ref, key_ref, value_ref = (stage.at[i] for i in range(3))
     half_width = half_ref.shape[1]
@@ -220,6 +220,11 @@
             cut_ref[:rows, width:] = key_ref[:, columns]
             cut_ref[rows:, :width] = value_ref[: rows // 2, columns]
             cut_ref[rows:, width:] = value_ref[rows // 2 :, columns]
+
+    cut_rows, half_rows = cut_ref.shape[0], half_ref.shape[0]
+    both_ref[:cut_rows, :] = cut_ref[...]
+    both_ref[cut_rows : cut_rows + half_rows, :] = half_ref[:, : 2 * width]
+    both_ref[cut_rows + half_rows :, :] = half_ref[:, 2 * width :]
 
 
 def angle_tables(row_count, model_width, step):
@@ -271,7 +276,8 @@
     rows, width = cuts.shape[1] * 2 // 3, cuts.shape[2] // 2
     wide = query_ref.shape[1]
     spots = [pl.multiple_of((info[0] ^ k) * block_len, block_len) for k in range(tm_count)]
-    cut_copies = load(cut_refs, [cuts.at[k] for k in range(dp_count)], cut_sems)
+    sources = [ref.at[: cuts.shape[1], :] for ref in cut_refs]
+    cut_copies = load(sources, [cuts.at[k] for k in range(dp_count)], cut_sems)
     normed_copies = load(
         normed_refs, [normed.at[pl.ds(spot, block_len), :] for spot in spots], normed_sems
     )
@@ -385,7 +391,11 @@
     rows = own_ref.shape[0]
     own = lax.rem(info[1], 2)
     pair_ref[pl.ds(pl.multiple_of(own * rows, 16), rows), :] = own_ref[...]
-    pair_ref[pl.ds(pl.multiple_of((1 - own) * rows, 16), rows), :] = beside_ref[...]
+    first = beside_ref.shape[0] - 2 * rows
+    other = pl.ds(pl.multiple_of((1 - own) * rows, 16), rows)
+    width = beside_ref.shape[1]
+    pair_ref[other, :width] = beside_ref[first : first + rows, :]
+    pair_ref[other, width:] = beside_ref[first + rows :, :]
 
 
 def out_kernel(tm_count, pair_count, info, *refs):
@@ -445,10 +455,11 @@
     total_len = tm_count * block_len
     row_count = 4 * block_len
 
-    cut, half_output, normed_own = call(
+    cut, both, half_output, normed_own = call(
         functools.partial(prepare_kernel, tm_count),
         (
             shaped(in_rows // 2 * 3, 2 * width),
+            shaped(in_rows // 2 * 3 + 2 * out_rows, 2 * width),
             shaped(out_rows, model_width // 2),
             shaped(block_len, model_width),
         ),
@@ -465,13 +476,16 @@
         room=56,
     )
     cut_far = send_far(cut, "dp")
+    normed_far = send_far(normed_own, "tm")
+    cut_pieces = send_beside(cut_far | {0: both}, "dp")
+    cut_pieces[0] = cut
+    arrived = [cut_far[k] for k in range(2, dp_count, 2)] + cut_pieces[3 : dp_count - 2 : 2]
     pair = call(
         pair_kernel,
         shaped(2 * out_rows, model_width // 2),
-        (scalar, (half_output, near), (swap(half_output, "dp", 1), near)),
+        (scalar, (half_output, near), (cut_pieces[1], near)),
         micros=0.5,
     )
-    cut_pieces = send_beside(cut_far, "dp")
     step = 32
     sines, cosines = angle_tables(row_count, model_width, step)
     relative = call(
@@ -481,7 +495,9 @@
         [pltpu.VMEM((row_count, model_width), half)],
         micros=2.0,
     )
-    normed_pieces = send_beside(send_far(normed_own, "tm"), "tm")
+    normed_pieces = send_beside(
+        {k: later(x, *arrived, relative, pair) for k, x in normed_far.items()}, "tm"
+    )
     pairs = send_far(later(pair, *[cut_far[k] for k in range(2, dp_count, 2)]), "dp")
     query, key, value = call(
         functools.partial(project_kernel, tm_count, dp_count, head_size),

time: 77.5 us -> 68.1 us (0.88)
  starting transfers between devices: 24.9 us -> 19.8 us
  waiting for transfers between devices: 25.8 us -> 21.3 us
    ppermute x21 -> x20, starting transfers between devices: 24.9 us -> 19.8 us  [swap(): return lax.ppermute(block, axis, [(i, i ^ distance) for i in range(count)])]
    ppermute x21 -> x20, waiting for transfers between devices: 25.8 us -> 21.3 us  [swap(): return lax.ppermute(block, axis, [(i, i ^ distance) for i in range(count)])]
  transfers between devices with their start and end apart: 21 -> 20, of which waited for: 11 -> 9; matrix products, arithmetic and copies ran while one was open for 1% -> 1% of each run, Pallas kernels for 22% -> 25%
where the time goes in v4:
time: 68.1 us; the launch traced here: 67.9 us
  Pallas kernels  24.1 us (35%)
  waiting for transfers between devices  21.3 us (31%)
  starting transfers between devices  19.8 us (29%)
  other arithmetic  1.53 us (2%)
  between operations  1.07 us (2%)
    pallas_call x8, Pallas kernels, call(): pl.pallas_call(kernel, out_shape=out_shape, in_specs=list(specs), out_spe...  24.1 us
    ppermute x20, waiting for transfers between devices, swap(): return lax.ppermute(block, axis, [(i, i ^ distance) for i in range(count)])  21.3 us
    ppermute x20, starting transfers between devices, swap(): return lax.ppermute(block, axis, [(i, i ^ distance) for i in range(count)])  19.8 us
  transfers between devices with their start and end apart: 20, of which 9 were waited for; matrix products, arithmetic and copies ran while one was open for 1% of the time, Pallas kernels for 25%

profile of v4, /device:TPU:0, one launch (start us, length us, event | category | flops | bytes accessed | tf_op | source)
XLA Modules:
  0.0 67.9 jit_solution(11517834744733822450)
XLA Ops:
  0.7 0.7 pad_add_fusion.info
  1.4 3.6 %shard_map.100 = (bf16[288,384]{1,0:T(8,128)(2,1)}, bf16[480,384]{1,0:T(8,128)(2,1)}, bf16[96,768]{1,0:T(8,128)(2,1)}, bf16[256,1536]{1,0:T(8,128)(2,1)}) custom-call(s32[3]{0:T(128)} %pad_add_fusion.info, bf16[192,768]{1,0:T(8,128)(2,1)} %refs_0_.1, bf16[192,768]{1,0:T(8,128)(2,1)} %refs_1_.1, bf16[192,768]{1,0:T(8,128)(2,1)} %refs_2_.1, ...), custom_call_target="tpu_custom_call" | custom-call | flops 1100000000 | bytes 4096 | tf_op jit(solution)/shard_map/pallas_call | solution.py:165
  5.0 3.1 %collective-permute-start = (bf16[288,384]{1,0:T(8,128)(2,1)}, bf16[288,384]{1,0:T(8,128)(2,1)S(1)}, u32[]{:S(2)}, u32[]{:S(2)}) collective-permute-start(bf16[288,384]{1,0:T(8,128)(2,1)} %get-tuple-element.22.refs_4_), channel_id=1, source_target_pairs={{0,8},{4,12},{8,0},{12,4},{16,24},{20,28},{24,16},{28,20},{1,9},{5... | collective-permute-start | bytes 663560 | tf_op jit(solution)/shard_map/ppermute | solution.py:184
  8.1 2.6 %collective-permute-start.1 = (bf16[288,384]{1,0:T(8,128)(2,1)}, bf16[288,384]{1,0:T(8,128)(2,1)S(1)}, u32[]{:S(2)}, u32[]{:S(2)}) collective-permute-start(bf16[288,384]{1,0:T(8,128)(2,1)} %get-tuple-element.22.refs_4_), channel_id=1, source_target_pairs={{0,16},{4,20},{8,24},{12,28},{16,0},{20,4},{24,8},{28,12},{1,17},{... | collective-permute-start | bytes 663560 | tf_op jit(solution)/shard_map/ppermute | solution.py:184
  10.7 1.7 %collective-permute-start.5 = (bf16[480,384]{1,0:T(8,128)(2,1)}, bf16[480,384]{1,0:T(8,128)(2,1)S(1)}, u32[]{:S(2)}, u32[]{:S(2)}) collective-permute-start(bf16[480,384]{1,0:T(8,128)(2,1)} %get-tuple-element.24), channel_id=1, source_target_pairs={{0,4},{4,0},{8,12},{12,8},{16,20},{20,16},{24,28},{28,24},{1,5},{5... | collective-permute-start | bytes 1105928 | tf_op jit(solution)/shard_map/ppermute | solution.py:184
  12.4 1.5 %collective-permute-start.7 = (bf16[256,1536]{1,0:T(8,128)(2,1)}, bf16[256,1536]{1,0:T(8,128)(2,1)S(1)}, u32[]{:S(2)}, u32[]{:S(2)}) collective-permute-start(bf16[256,1536]{1,0:T(8,128)(2,1)} %get-tuple-element.25.refs_0_), channel_id=1, source_target_pairs={{0,2},{1,3},{2,0},{3,1},{4,6},{5,7},{6,4},{7,5},{8,10},{9,11},{10,... | collective-permute-start | bytes 2359304 | tf_op jit(solution)/shard_map/ppermute | solution.py:184
  14.0 0.8 %multiply_cosine_fusion = (f32[64,768]{1,0:T(8,128)S(1)}, f32[64,768]{1,0:T(8,128)S(1)}) fusion(f32[768]{0:T(1024)S(1)} %multiply_exponential_fusion, f32[64]{0:T(128)S(1)} %pad_maximum_fusion), kind=kLoop, calls=%fused_computation | loop fusion | flops 49152 | bytes 396544 | tf_op jit(solution)/shard_map/cos | solution.py:238
  14.8 2.9 %collective-permute-done.refs_6_ = bf16[288,384]{1,0:T(8,128)(2,1)S(1)} collective-permute-done((bf16[288,384]{1,0:T(8,128)(2,1)}, bf16[288,384]{1,0:T(8,128)(2,1)S(1)}, u32[]{:S(2)}, u32[]{:S(2)}) %collective-permute-start) | collective-permute-done | bytes 221216 | tf_op jit(solution)/shard_map/ppermute | solution.py:184
  17.7 1.7 %collective-permute-start.3 = (bf16[288,384]{1,0:T(8,128)(2,1)S(1)}, bf16[288,384]{1,0:T(8,128)(2,1)S(1)}, u32[]{:S(2)}, u32[]{:S(2)}) collective-permute-start(bf16[288,384]{1,0:T(8,128)(2,1)S(1)} %collective-permute-done.refs_6_), channel_id=1, source_target_pairs={{0,4},{4,0},{8,12},{12,8},{16,20},{20,16},{24,28},{28,24},{1,5},{5... | collective-permute-start | bytes 663560 | tf_op jit(solution)/shard_map/ppermute | solution.py:184
  19.4 7.7 %collective-permute-done.1.refs_8_ = bf16[288,384]{1,0:T(8,128)(2,1)S(1)} collective-permute-done((bf16[288,384]{1,0:T(8,128)(2,1)}, bf16[288,384]{1,0:T(8,128)(2,1)S(1)}, u32[]{:S(2)}, u32[]{:S(2)}) %collective-permute-start.1) | collective-permute-done | bytes 221216 | tf_op jit(solution)/shard_map/ppermute | solution.py:184
  27.0 1.5 %collective-permute-start.4 = (bf16[288,384]{1,0:T(8,128)(2,1)S(1)}, bf16[288,384]{1,0:T(8,128)(2,1)S(1)}, u32[]{:S(2)}, u32[]{:S(2)}) collective-permute-start(bf16[288,384]{1,0:T(8,128)(2,1)S(1)} %collective-permute-done.1.refs_8_), channel_id=1, source_target_pairs={{0,4},{4,0},{8,12},{12,8},{16,20},{20,16},{24,28},{28,24},{1,5},{5... | collective-permute-start | bytes 663560 | tf_op jit(solution)/shard_map/ppermute | solution.py:184
  28.6 1.7 %shard_map.101.relative = bf16[1024,256]{1,0:T(8,128)(2,1)S(1)} custom-call(s32[3]{0:T(128)S(1)} %copy-done, f32[64,768]{1,0:T(8,128)S(1)} %get-tuple-element.40.sin_ref, f32[64,768]{1,0:T(8,128)S(1)} %get-tuple-element.39.cos_ref, bf16[192,1536]{1,0:T(8,128)(2,1)S(1)} %bitcast.7), custom_call_target="tpu_custom_call" | custom-call | flops 2200000000 | bytes 4096 | tf_op jit(solution)/shard_map/pallas_call | solution.py:165
  30.3 0.6 shard_map.102.refs_4_
  30.9 2.0 %collective-permute-done.4.refs_9_ = bf16[288,384]{1,0:T(8,128)(2,1)S(1)} collective-permute-done((bf16[288,384]{1,0:T(8,128)(2,1)S(1)}, bf16[288,384]{1,0:T(8,128)(2,1)S(1)}, u32[]{:S(2)}, u32[]{:S(2)}) %collective-permute-start.4) | collective-permute-done | bytes 221216 | tf_op jit(solution)/shard_map/ppermute | solution.py:184
  33.5 1.5 %collective-permute-start.9 = (bf16[288,384]{1,0:T(8,128)(2,1)S(1)}, bf16[288,384]{1,0:T(8,128)(2,1)S(1)}, u32[]{:S(2)}, u32[]{:S(2)}) collective-permute-start(bf16[288,384]{1,0:T(8,128)(2,1)S(1)} %collective-permute-done.2.refs_10_), channel_id=1, source_target_pairs={{0,4},{4,0},{8,12},{12,8},{16,20},{20,16},{24,28},{28,24},{1,5},{5... | collective-permute-start | bytes 663560 | tf_op jit(solution)/shard_map/ppermute | solution.py:184
  35.0 2.5 %collective-permute-start.15 = (bf16[192,768]{1,0:T(8,128)(2,1)S(1)}, bf16[192,768]{1,0:T(8,128)(2,1)S(1)}, u32[]{:S(2)}, u32[]{:S(2)}) collective-permute-start(bf16[192,768]{1,0:T(8,128)(2,1)S(1)} %shard_map.102.refs_4_), channel_id=1, source_target_pairs={{0,24},{4,28},{8,16},{12,20},{16,8},{20,12},{24,0},{28,4},{1,25},{... | collective-permute-start | bytes 884744 | tf_op jit(solution)/shard_map/ppermute | solution.py:184
  37.5 3.4 %collective-permute-done.9.refs_11_ = bf16[288,384]{1,0:T(8,128)(2,1)S(1)} collective-permute-done((bf16[288,384]{1,0:T(8,128)(2,1)S(1)}, bf16[288,384]{1,0:T(8,128)(2,1)S(1)}, u32[]{:S(2)}, u32[]{:S(2)}) %collective-permute-start.9) | collective-permute-done | bytes 221216 | tf_op jit(solution)/shard_map/ppermute | solution.py:184
  40.9 7.6 %shard_map.103 = (bf16[1024,256]{1,0:T(8,128)(2,1)S(1)}, bf16[1024,256]{1,0:T(8,128)(2,1)S(1)}, bf16[1536,256]{1,0:T(8,128)(2,1)S(1)}) custom-call(s32[3]{0:T(128)S(1)} %copy-done, bf16[256,1536]{1,0:T(8,128)(2,1)S(1)} %copy-done.2, bf16[256,1536]{1,0:T(8,128)(2,1)S(1)} %collective-permute-done.6.refs_1_, ...), custom_call_target="tpu_custom_call" | custom-call | flops 6600000000 | bytes 4096 | tf_op jit(solution)/shard_map/pallas_call | solution.py:165
  48.5 5.0 %shard_map.104.weights_ref = bf16[4,2,256,768]{3,2,1,0:T(8,128)(2,1)S(1)} custom-call(s32[3]{0:T(128)S(1)} %copy-done, bf16[1024,256]{1,0:T(8,128)(2,1)S(1)} %get-tuple-element.27.query, bf16[1024,256]{1,0:T(8,128)(2,1)S(1)} %get-tuple-element.28.key, bf16[1024,256]{1,0:T(8,128)(2,1)S(1)} %shard_map.101.relative, f32[8,96]{1,0:T(8,128)S(1)} %copy-done.5, ...), custom_call_target="tpu_custom_call" | custom-call | flops 5500000256 | bytes 4096 | tf_op jit(solution)/shard_map/pallas_call | solution.py:165
  53.5 1.2 %shard_map.106 = bf16[256,384]{1,0:T(8,128)(2,1)S(1)} custom-call(s32[3]{0:T(128)S(1)} %copy-done, bf16[4,2,256,768]{3,2,1,0:T(8,128)(2,1)S(1)} %shard_map.104.weights_ref, bf16[1536,256]{1,0:T(8,128)(2,1)S(1)} %get-tuple-element.29.value), custom_call_target="tpu_custom_call" | custom-call | flops 1100000000 | bytes 4096 | tf_op jit(solution)/shard_map/pallas_call | solution.py:165
  54.7 1.6 %collective-permute-start.11 = (bf16[256,384]{1,0:T(8,128)(2,1)S(1)}, bf16[256,384]{1,0:T(8,128)(2,1)S(1)}, u32[]{:S(2)}, u32[]{:S(2)}) collective-permute-start(bf16[256,384]{1,0:T(8,128)(2,1)S(1)} %shard_map.106), channel_id=1, source_target_pairs={{0,2},{1,3},{2,0},{3,1},{4,6},{5,7},{6,4},{7,5},{8,10},{9,11},{10,... | collective-permute-start | bytes 589832 | tf_op jit(solution)/shard_map/ppermute | solution.py:184
  56.3 1.2 %shard_map.105 = (bf16[128,384]{1,0:T(8,128)(2,1)S(1)}, bf16[128,384]{1,0:T(8,128)(2,1)S(1)}) custom-call(s32[3]{0:T(128)S(1)} %copy-done, bf16[4,2,256,768]{3,2,1,0:T(8,128)(2,1)S(1)} %shard_map.104.weights_ref, bf16[1536,256]{1,0:T(8,128)(2,1)S(1)} %get-tuple-element.29.value), custom_call_target="tpu_custom_call" | custom-call | flops 1100000000 | bytes 4096 | tf_op jit(solution)/shard_map/pallas_call | solution.py:165
  58.0 3.9 %collective-permute-done.14.refs_6_ = bf16[192,768]{1,0:T(8,128)(2,1)S(1)} collective-permute-done((bf16[192,768]{1,0:T(8,128)(2,1)S(1)}, bf16[192,768]{1,0:T(8,128)(2,1)S(1)}, u32[]{:S(2)}, u32[]{:S(2)}) %collective-permute-start.14) | collective-permute-done | bytes 294944 | tf_op jit(solution)/shard_map/ppermute | solution.py:184
  64.5 3.3 %shard_map.107 = bf16[256,1536]{1,0:T(8,128)(2,1)} custom-call(s32[3]{0:T(128)S(1)} %copy-done, bf16[128,384]{1,0:T(8,128)(2,1)S(1)} %get-tuple-element.30.refs_0_, bf16[128,384]{1,0:T(8,128)(2,1)S(1)} %collective-permute-done.10.refs_1_, bf16[128,384]{1,0:T(8,128)(2,1)S(1)} %get-tuple-element.38.refs_2_, ...), custom_call_target="tpu_custom_call" | custom-call | flops 2750000128 | bytes 4096 | tf_op jit(solution)/shard_map/pallas_call | solution.py:165
  (47 shorter events, 3.8 us)
Async XLA Ops:
  0.0 28.6 %copy-start.3 = (bf16[1536,192]{0,1:T(8,128)(2,1)S(1)}, bf16[1536,192]{0,1:T(8,128)(2,1)}, u32[]{:S(2)}) copy-start(bf16[1536,192]{0,1:T(8,128)(2,1)} %param.17) | copy-start | bytes 1769476
  1.4 27.2 %copy-start = (s32[3]{0:T(128)S(1)}, s32[3]{0:T(128)}, u32[]{:S(2)}) copy-start(s32[3]{0:T(128)} %pad_add_fusion.info) | copy-start | bytes 40
  5.0 12.7 %collective-permute-start = (bf16[288,384]{1,0:T(8,128)(2,1)}, bf16[288,384]{1,0:T(8,128)(2,1)S(1)}, u32[]{:S(2)}, u32[]{:S(2)}) collective-permute-start(bf16[288,384]{1,0:T(8,128)(2,1)} %get-tuple-element.22.refs_4_), channel_id=1, source_target_pairs={{0,8},{4,12},{8,0},{12,4},{16,24},{20,28},{24,16},{28,20},{1,9},{5... | collective-permute-start | bytes 663560 | tf_op jit(solution)/shard_map/ppermute | solution.py:184
  8.1 18.9 %collective-permute-start.1 = (bf16[288,384]{1,0:T(8,128)(2,1)}, bf16[288,384]{1,0:T(8,128)(2,1)S(1)}, u32[]{:S(2)}, u32[]{:S(2)}) collective-permute-start(bf16[288,384]{1,0:T(8,128)(2,1)} %get-tuple-element.22.refs_4_), channel_id=1, source_target_pairs={{0,16},{4,20},{8,24},{12,28},{16,0},{20,4},{24,8},{28,12},{1,17},{... | collective-permute-start | bytes 663560 | tf_op jit(solution)/shard_map/ppermute | solution.py:184
  10.7 20.2 %collective-permute-start.2 = (bf16[288,384]{1,0:T(8,128)(2,1)}, bf16[288,384]{1,0:T(8,128)(2,1)S(1)}, u32[]{:S(2)}, u32[]{:S(2)}) collective-permute-start(bf16[288,384]{1,0:T(8,128)(2,1)} %get-tuple-element.22.refs_4_), channel_id=1, source_target_pairs={{0,24},{4,28},{8,16},{12,20},{16,8},{20,12},{24,0},{28,4},{1,25},{... | collective-permute-start | bytes 663560 | tf_op jit(solution)/shard_map/ppermute | solution.py:184
  10.7 19.6 %collective-permute-start.5 = (bf16[480,384]{1,0:T(8,128)(2,1)}, bf16[480,384]{1,0:T(8,128)(2,1)S(1)}, u32[]{:S(2)}, u32[]{:S(2)}) collective-permute-start(bf16[480,384]{1,0:T(8,128)(2,1)} %get-tuple-element.24), channel_id=1, source_target_pairs={{0,4},{4,0},{8,12},{12,8},{16,20},{20,16},{24,28},{28,24},{1,5},{5... | collective-permute-start | bytes 1105928 | tf_op jit(solution)/shard_map/ppermute | solution.py:184
  12.4 20.6 %collective-permute-start.7 = (bf16[256,1536]{1,0:T(8,128)(2,1)}, bf16[256,1536]{1,0:T(8,128)(2,1)S(1)}, u32[]{:S(2)}, u32[]{:S(2)}) collective-permute-start(bf16[256,1536]{1,0:T(8,128)(2,1)} %get-tuple-element.25.refs_0_), channel_id=1, source_target_pairs={{0,2},{1,3},{2,0},{3,1},{4,6},{5,7},{6,4},{7,5},{8,10},{9,11},{10,... | collective-permute-start | bytes 2359304 | tf_op jit(solution)/shard_map/ppermute | solution.py:184
  17.7 13.2 %collective-permute-start.3 = (bf16[288,384]{1,0:T(8,128)(2,1)S(1)}, bf16[288,384]{1,0:T(8,128)(2,1)S(1)}, u32[]{:S(2)}, u32[]{:S(2)}) collective-permute-start(bf16[288,384]{1,0:T(8,128)(2,1)S(1)} %collective-permute-done.refs_6_), channel_id=1, source_target_pairs={{0,4},{4,0},{8,12},{12,8},{16,20},{20,16},{24,28},{28,24},{1,5},{5... | collective-permute-start | bytes 663560 | tf_op jit(solution)/shard_map/ppermute | solution.py:184
  27.0 5.9 %collective-permute-start.4 = (bf16[288,384]{1,0:T(8,128)(2,1)S(1)}, bf16[288,384]{1,0:T(8,128)(2,1)S(1)}, u32[]{:S(2)}, u32[]{:S(2)}) collective-permute-start(bf16[288,384]{1,0:T(8,128)(2,1)S(1)} %collective-permute-done.1.refs_8_), channel_id=1, source_target_pairs={{0,4},{4,0},{8,12},{12,8},{16,20},{20,16},{24,28},{28,24},{1,5},{5... | collective-permute-start | bytes 663560 | tf_op jit(solution)/shard_map/ppermute | solution.py:184
  30.9 17.6 %copy-start.5 = (f32[8,96]{1,0:T(8,128)S(1)}, f32[8,96]{1,0:T(8,128)}, u32[]{:S(2)}) copy-start(f32[8,96]{1,0:T(8,128)} %content_ref.1) | copy-start | bytes 9220
  30.9 17.6 %copy-start.6 = (f32[8,96]{1,0:T(8,128)S(1)}, f32[8,96]{1,0:T(8,128)}, u32[]{:S(2)}) copy-start(f32[8,96]{1,0:T(8,128)} %position_ref.1) | copy-start | bytes 9220
  33.0 7.9 %collective-permute-start.6 = (bf16[256,1536]{1,0:T(8,128)(2,1)S(1)}, bf16[256,1536]{1,0:T(8,128)(2,1)S(1)}, u32[]{:S(2)}, u32[]{:S(2)}) collective-permute-start(bf16[256,1536]{1,0:T(8,128)(2,1)S(1)} %copy-done.2), channel_id=1, source_target_pairs={{0,1},{1,0},{2,3},{3,2},{4,5},{5,4},{6,7},{7,6},{8,9},{9,8},{10,11... | collective-permute-start | bytes 2359304 | tf_op jit(solution)/shard_map/ppermute | solution.py:184
  33.0 7.9 %collective-permute-start.8 = (bf16[256,1536]{1,0:T(8,128)(2,1)S(1)}, bf16[256,1536]{1,0:T(8,128)(2,1)S(1)}, u32[]{:S(2)}, u32[]{:S(2)}) collective-permute-start(bf16[256,1536]{1,0:T(8,128)(2,1)S(1)} %collective-permute-done.7.refs_2_), channel_id=1, source_target_pairs={{0,1},{1,0},{2,3},{3,2},{4,5},{5,4},{6,7},{7,6},{8,9},{9,8},{10,11... | collective-permute-start | bytes 2359304 | tf_op jit(solution)/shard_map/ppermute | solution.py:184
  33.5 7.4 %collective-permute-start.9 = (bf16[288,384]{1,0:T(8,128)(2,1)S(1)}, bf16[288,384]{1,0:T(8,128)(2,1)S(1)}, u32[]{:S(2)}, u32[]{:S(2)}) collective-permute-start(bf16[288,384]{1,0:T(8,128)(2,1)S(1)} %collective-permute-done.2.refs_10_), channel_id=1, source_target_pairs={{0,4},{4,0},{8,12},{12,8},{16,20},{20,16},{24,28},{28,24},{1,5},{5... | collective-permute-start | bytes 663560 | tf_op jit(solution)/shard_map/ppermute | solution.py:184
  35.0 22.5 %collective-permute-start.15 = (bf16[192,768]{1,0:T(8,128)(2,1)S(1)}, bf16[192,768]{1,0:T(8,128)(2,1)S(1)}, u32[]{:S(2)}, u32[]{:S(2)}) collective-permute-start(bf16[192,768]{1,0:T(8,128)(2,1)S(1)} %shard_map.102.refs_4_), channel_id=1, source_target_pairs={{0,24},{4,28},{8,16},{12,20},{16,8},{20,12},{24,0},{28,4},{1,25},{... | collective-permute-start | bytes 884744 | tf_op jit(solution)/shard_map/ppermute | solution.py:184
  37.5 24.4 %collective-permute-start.14 = (bf16[192,768]{1,0:T(8,128)(2,1)S(1)}, bf16[192,768]{1,0:T(8,128)(2,1)S(1)}, u32[]{:S(2)}, u32[]{:S(2)}) collective-permute-start(bf16[192,768]{1,0:T(8,128)(2,1)S(1)} %shard_map.102.refs_4_), channel_id=1, source_target_pairs={{0,16},{4,20},{8,24},{12,28},{16,0},{20,4},{24,8},{28,12},{1,17},{... | collective-permute-start | bytes 884744 | tf_op jit(solution)/shard_map/ppermute | solution.py:184
  40.9 21.0 %collective-permute-start.13 = (bf16[192,768]{1,0:T(8,128)(2,1)S(1)}, bf16[192,768]{1,0:T(8,128)(2,1)S(1)}, u32[]{:S(2)}, u32[]{:S(2)}) collective-permute-start(bf16[192,768]{1,0:T(8,128)(2,1)S(1)} %shard_map.102.refs_4_), channel_id=1, source_target_pairs={{0,8},{4,12},{8,0},{12,4},{16,24},{20,28},{24,16},{28,20},{1,9},{5... | collective-permute-start | bytes 884744 | tf_op jit(solution)/shard_map/ppermute | solution.py:184
  54.7 7.7 %collective-permute-start.11 = (bf16[256,384]{1,0:T(8,128)(2,1)S(1)}, bf16[256,384]{1,0:T(8,128)(2,1)S(1)}, u32[]{:S(2)}, u32[]{:S(2)}) collective-permute-start(bf16[256,384]{1,0:T(8,128)(2,1)S(1)} %shard_map.106), channel_id=1, source_target_pairs={{0,2},{1,3},{2,0},{3,1},{4,6},{5,7},{6,4},{7,5},{8,10},{9,11},{10,... | collective-permute-start | bytes 589832 | tf_op jit(solution)/shard_map/ppermute | solution.py:184
  57.4 5.1 %collective-permute-start.10 = (bf16[128,384]{1,0:T(8,128)(2,1)S(1)}, bf16[128,384]{1,0:T(8,128)(2,1)S(1)}, u32[]{:S(2)}, u32[]{:S(2)}) collective-permute-start(bf16[128,384]{1,0:T(8,128)(2,1)S(1)} %get-tuple-element.31), channel_id=1, source_target_pairs={{0,1},{1,0},{2,3},{3,2},{4,5},{5,4},{6,7},{7,6},{8,9},{9,8},{10,11... | collective-permute-start | bytes 294920 | tf_op jit(solution)/shard_map/ppermute | solution.py:184
  57.5 5.5 %collective-permute-start.19 = (bf16[192,768]{1,0:T(8,128)(2,1)S(1)}, bf16[192,768]{1,0:T(8,128)(2,1)S(1)}, u32[]{:S(2)}, u32[]{:S(2)}) collective-permute-start(bf16[192,768]{1,0:T(8,128)(2,1)S(1)} %collective-permute-done.15.refs_7_), channel_id=1, source_target_pairs={{0,1},{1,0},{2,3},{3,2},{4,5},{5,4},{6,7},{7,6},{8,9},{9,8},{10,11... | collective-permute-start | bytes 884744 | tf_op jit(solution)/shard_map/ppermute | solution.py:184
  61.9 1.6 %collective-permute-start.18 = (bf16[192,768]{1,0:T(8,128)(2,1)S(1)}, bf16[192,768]{1,0:T(8,128)(2,1)S(1)}, u32[]{:S(2)}, u32[]{:S(2)}) collective-permute-start(bf16[192,768]{1,0:T(8,128)(2,1)S(1)} %collective-permute-done.14.refs_6_), channel_id=1, source_target_pairs={{0,1},{1,0},{2,3},{3,2},{4,5},{5,4},{6,7},{7,6},{8,9},{9,8},{10,11... | collective-permute-start | bytes 884744 | tf_op jit(solution)/shard_map/ppermute | solution.py:184
  61.9 2.0 %collective-permute-start.17 = (bf16[192,768]{1,0:T(8,128)(2,1)S(1)}, bf16[192,768]{1,0:T(8,128)(2,1)S(1)}, u32[]{:S(2)}, u32[]{:S(2)}) collective-permute-start(bf16[192,768]{1,0:T(8,128)(2,1)S(1)} %collective-permute-done.13.refs_5_), channel_id=1, source_target_pairs={{0,1},{1,0},{2,3},{3,2},{4,5},{5,4},{6,7},{7,6},{8,9},{9,8},{10,11... | collective-permute-start | bytes 884744 | tf_op jit(solution)/shard_map/ppermute | solution.py:184
  62.4 1.9 %collective-permute-start.16 = (bf16[192,768]{1,0:T(8,128)(2,1)S(1)}, bf16[192,768]{1,0:T(8,128)(2,1)S(1)}, u32[]{:S(2)}, u32[]{:S(2)}) collective-permute-start(bf16[192,768]{1,0:T(8,128)(2,1)S(1)} %shard_map.102.refs_4_), channel_id=1, source_target_pairs={{0,1},{1,0},{2,3},{3,2},{4,5},{5,4},{6,7},{7,6},{8,9},{9,8},{10,11... | collective-permute-start | bytes 884744 | tf_op jit(solution)/shard_map/ppermute | solution.py:184
  62.5 1.9 %collective-permute-start.12 = (bf16[128,384]{1,0:T(8,128)(2,1)S(1)}, bf16[128,384]{1,0:T(8,128)(2,1)S(1)}, u32[]{:S(2)}, u32[]{:S(2)}) collective-permute-start(bf16[128,384]{1,0:T(8,128)(2,1)S(1)} %get-tuple-element.37), channel_id=1, source_target_pairs={{0,1},{1,0},{2,3},{3,2},{4,5},{5,4},{6,7},{7,6},{8,9},{9,8},{10,11... | collective-permute-start | bytes 294920 | tf_op jit(solution)/shard_map/ppermute | solution.py:184
  (4 other events, 28.2 us)

commit v5 on v4

--- a/solution.py
+++ b/solution.py
@@ -268,19 +268,23 @@
     return copies
 
 
-def project_kernel(tm_count, dp_count, head_size, info, *refs):
-    normed_refs, refs = refs[:tm_count], refs[tm_count:]
+def gather_kernel(tm_count, info, *refs):
+    normed, sems = refs[tm_count:]
+    block_len = refs[0].shape[0]
+    spots = [pl.multiple_of((info[0] ^ k) * block_len, block_len) for k in range(tm_count)]
+    targets = [normed.at[pl.ds(spot, block_len), :] for spot in spots]
+    for copy in load(refs[:tm_count], targets, sems):
+        copy.wait()
+
+
+def project_kernel(tm_count, dp_count, head_size, info, normed, *refs):
     cut_refs, refs = refs[:dp_count], refs[dp_count:]
-    query_ref, key_ref, value_ref, normed, cuts, weight, cut_sems, normed_sems = refs
+    query_ref, key_ref, value_ref, cuts, weight, cut_sems = refs
     block_len = normed.shape[0] // tm_count
     rows, width = cuts.shape[1] * 2 // 3, cuts.shape[2] // 2
     wide = query_ref.shape[1]
-    spots = [pl.multiple_of((info[0] ^ k) * block_len, block_len) for k in range(tm_count)]
     sources = [ref.at[: cuts.shape[1], :] for ref in cut_refs]
     cut_copies = load(sources, [cuts.at[k] for k in range(dp_count)], cut_sems)
-    normed_copies = load(
-        normed_refs, [normed.at[pl.ds(spot, block_len), :] for spot in spots], normed_sems
-    )
     weight[...] = jnp.zeros_like(weight)
     value_ref[:block_len, :] = jnp.zeros_like(value_ref[:block_len, :])
     value_ref[(tm_count + 1) * block_len :, :] = jnp.zeros_like(value_ref[:block_len, :])
@@ -298,15 +302,14 @@
                 weight[
                     pl.ds(start + part * (rows // 2), rows // 2), target : target + head_size
                 ] = cuts[k, rows:, source : source + head_size]
-    for copy in normed_copies:
-        copy.wait()
-    shift = slice(block_len, (tm_count + 1) * block_len)
-    for part, ref in enumerate((query_ref, key_ref, value_ref.at[shift, :])):
-        ref[...] = jnp.dot(
-            normed[...],
-            weight[:, part * wide : (part + 1) * wide],
-            preferred_element_type=jnp.float32,
+    step = tm_count * block_len
+    for start in range(0, tm_count * block_len, step):
+        projected = jnp.dot(
+            normed[start : start + step, :], weight[...], preferred_element_type=jnp.float32
         ).astype(half)
+        query_ref[start : start + step, :] = projected[:, :wide]
+        key_ref[start : start + step, :] = projected[:, wide : 2 * wide]
+        value_ref[block_len + start : block_len + start + step, :] = projected[:, 2 * wide :]
 
 
 def softmax_kernel(
@@ -499,6 +502,13 @@
         {k: later(x, *arrived, relative, pair) for k, x in normed_far.items()}, "tm"
     )
     pairs = send_far(later(pair, *[cut_far[k] for k in range(2, dp_count, 2)]), "dp")
+    normed = call(
+        functools.partial(gather_kernel, tm_count),
+        shaped(total_len, model_width),
+        (scalar, *((x, far) for x in normed_pieces)),
+        [pltpu.SemaphoreType.DMA((tm_count,))],
+        micros=2.0,
+    )
     query, key, value = call(
         functools.partial(project_kernel, tm_count, dp_count, head_size),
         (
@@ -506,13 +516,11 @@
             shaped(total_len, wide),
             shaped(total_len + 2 * block_len, wide),
         ),
-        (scalar, *((x, far) for x in normed_pieces), *((x, far) for x in cut_pieces)),
+        (scalar, (normed, near), *((x, far) for x in cut_pieces)),
         [
-            pltpu.VMEM((total_len, model_width), half),
             pltpu.VMEM((dp_count, in_rows // 2 * 3, 2 * width), half),
             pltpu.VMEM((model_width, 3 * wide), half),
             pltpu.SemaphoreType.DMA((dp_count,)),
-            pltpu.SemaphoreType.DMA((tm_count,)),
         ],
         micros=6.0,
     )

time: 68.1 us -> 68.1 us (level)
  waiting for transfers between devices: 21.3 us -> 18.9 us
  starting transfers between devices: 19.8 us -> 21.7 us
    ppermute x20, waiting for transfers between devices: 21.3 us -> 18.9 us  [swap(): return lax.ppermute(block, axis, [(i, i ^ distance) for i in range(count)])]
    ppermute x20, starting transfers between devices: 19.8 us -> 21.7 us  [swap(): return lax.ppermute(block, axis, [(i, i ^ distance) for i in range(count)])]
    pallas_call x8 -> x9, Pallas kernels: 24.1 us -> 24.7 us  [call(): pl.pallas_call(kernel, out_shape=out_shape, in_specs=list(specs), out_spe...]
  transfers between devices with their start and end apart: 20 -> 20, of which waited for: 9 -> 9; matrix products, arithmetic and copies ran while one was open for 1% -> 1% of each run, Pallas kernels for 25% -> 26%
where the time goes in v5:
time: 68.1 us; the launch traced here: 67.9 us
  Pallas kernels  24.7 us (36%)
  starting transfers between devices  21.7 us (32%)
  waiting for transfers between devices  18.9 us (28%)
  other arithmetic  1.53 us (2%)
  between operations  1.07 us (2%)
    pallas_call x9, Pallas kernels, call(): pl.pallas_call(kernel, out_shape=out_shape, in_specs=list(specs), out_spe...  24.7 us
    ppermute x20, starting transfers between devices, swap(): return lax.ppermute(block, axis, [(i, i ^ distance) for i in range(count)])  21.7 us
    ppermute x20, waiting for transfers between devices, swap(): return lax.ppermute(block, axis, [(i, i ^ distance) for i in range(count)])  18.9 us
  transfers between devices with their start and end apart: 20, of which 9 were waited for; matrix products, arithmetic and copies ran while one was open for 1% of the time, Pallas kernels for 26%

profile of v5, /device:TPU:0, one launch (start us, length us, event | category | flops | bytes accessed | tf_op | source)
XLA Modules:
  0.0 67.9 jit_solution(17517401688046500254)
XLA Ops:
  0.7 0.7 pad_add_fusion.info
  1.4 3.6 %shard_map.100 = (bf16[288,384]{1,0:T(8,128)(2,1)}, bf16[480,384]{1,0:T(8,128)(2,1)}, bf16[96,768]{1,0:T(8,128)(2,1)}, bf16[256,1536]{1,0:T(8,128)(2,1)}) custom-call(s32[3]{0:T(128)} %pad_add_fusion.info, bf16[192,768]{1,0:T(8,128)(2,1)} %refs_0_.1, bf16[192,768]{1,0:T(8,128)(2,1)} %refs_1_.1, bf16[192,768]{1,0:T(8,128)(2,1)} %refs_2_.1, ...), custom_call_target="tpu_custom_call" | custom-call | flops 1100000000 | bytes 4096 | tf_op jit(solution)/shard_map/pallas_call | solution.py:165
  5.0 3.1 %collective-permute-start = (bf16[288,384]{1,0:T(8,128)(2,1)}, bf16[288,384]{1,0:T(8,128)(2,1)S(1)}, u32[]{:S(2)}, u32[]{:S(2)}) collective-permute-start(bf16[288,384]{1,0:T(8,128)(2,1)} %get-tuple-element.22.refs_0_), channel_id=1, source_target_pairs={{0,8},{4,12},{8,0},{12,4},{16,24},{20,28},{24,16},{28,20},{1,9},{5... | collective-permute-start | bytes 663560 | tf_op jit(solution)/shard_map/ppermute | solution.py:184
  8.1 2.6 %collective-permute-start.1 = (bf16[288,384]{1,0:T(8,128)(2,1)}, bf16[288,384]{1,0:T(8,128)(2,1)S(1)}, u32[]{:S(2)}, u32[]{:S(2)}) collective-permute-start(bf16[288,384]{1,0:T(8,128)(2,1)} %get-tuple-element.22.refs_0_), channel_id=1, source_target_pairs={{0,16},{4,20},{8,24},{12,28},{16,0},{20,4},{24,8},{28,12},{1,17},{... | collective-permute-start | bytes 663560 | tf_op jit(solution)/shard_map/ppermute | solution.py:184
  10.7 1.7 %collective-permute-start.5 = (bf16[480,384]{1,0:T(8,128)(2,1)}, bf16[480,384]{1,0:T(8,128)(2,1)S(1)}, u32[]{:S(2)}, u32[]{:S(2)}) collective-permute-start(bf16[480,384]{1,0:T(8,128)(2,1)} %get-tuple-element.24), channel_id=1, source_target_pairs={{0,4},{4,0},{8,12},{12,8},{16,20},{20,16},{24,28},{28,24},{1,5},{5... | collective-permute-start | bytes 1105928 | tf_op jit(solution)/shard_map/ppermute | solution.py:184
  12.4 1.5 %collective-permute-start.7 = (bf16[256,1536]{1,0:T(8,128)(2,1)}, bf16[256,1536]{1,0:T(8,128)(2,1)S(1)}, u32[]{:S(2)}, u32[]{:S(2)}) collective-permute-start(bf16[256,1536]{1,0:T(8,128)(2,1)} %get-tuple-element.25.refs_0_), channel_id=1, source_target_pairs={{0,2},{1,3},{2,0},{3,1},{4,6},{5,7},{6,4},{7,5},{8,10},{9,11},{10,... | collective-permute-start | bytes 2359304 | tf_op jit(solution)/shard_map/ppermute | solution.py:184
  14.0 0.8 %multiply_cosine_fusion = (f32[64,768]{1,0:T(8,128)S(1)}, f32[64,768]{1,0:T(8,128)S(1)}) fusion(f32[768]{0:T(1024)S(1)} %multiply_exponential_fusion, f32[64]{0:T(128)S(1)} %pad_maximum_fusion), kind=kLoop, calls=%fused_computation | loop fusion | flops 49152 | bytes 396544 | tf_op jit(solution)/shard_map/cos | solution.py:238
  14.8 2.9 %collective-permute-done.refs_2_ = bf16[288,384]{1,0:T(8,128)(2,1)S(1)} collective-permute-done((bf16[288,384]{1,0:T(8,128)(2,1)}, bf16[288,384]{1,0:T(8,128)(2,1)S(1)}, u32[]{:S(2)}, u32[]{:S(2)}) %collective-permute-start) | collective-permute-done | bytes 221216 | tf_op jit(solution)/shard_map/ppermute | solution.py:184
  17.7 1.7 %collective-permute-start.3 = (bf16[288,384]{1,0:T(8,128)(2,1)S(1)}, bf16[288,384]{1,0:T(8,128)(2,1)S(1)}, u32[]{:S(2)}, u32[]{:S(2)}) collective-permute-start(bf16[288,384]{1,0:T(8,128)(2,1)S(1)} %collective-permute-done.refs_2_), channel_id=1, source_target_pairs={{0,4},{4,0},{8,12},{12,8},{16,20},{20,16},{24,28},{28,24},{1,5},{5... | collective-permute-start | bytes 663560 | tf_op jit(solution)/shard_map/ppermute | solution.py:184
  19.4 7.7 %collective-permute-done.1.refs_4_ = bf16[288,384]{1,0:T(8,128)(2,1)S(1)} collective-permute-done((bf16[288,384]{1,0:T(8,128)(2,1)}, bf16[288,384]{1,0:T(8,128)(2,1)S(1)}, u32[]{:S(2)}, u32[]{:S(2)}) %collective-permute-start.1) | collective-permute-done | bytes 221216 | tf_op jit(solution)/shard_map/ppermute | solution.py:184
  27.0 1.5 %collective-permute-start.4 = (bf16[288,384]{1,0:T(8,128)(2,1)S(1)}, bf16[288,384]{1,0:T(8,128)(2,1)S(1)}, u32[]{:S(2)}, u32[]{:S(2)}) collective-permute-start(bf16[288,384]{1,0:T(8,128)(2,1)S(1)} %collective-permute-done.1.refs_4_), channel_id=1, source_target_pairs={{0,4},{4,0},{8,12},{12,8},{16,20},{20,16},{24,28},{28,24},{1,5},{5... | collective-permute-start | bytes 663560 | tf_op jit(solution)/shard_map/ppermute | solution.py:184
  28.6 1.7 %shard_map.101.relative = bf16[1024,256]{1,0:T(8,128)(2,1)S(1)} custom-call(s32[3]{0:T(128)S(1)} %copy-done, f32[64,768]{1,0:T(8,128)S(1)} %get-tuple-element.40.sin_ref, f32[64,768]{1,0:T(8,128)S(1)} %get-tuple-element.39.cos_ref, bf16[192,1536]{1,0:T(8,128)(2,1)S(1)} %bitcast.7), custom_call_target="tpu_custom_call" | custom-call | flops 2200000000 | bytes 4096 | tf_op jit(solution)/shard_map/pallas_call | solution.py:165
  30.9 2.0 %collective-permute-done.4.refs_5_ = bf16[288,384]{1,0:T(8,128)(2,1)S(1)} collective-permute-done((bf16[288,384]{1,0:T(8,128)(2,1)S(1)}, bf16[288,384]{1,0:T(8,128)(2,1)S(1)}, u32[]{:S(2)}, u32[]{:S(2)}) %collective-permute-start.4) | collective-permute-done | bytes 221216 | tf_op jit(solution)/shard_map/ppermute | solution.py:184
  33.5 1.5 %collective-permute-start.9 = (bf16[288,384]{1,0:T(8,128)(2,1)S(1)}, bf16[288,384]{1,0:T(8,128)(2,1)S(1)}, u32[]{:S(2)}, u32[]{:S(2)}) collective-permute-start(bf16[288,384]{1,0:T(8,128)(2,1)S(1)} %collective-permute-done.2.refs_6_), channel_id=1, source_target_pairs={{0,4},{4,0},{8,12},{12,8},{16,20},{20,16},{24,28},{28,24},{1,5},{5... | collective-permute-start | bytes 663560 | tf_op jit(solution)/shard_map/ppermute | solution.py:184
  35.0 2.5 %collective-permute-start.15 = (bf16[192,768]{1,0:T(8,128)(2,1)S(1)}, bf16[192,768]{1,0:T(8,128)(2,1)S(1)}, u32[]{:S(2)}, u32[]{:S(2)}) collective-permute-start(bf16[192,768]{1,0:T(8,128)(2,1)S(1)} %shard_map.102.refs_4_), channel_id=1, source_target_pairs={{0,24},{4,28},{8,16},{12,20},{16,8},{20,12},{24,0},{28,4},{1,25},{... | collective-permute-start | bytes 884744 | tf_op jit(solution)/shard_map/ppermute | solution.py:184
  37.5 1.9 %collective-permute-start.13 = (bf16[192,768]{1,0:T(8,128)(2,1)S(1)}, bf16[192,768]{1,0:T(8,128)(2,1)S(1)}, u32[]{:S(2)}, u32[]{:S(2)}) collective-permute-start(bf16[192,768]{1,0:T(8,128)(2,1)S(1)} %shard_map.102.refs_4_), channel_id=1, source_target_pairs={{0,8},{4,12},{8,0},{12,4},{16,24},{20,28},{24,16},{28,20},{1,9},{5... | collective-permute-start | bytes 884744 | tf_op jit(solution)/shard_map/ppermute | solution.py:184
  39.4 1.0 %shard_map.103.normed = bf16[1024,1536]{1,0:T(8,128)(2,1)S(1)} custom-call(s32[3]{0:T(128)S(1)} %copy-done, bf16[256,1536]{1,0:T(8,128)(2,1)S(1)} %copy-done.2, bf16[256,1536]{1,0:T(8,128)(2,1)S(1)} %collective-permute-done.6.refs_1_, bf16[256,1536]{1,0:T(8,128)(2,1)S(1)} %collective-permute-done.7.refs_2_, bf16[256,1536]{1,0:T(8,128)(2,1)S(1)} %collective-permute-done.8.refs_3_), custom_call_target="tpu_custom_call" | custom-call | flops 2200000000 | bytes 4096 | tf_op jit(solution)/shard_map/pallas_call | solution.py:165
  40.9 7.1 %shard_map.104 = (bf16[1024,256]{1,0:T(8,128)(2,1)S(1)}, bf16[1024,256]{1,0:T(8,128)(2,1)S(1)}, bf16[1536,256]{1,0:T(8,128)(2,1)S(1)}) custom-call(s32[3]{0:T(128)S(1)} %copy-done, bf16[1024,1536]{1,0:T(8,128)(2,1)S(1)} %shard_map.103.normed, bf16[288,384]{1,0:T(8,128)(2,1)S(1)} %copy-done.4, bf16[480,384]{1,0:T(8,128)(2,1)S(1)} %collective-permute-done.5.beside_ref.refs_1_, ...), custom_call_target="tpu_custom_call" | custom-call | flops 6600000000 | bytes 4096 | tf_op jit(solution)/shard_map/pallas_call | solution.py:165
  48.1 5.0 %shard_map.105.weights_ref = bf16[4,2,256,768]{3,2,1,0:T(8,128)(2,1)S(1)} custom-call(s32[3]{0:T(128)S(1)} %copy-done, bf16[1024,256]{1,0:T(8,128)(2,1)S(1)} %get-tuple-element.27.query, bf16[1024,256]{1,0:T(8,128)(2,1)S(1)} %get-tuple-element.28.key, bf16[1024,256]{1,0:T(8,128)(2,1)S(1)} %shard_map.101.relative, f32[8,96]{1,0:T(8,128)S(1)} %copy-done.5, ...), custom_call_target="tpu_custom_call" | custom-call | flops 5500000256 | bytes 4096 | tf_op jit(solution)/shard_map/pallas_call | solution.py:165
  53.1 1.2 %shard_map.107 = bf16[256,384]{1,0:T(8,128)(2,1)S(1)} custom-call(s32[3]{0:T(128)S(1)} %copy-done, bf16[4,2,256,768]{3,2,1,0:T(8,128)(2,1)S(1)} %shard_map.105.weights_ref, bf16[1536,256]{1,0:T(8,128)(2,1)S(1)} %get-tuple-element.29.value), custom_call_target="tpu_custom_call" | custom-call | flops 1100000000 | bytes 4096 | tf_op jit(solution)/shard_map/pallas_call | solution.py:165
  54.2 1.5 %collective-permute-start.11 = (bf16[256,384]{1,0:T(8,128)(2,1)S(1)}, bf16[256,384]{1,0:T(8,128)(2,1)S(1)}, u32[]{:S(2)}, u32[]{:S(2)}) collective-permute-start(bf16[256,384]{1,0:T(8,128)(2,1)S(1)} %shard_map.107), channel_id=1, source_target_pairs={{0,2},{1,3},{2,0},{3,1},{4,6},{5,7},{6,4},{7,5},{8,10},{9,11},{10,... | collective-permute-start | bytes 589832 | tf_op jit(solution)/shard_map/ppermute | solution.py:184
  55.8 1.2 %shard_map.106 = (bf16[128,384]{1,0:T(8,128)(2,1)S(1)}, bf16[128,384]{1,0:T(8,128)(2,1)S(1)}) custom-call(s32[3]{0:T(128)S(1)} %copy-done, bf16[4,2,256,768]{3,2,1,0:T(8,128)(2,1)S(1)} %shard_map.105.weights_ref, bf16[1536,256]{1,0:T(8,128)(2,1)S(1)} %get-tuple-element.29.value), custom_call_target="tpu_custom_call" | custom-call | flops 1100000000 | bytes 4096 | tf_op jit(solution)/shard_map/pallas_call | solution.py:165
  57.5 4.3 %collective-permute-done.14.refs_6_ = bf16[192,768]{1,0:T(8,128)(2,1)S(1)} collective-permute-done((bf16[192,768]{1,0:T(8,128)(2,1)S(1)}, bf16[192,768]{1,0:T(8,128)(2,1)S(1)}, u32[]{:S(2)}, u32[]{:S(2)}) %collective-permute-start.14) | collective-permute-done | bytes 294944 | tf_op jit(solution)/shard_map/ppermute | solution.py:184
  64.5 3.3 %shard_map.108 = bf16[256,1536]{1,0:T(8,128)(2,1)} custom-call(s32[3]{0:T(128)S(1)} %copy-done, bf16[128,384]{1,0:T(8,128)(2,1)S(1)} %get-tuple-element.30.refs_0_, bf16[128,384]{1,0:T(8,128)(2,1)S(1)} %collective-permute-done.10.refs_1_, bf16[128,384]{1,0:T(8,128)(2,1)S(1)} %get-tuple-element.38.refs_2_, ...), custom_call_target="tpu_custom_call" | custom-call | flops 2750000128 | bytes 4096 | tf_op jit(solution)/shard_map/pallas_call | solution.py:165
  (48 shorter events, 4.8 us)
Async XLA Ops:
  0.0 28.6 %copy-start.3 = (bf16[1536,192]{0,1:T(8,128)(2,1)S(1)}, bf16[1536,192]{0,1:T(8,128)(2,1)}, u32[]{:S(2)}) copy-start(bf16[1536,192]{0,1:T(8,128)(2,1)} %param.17) | copy-start | bytes 1769476
  1.4 27.2 %copy-start = (s32[3]{0:T(128)S(1)}, s32[3]{0:T(128)}, u32[]{:S(2)}) copy-start(s32[3]{0:T(128)} %pad_add_fusion.info) | copy-start | bytes 40
  5.0 12.7 %collective-permute-start = (bf16[288,384]{1,0:T(8,128)(2,1)}, bf16[288,384]{1,0:T(8,128)(2,1)S(1)}, u32[]{:S(2)}, u32[]{:S(2)}) collective-permute-start(bf16[288,384]{1,0:T(8,128)(2,1)} %get-tuple-element.22.refs_0_), channel_id=1, source_target_pairs={{0,8},{4,12},{8,0},{12,4},{16,24},{20,28},{24,16},{28,20},{1,9},{5... | collective-permute-start | bytes 663560 | tf_op jit(solution)/shard_map/ppermute | solution.py:184
  8.1 18.9 %collective-permute-start.1 = (bf16[288,384]{1,0:T(8,128)(2,1)}, bf16[288,384]{1,0:T(8,128)(2,1)S(1)}, u32[]{:S(2)}, u32[]{:S(2)}) collective-permute-start(bf16[288,384]{1,0:T(8,128)(2,1)} %get-tuple-element.22.refs_0_), channel_id=1, source_target_pairs={{0,16},{4,20},{8,24},{12,28},{16,0},{20,4},{24,8},{28,12},{1,17},{... | collective-permute-start | bytes 663560 | tf_op jit(solution)/shard_map/ppermute | solution.py:184
  10.7 20.2 %collective-permute-start.2 = (bf16[288,384]{1,0:T(8,128)(2,1)}, bf16[288,384]{1,0:T(8,128)(2,1)S(1)}, u32[]{:S(2)}, u32[]{:S(2)}) collective-permute-start(bf16[288,384]{1,0:T(8,128)(2,1)} %get-tuple-element.22.refs_0_), channel_id=1, source_target_pairs={{0,24},{4,28},{8,16},{12,20},{16,8},{20,12},{24,0},{28,4},{1,25},{... | collective-permute-start | bytes 663560 | tf_op jit(solution)/shard_map/ppermute | solution.py:184
  10.7 19.6 %collective-permute-start.5 = (bf16[480,384]{1,0:T(8,128)(2,1)}, bf16[480,384]{1,0:T(8,128)(2,1)S(1)}, u32[]{:S(2)}, u32[]{:S(2)}) collective-permute-start(bf16[480,384]{1,0:T(8,128)(2,1)} %get-tuple-element.24), channel_id=1, source_target_pairs={{0,4},{4,0},{8,12},{12,8},{16,20},{20,16},{24,28},{28,24},{1,5},{5... | collective-permute-start | bytes 1105928 | tf_op jit(solution)/shard_map/ppermute | solution.py:184
  12.4 20.6 %collective-permute-start.7 = (bf16[256,1536]{1,0:T(8,128)(2,1)}, bf16[256,1536]{1,0:T(8,128)(2,1)S(1)}, u32[]{:S(2)}, u32[]{:S(2)}) collective-permute-start(bf16[256,1536]{1,0:T(8,128)(2,1)} %get-tuple-element.25.refs_0_), channel_id=1, source_target_pairs={{0,2},{1,3},{2,0},{3,1},{4,6},{5,7},{6,4},{7,5},{8,10},{9,11},{10,... | collective-permute-start | bytes 2359304 | tf_op jit(solution)/shard_map/ppermute | solution.py:184
  17.7 13.2 %collective-permute-start.3 = (bf16[288,384]{1,0:T(8,128)(2,1)S(1)}, bf16[288,384]{1,0:T(8,128)(2,1)S(1)}, u32[]{:S(2)}, u32[]{:S(2)}) collective-permute-start(bf16[288,384]{1,0:T(8,128)(2,1)S(1)} %collective-permute-done.refs_2_), channel_id=1, source_target_pairs={{0,4},{4,0},{8,12},{12,8},{16,20},{20,16},{24,28},{28,24},{1,5},{5... | collective-permute-start | bytes 663560 | tf_op jit(solution)/shard_map/ppermute | solution.py:184
  27.0 5.9 %collective-permute-start.4 = (bf16[288,384]{1,0:T(8,128)(2,1)S(1)}, bf16[288,384]{1,0:T(8,128)(2,1)S(1)}, u32[]{:S(2)}, u32[]{:S(2)}) collective-permute-start(bf16[288,384]{1,0:T(8,128)(2,1)S(1)} %collective-permute-done.1.refs_4_), channel_id=1, source_target_pairs={{0,4},{4,0},{8,12},{12,8},{16,20},{20,16},{24,28},{28,24},{1,5},{5... | collective-permute-start | bytes 663560 | tf_op jit(solution)/shard_map/ppermute | solution.py:184
  30.9 10.0 %copy-start.4 = (bf16[288,384]{1,0:T(8,128)(2,1)S(1)}, bf16[288,384]{1,0:T(8,128)(2,1)}, u32[]{:S(2)}) copy-start(bf16[288,384]{1,0:T(8,128)(2,1)} %get-tuple-element.22.refs_0_) | copy-start | bytes 663556
  33.0 4.5 %collective-permute-start.6 = (bf16[256,1536]{1,0:T(8,128)(2,1)S(1)}, bf16[256,1536]{1,0:T(8,128)(2,1)S(1)}, u32[]{:S(2)}, u32[]{:S(2)}) collective-permute-start(bf16[256,1536]{1,0:T(8,128)(2,1)S(1)} %copy-done.2), channel_id=1, source_target_pairs={{0,1},{1,0},{2,3},{3,2},{4,5},{5,4},{6,7},{7,6},{8,9},{9,8},{10,11... | collective-permute-start | bytes 2359304 | tf_op jit(solution)/shard_map/ppermute | solution.py:184
  33.0 6.4 %collective-permute-start.8 = (bf16[256,1536]{1,0:T(8,128)(2,1)S(1)}, bf16[256,1536]{1,0:T(8,128)(2,1)S(1)}, u32[]{:S(2)}, u32[]{:S(2)}) collective-permute-start(bf16[256,1536]{1,0:T(8,128)(2,1)S(1)} %collective-permute-done.7.refs_2_), channel_id=1, source_target_pairs={{0,1},{1,0},{2,3},{3,2},{4,5},{5,4},{6,7},{7,6},{8,9},{9,8},{10,11... | collective-permute-start | bytes 2359304 | tf_op jit(solution)/shard_map/ppermute | solution.py:184
  33.5 7.4 %collective-permute-start.9 = (bf16[288,384]{1,0:T(8,128)(2,1)S(1)}, bf16[288,384]{1,0:T(8,128)(2,1)S(1)}, u32[]{:S(2)}, u32[]{:S(2)}) collective-permute-start(bf16[288,384]{1,0:T(8,128)(2,1)S(1)} %collective-permute-done.2.refs_6_), channel_id=1, source_target_pairs={{0,4},{4,0},{8,12},{12,8},{16,20},{20,16},{24,28},{28,24},{1,5},{5... | collective-permute-start | bytes 663560 | tf_op jit(solution)/shard_map/ppermute | solution.py:184
  35.0 22.0 %collective-permute-start.15 = (bf16[192,768]{1,0:T(8,128)(2,1)S(1)}, bf16[192,768]{1,0:T(8,128)(2,1)S(1)}, u32[]{:S(2)}, u32[]{:S(2)}) collective-permute-start(bf16[192,768]{1,0:T(8,128)(2,1)S(1)} %shard_map.102.refs_4_), channel_id=1, source_target_pairs={{0,24},{4,28},{8,16},{12,20},{16,8},{20,12},{24,0},{28,4},{1,25},{... | collective-permute-start | bytes 884744 | tf_op jit(solution)/shard_map/ppermute | solution.py:184
  37.5 24.4 %collective-permute-start.14 = (bf16[192,768]{1,0:T(8,128)(2,1)S(1)}, bf16[192,768]{1,0:T(8,128)(2,1)S(1)}, u32[]{:S(2)}, u32[]{:S(2)}) collective-permute-start(bf16[192,768]{1,0:T(8,128)(2,1)S(1)} %shard_map.102.refs_4_), channel_id=1, source_target_pairs={{0,16},{4,20},{8,24},{12,28},{16,0},{20,4},{24,8},{28,12},{1,17},{... | collective-permute-start | bytes 884744 | tf_op jit(solution)/shard_map/ppermute | solution.py:184
  37.5 24.4 %collective-permute-start.13 = (bf16[192,768]{1,0:T(8,128)(2,1)S(1)}, bf16[192,768]{1,0:T(8,128)(2,1)S(1)}, u32[]{:S(2)}, u32[]{:S(2)}) collective-permute-start(bf16[192,768]{1,0:T(8,128)(2,1)S(1)} %shard_map.102.refs_4_), channel_id=1, source_target_pairs={{0,8},{4,12},{8,0},{12,4},{16,24},{20,28},{24,16},{28,20},{1,9},{5... | collective-permute-start | bytes 884744 | tf_op jit(solution)/shard_map/ppermute | solution.py:184
  54.2 10.2 %copy-start.1 = (bf16[1,256,1536]{2,1,0:T(8,128)(2,1)S(1)}, bf16[1,256,1536]{2,1,0:T(8,128)(2,1)}, u32[]{:S(2)}) copy-start(bf16[1,256,1536]{2,1,0:T(8,128)(2,1)} %param.10) | copy-start | bytes 2359300
  54.2 8.2 %collective-permute-start.11 = (bf16[256,384]{1,0:T(8,128)(2,1)S(1)}, bf16[256,384]{1,0:T(8,128)(2,1)S(1)}, u32[]{:S(2)}, u32[]{:S(2)}) collective-permute-start(bf16[256,384]{1,0:T(8,128)(2,1)S(1)} %shard_map.107), channel_id=1, source_target_pairs={{0,2},{1,3},{2,0},{3,1},{4,6},{5,7},{6,4},{7,5},{8,10},{9,11},{10,... | collective-permute-start | bytes 589832 | tf_op jit(solution)/shard_map/ppermute | solution.py:184
  57.0 5.5 %collective-permute-start.10 = (bf16[128,384]{1,0:T(8,128)(2,1)S(1)}, bf16[128,384]{1,0:T(8,128)(2,1)S(1)}, u32[]{:S(2)}, u32[]{:S(2)}) collective-permute-start(bf16[128,384]{1,0:T(8,128)(2,1)S(1)} %get-tuple-element.31), channel_id=1, source_target_pairs={{0,1},{1,0},{2,3},{3,2},{4,5},{5,4},{6,7},{7,6},{8,9},{9,8},{10,11... | collective-permute-start | bytes 294920 | tf_op jit(solution)/shard_map/ppermute | solution.py:184
  57.1 6.0 %collective-permute-start.19 = (bf16[192,768]{1,0:T(8,128)(2,1)S(1)}, bf16[192,768]{1,0:T(8,128)(2,1)S(1)}, u32[]{:S(2)}, u32[]{:S(2)}) collective-permute-start(bf16[192,768]{1,0:T(8,128)(2,1)S(1)} %collective-permute-done.15.refs_7_), channel_id=1, source_target_pairs={{0,1},{1,0},{2,3},{3,2},{4,5},{5,4},{6,7},{7,6},{8,9},{9,8},{10,11... | collective-permute-start | bytes 884744 | tf_op jit(solution)/shard_map/ppermute | solution.py:184
  61.9 1.6 %collective-permute-start.18 = (bf16[192,768]{1,0:T(8,128)(2,1)S(1)}, bf16[192,768]{1,0:T(8,128)(2,1)S(1)}, u32[]{:S(2)}, u32[]{:S(2)}) collective-permute-start(bf16[192,768]{1,0:T(8,128)(2,1)S(1)} %collective-permute-done.14.refs_6_), channel_id=1, source_target_pairs={{0,1},{1,0},{2,3},{3,2},{4,5},{5,4},{6,7},{7,6},{8,9},{9,8},{10,11... | collective-permute-start | bytes 884744 | tf_op jit(solution)/shard_map/ppermute | solution.py:184
  61.9 2.0 %collective-permute-start.17 = (bf16[192,768]{1,0:T(8,128)(2,1)S(1)}, bf16[192,768]{1,0:T(8,128)(2,1)S(1)}, u32[]{:S(2)}, u32[]{:S(2)}) collective-permute-start(bf16[192,768]{1,0:T(8,128)(2,1)S(1)} %collective-permute-done.13.refs_5_), channel_id=1, source_target_pairs={{0,1},{1,0},{2,3},{3,2},{4,5},{5,4},{6,7},{7,6},{8,9},{9,8},{10,11... | collective-permute-start | bytes 884744 | tf_op jit(solution)/shard_map/ppermute | solution.py:184
  62.4 1.9 %collective-permute-start.16 = (bf16[192,768]{1,0:T(8,128)(2,1)S(1)}, bf16[192,768]{1,0:T(8,128)(2,1)S(1)}, u32[]{:S(2)}, u32[]{:S(2)}) collective-permute-start(bf16[192,768]{1,0:T(8,128)(2,1)S(1)} %shard_map.102.refs_4_), channel_id=1, source_target_pairs={{0,1},{1,0},{2,3},{3,2},{4,5},{5,4},{6,7},{7,6},{8,9},{9,8},{10,11... | collective-permute-start | bytes 884744 | tf_op jit(solution)/shard_map/ppermute | solution.py:184
  62.5 1.9 %collective-permute-start.12 = (bf16[128,384]{1,0:T(8,128)(2,1)S(1)}, bf16[128,384]{1,0:T(8,128)(2,1)S(1)}, u32[]{:S(2)}, u32[]{:S(2)}) collective-permute-start(bf16[128,384]{1,0:T(8,128)(2,1)S(1)} %get-tuple-element.37), channel_id=1, source_target_pairs={{0,1},{1,0},{2,3},{3,2},{4,5},{5,4},{6,7},{7,6},{8,9},{9,8},{10,11... | collective-permute-start | bytes 294920 | tf_op jit(solution)/shard_map/ppermute | solution.py:184
  (4 other events, 21.4 us)
